TPU v7x, 32 devices: a whole 2x2x4 slice. The times are simulated.
32 devices in a mesh: groups: 2 (over x), seq: 16 (over z, y, core).
Axes of the slice: x: 2, y: 2, z: 4, core: 2. Of those that a mesh axis runs over, the one named last changes fastest.
Arguments:
- cache_keys: bfloat16 [131072, 1024], P(('groups', 'seq')), parts along dimension 0, may hold values from -48 to 48
- cache_values: bfloat16 [131072, 1024], P(('groups', 'seq')), parts along dimension 0, may hold values from -6 to 6
- sketch_matrix: float32 [1024, 160], replicated, may hold values from -6 to 6
- queries: bfloat16 [6, 8192], P('groups'), parts along dimension 0, may hold values from -2000 to 2000
- fresh_keys: bfloat16 [6, 1024], P('groups'), parts along dimension 0, may hold values from -20 to 20
- fresh_values: bfloat16 [6, 1024], P('groups'), parts along dimension 0, may hold values from -6 to 6
- chosen: int32 [6, 8, 256], P('groups'), parts along dimension 0, may hold values from 0 to 8191, as said below
- shard_counts: int32 [6, 8, 16], P('groups'), parts along dimension 0, may hold values from 0 to 48, as said below
- outliers: int32 [64], P('groups'), parts along dimension 0, may hold values from 0 to 8191, as said below
Outputs:
- attended: bfloat16 [6, 8192], P('groups', 'seq'), parts along dimension 0
- key_factor: float32 [131072, 160], P(('groups', 'seq')), parts along dimension 0
There are 2 independent parts, one for each index of `groups`. A program takes and returns all parts, laid end to end along the dimension named above; an argument that names none is the same for every part. Nothing has to cross between parts.
Inputs may be any that keep to these rules, and one draw needn't show every extreme that they name: Each list chosen[t, g] holds distinct span numbers in ascending order, none of them an outlier span; shard s holds spans s * 512 to (s+1) * 512 - 1. shard_counts[t, g, s] is the number of entries of chosen[t, g] on shard s; they sum to 256; the most is 48, reached in every list. `outliers`: distinct span numbers in ascending order; at most 4 on one shard, reached on some shard.
All inputs are finite; a program needn't handle non-finite values.
Results may differ from a plain program's by a relative error of at most 0.0228.
Values may be sent and summed in bfloat16 or wider, within the bound.
No kernel may reach another device: no remote copies, remote signals or barrier semaphores. Data moves between devices by JAX's collectives and lax.ppermute only.
A program may use at most 128 MiB of HBM per device.

v0:
```python
import functools

import jax
import jax.numpy as jnp
from jax import lax
from jax.experimental import pallas as pl
from jax.experimental.pallas import tpu as pltpu
from jax.sharding import PartitionSpec as P

KVH = 8
HD = 128
QH = 64
SPAN = 8
OMOST = 4
BF = jnp.bfloat16
F32 = jnp.float32
DEAD = -1e30
LANES = 128
MAIN = 640
PART = 8
AHEAD = 3
NT = (((1,), (1,)), ((), ()))
TN = (((0,), (0,)), ((), ()))


def vmem():
    return pl.BlockSpec(memory_space=pltpu.VMEM)


def smem():
    return pl.BlockSpec(memory_space=pltpu.SMEM)


def hbm():
    return pl.BlockSpec(memory_space=pltpu.HBM)


def in_hbm(x):
    return pltpu.with_memory_space_constraint(x, pltpu.HBM)


def anywhere():
    return pl.BlockSpec(memory_space=pl.ANY)


def round_up(x, m):
    return (x + m - 1) // m * m


def split2(x):
    high = x.astype(BF)
    return high, (x - high.astype(F32)).astype(BF)


def split3(x):
    high = x.astype(BF).astype(F32)
    rest = x - high
    middle = rest.astype(BF).astype(F32)
    return high, middle, rest - middle


def sketch_kernel(
    me_ref, st_hbm, keys_hbm, keep_ref, send_ref, st_ref, keys_ref, acc_ref, st_sem, sem, *, scale, chunk
):
    seq_len = keys_ref.shape[0]
    rank = st_ref.shape[0]
    half = rank // 2
    n = seq_len // chunk
    st_copy = pltpu.make_async_copy(st_hbm, st_ref, st_sem)
    st_copy.start()
    copies = [
        pltpu.make_async_copy(
            keys_hbm.at[pl.ds(i * chunk, chunk)], keys_ref.at[pl.ds(i * chunk, chunk)], sem.at[i]
        )
        for i in range(n)
    ]
    for c in copies[:AHEAD]:
        c.start()
    st_copy.wait()
    st = st_ref[...].astype(BF)

    def rows(i):
        return keys_ref[i * chunk:(i + 1) * chunk, :]

    def first(i):
        return lax.dot_general(st, rows(i), NT, preferred_element_type=F32).astype(BF)

    def second(i, y):
        return jnp.dot(y, rows(i), preferred_element_type=F32)

    def arrive(i):
        copies[i].wait()
        if i + AHEAD < n:
            copies[i + AHEAD].start()

    arrive(0)
    y = first(0)
    for i in range(1, n):
        arrive(i)
        y_next = first(i)
        z = second(i - 1, y)
        if i == 1:
            acc_ref[...] = z
        else:
            acc_ref[...] += z
        y = y_next
    acc_ref[...] = (acc_ref[...] + second(n - 1, y)) * scale
    core = me_ref[0] % 2
    keep_ref[...] = acc_ref[pl.ds(pl.multiple_of(core * half, 8), half), :]
    send_ref[...] = acc_ref[pl.ds(pl.multiple_of((1 - core) * half, 8), half), :]


def sketch_share(me, sketch_t, cache_keys, length):
    seq_len, width = cache_keys.shape
    rank = sketch_t.shape[0]
    chunk = min(512, seq_len)
    half = jax.ShapeDtypeStruct((rank // 2, width), F32)
    return pl.pallas_call(
        functools.partial(sketch_kernel, scale=1.0 / length, chunk=chunk),
        in_specs=[smem(), hbm(), hbm()],
        out_specs=[vmem(), vmem()],
        out_shape=[half, half],
        scratch_shapes=[
            pltpu.VMEM((rank, width), F32),
            pltpu.VMEM((seq_len, width), BF),
            pltpu.VMEM((rank, width), F32),
            pltpu.SemaphoreType.DMA,
            pltpu.SemaphoreType.DMA((seq_len // chunk,)),
        ],
        compiler_params=pltpu.CompilerParams(vmem_limit_bytes=24 << 20),
        name="sketch_share",
    )(me, in_hbm(sketch_t), in_hbm(cache_keys))


def slots_kernel(me_ref, chosen_ref, counts_ref, outl_ref, after_ref, slots_ref, live_ref, tie_ref, *, most, spans, steps):
    me = me_ref[0]
    base = me * spans
    tie_ref[...] = jnp.zeros_like(tie_ref)

    n_out = outl_ref.shape[0]
    o_first = jnp.int32(0)
    o_here = jnp.int32(0)
    for i in range(n_out):
        s = outl_ref[i]
        o_first = o_first + (s < base).astype(jnp.int32)
        o_here = o_here + ((s >= base) & (s < base + spans)).astype(jnp.int32)
    n_at = KVH * (steps + 1)
    live_ref[n_at] = jnp.minimum(o_here, OMOST)
    live_ref[n_at + 1] = me
    for j in range(OMOST):
        live_ref[n_at + 2 + j] = jnp.clip(outl_ref[jnp.minimum(o_first + j, n_out - 1)] - base, 0, spans - 1)

    sel = chosen_ref.shape[1]
    shards = counts_ref.shape[1]
    for g in range(KVH):
        at = jnp.int32(0)
        for t in range(steps):
            i = t * KVH + g
            start = jnp.int32(0)
            for r in range(shards):
                start = start + jnp.where(r < me, counts_ref[i, r], 0)
            count = jnp.minimum(counts_ref[i, me], most)
            live_ref[g * (steps + 1) + t] = at

            def put(k, _, i=i, start=start, at=at, g=g):
                for j in range(PART):
                    slot = k * PART + j
                    picked = chosen_ref[i, jnp.minimum(start + slot, sel - 1)]
                    slots_ref[g, at + slot] = jnp.clip(picked - base, 0, spans - 1)
                return 0

            lax.fori_loop(0, (count + PART - 1) // PART, put, 0)
            at = at + count
        live_ref[g * (steps + 1) + steps] = at
        for j in range(PART):
            slots_ref[g, at + j] = 0


def known_kernel(
    live_ref, q_ref, fk_ref, ca_ref, sa_ref, cb_ref, sb_ref, cq_ref, sq_ref, keys_hbm, after_ref,
    kx_ref, w_ref, tie_ref,
    okeys_ref, xtmp_ref, qtmp_ref, osem, *, per_device, rp
):
    steps = q_ref.shape[0]
    tie_ref[...] = jnp.zeros_like(tie_ref)
    n_at = KVH * (steps + 1)
    o_span = [live_ref[n_at + 2 + j] for j in range(OMOST)]
    o_copies = [
        pltpu.make_async_copy(
            keys_hbm.at[pl.ds(pl.multiple_of(o_span[j] // 2 * 16, 16), 16)], okeys_ref.at[j], osem.at[j]
        )
        for j in range(OMOST)
    ]
    for c in o_copies:
        c.start()

    lane = lax.broadcasted_iota(jnp.int32, (8, LANES), 1)
    sign = jnp.where(lane < HD // 2, -1.0, 1.0)

    qtmp_ref[...] = jnp.zeros_like(qtmp_ref)
    for t in range(steps):
        x = q_ref[t:t + 1, :].astype(F32)
        for h in range(QH):
            r = h // per_device * rp + t * per_device + h % per_device
            qtmp_ref[r:r + 1, :] = x[:, h * HD:(h + 1) * HD]
    scale = 1.0 / (HD ** 0.5)
    row = lax.broadcasted_iota(jnp.int32, (LANES, LANES), 0) % rp
    lane_r = lax.broadcasted_iota(jnp.int32, (LANES, LANES), 1)
    cq = jnp.zeros((LANES, LANES), F32)
    sq = jnp.zeros((LANES, LANES), F32)
    for t in range(steps):
        here = (row >= t * per_device) & (row < (t + 1) * per_device)
        cq = jnp.where(here, cq_ref[t:t + 1, :] * scale, cq)
        sq = jnp.where(here, sq_ref[t:t + 1, :] * scale, sq)
    sq = jnp.where(lane_r < HD // 2, -sq, sq)
    for pk in range(w_ref.shape[0]):
        x = qtmp_ref[pk * LANES:(pk + 1) * LANES, :]
        x = x * cq + pltpu.roll(x, HD // 2, 1) * sq
        z = jnp.where(lane_r < HD // 2, 1.0, -1.0) * pltpu.roll(x, HD // 2, 1)
        hi, lo = split2(jnp.concatenate([x.T, z.T], 0))
        w_ref[pk] = jnp.concatenate([hi, lo], 0)

    blk = cb_ref.shape[0] // SPAN
    turns = []
    for j in range(OMOST):
        a = o_span[j] // blk
        b = pl.ds(pl.multiple_of(o_span[j] % blk * SPAN, SPAN), SPAN)
        ca, sa = ca_ref[pl.ds(a, 1), :], sa_ref[pl.ds(a, 1), :]
        cb, sb = cb_ref[b, :], sb_ref[b, :]
        turns.append((ca * cb - sa * sb, (sa * cb + ca * sb) * sign))
    for c in o_copies:
        c.wait()
    x_rows = kx_ref.shape[1]
    xtmp_ref[...] = jnp.zeros_like(xtmp_ref)
    fs = sq_ref[:steps, :] * sign[:1]
    for g in range(KVH):
        sl = slice(g * HD, (g + 1) * HD)
        for j in range(OMOST):
            wide = okeys_ref[j, :, sl].astype(F32)
            x = jnp.where(o_span[j] % 2 == 0, wide[:8], wide[8:])
            xtmp_ref[j * SPAN:(j + 1) * SPAN, :] = x * turns[j][0] + pltpu.roll(x, HD // 2, 1) * turns[j][1]
        x = fk_ref[:, sl].astype(F32)
        o = OMOST * SPAN
        xtmp_ref[o:o + steps, :] = x * cq_ref[:steps, :] + pltpu.roll(x, HD // 2, 1) * fs
        kx_ref[g, :, :HD] = xtmp_ref[...].astype(BF)
        kx_ref[g, :, HD:] = jnp.zeros((x_rows, HD), BF)


def values_kernel(
    slots_ref, live_ref, fv_ref, values_hbm, after_ref, vg_ref, tie_ref, values_ref, vtmp_ref, sem, *, main
):
    steps = fv_ref.shape[0]
    rows_all = vtmp_ref.shape[0]
    copies = [
        pltpu.make_async_copy(values_hbm.at[:, pl.ds(g * HD, HD)], values_ref.at[g], sem.at[g]) for g in range(KVH)
    ]
    for c in copies[:AHEAD]:
        c.start()
    tie_ref[...] = jnp.zeros_like(tie_ref)
    vtmp_ref[...] = jnp.zeros_like(vtmp_ref)
    n_at = KVH * (steps + 1)

    for g in range(KVH):
        def rows_of(span, g=g):
            wide = values_ref[g, pl.ds(pl.multiple_of(span // 2 * 16, 16), 16), :].astype(F32)
            return jnp.where(span % 2 == 0, wide[:8], wide[8:])

        copies[g].wait()
        if g + AHEAD < KVH:
            copies[g + AHEAD].start()
        for j in range(OMOST):
            vtmp_ref[j * SPAN:(j + 1) * SPAN, :] = rows_of(live_ref[n_at + 2 + j])
        vtmp_ref[OMOST * SPAN:OMOST * SPAN + steps, :] = fv_ref[:, g * HD:(g + 1) * HD].astype(F32)
        count = live_ref[g * (steps + 1) + steps]

        def put(k, _, g=g, rows_of=rows_of):
            for j in range(PART):
                o = pl.multiple_of(LANES + (k * PART + j) * SPAN, SPAN)
                vtmp_ref[pl.ds(o, SPAN), :] = rows_of(slots_ref[g, k * PART + j])
            return 0

        lax.fori_loop(0, (count + PART - 1) // PART, put, 0)
        vg_ref[g, :LANES + main, :] = vtmp_ref[:LANES + main, :].astype(BF)
        if LANES + main < rows_all:
            def more(k, _, g=g):
                at = pl.ds(pl.multiple_of(LANES + main + k * LANES, LANES), LANES)
                vg_ref[g, at, :] = vtmp_ref[at, :].astype(BF)
                return 0

            lax.fori_loop(0, (jnp.maximum(count * SPAN - main, 0) + LANES - 1) // LANES, more, 0)


def attend_kernel(
    core_ref, slots_ref, live_ref, zmine_ref, zother_ref, kx_ref, w_ref, vg_ref, ca_ref, sa_ref, cb_ref, sb_ref,
    keys_hbm,
    kft_hbm, out_ref,
    keys_ref, z_ref, a_ref, qt_ref, kf_ref, kft_ref, kg_ref, cg_ref, sg_ref, sc_ref,
    sem, out_sem, *, per_device, steps, main, stop=9
):
    rank, width = z_ref.shape
    half = rank // 2
    seq_len = keys_ref.shape[0]
    load = pltpu.make_async_copy(keys_hbm, keys_ref, sem)
    load.start()

    core = core_ref[0] % 2
    z_ref[pl.ds(pl.multiple_of(core * half, 16), half), :] = zmine_ref[...]
    z_ref[pl.ds(pl.multiple_of((1 - core) * half, 16), half), :] = zother_ref[...]
    basis(z_ref, a_ref, qt_ref)
    qt = qt_ref[...]

    load.wait()
    if stop == 1:
        return
    chunk = seq_len // KVH
    for i in range(KVH):
        rows = slice(i * chunk, (i + 1) * chunk)
        kf = lax.dot_general(keys_ref[rows, :], qt, NT, preferred_element_type=F32)
        kf_ref[rows, :] = kf
        kft_ref[:, rows] = kf.T
    store = pltpu.make_async_copy(kft_ref, kft_hbm, out_sem)
    store.start()
    if stop == 2:
        store.wait()
        return

    blk = cb_ref.shape[0] // SPAN
    totals = [live_ref[g * (steps + 1) + steps] for g in range(KVH)]
    for g in range(KVH):
        def gather(k, _, g=g):
            for j in range(PART):
                slot = k * PART + j
                span = slots_ref[g, slot]
                src = pl.ds(pl.multiple_of(span * SPAN, SPAN), SPAN)
                dst = pl.ds(pl.multiple_of(slot * SPAN, SPAN), SPAN)
                kg_ref[g, dst, :] = kf_ref[src, :]
                a = span // blk
                b = pl.ds(pl.multiple_of(span % blk * SPAN, SPAN), SPAN)
                ca, sa = ca_ref[pl.ds(a, 1), :], sa_ref[pl.ds(a, 1), :]
                cb, sb = cb_ref[b, :], sb_ref[b, :]
                cg_ref[g, dst, :] = ca * cb - sa * sb
                sg_ref[g, dst, :] = sa * cb + ca * sb
            return 0

        lax.fori_loop(0, (totals[g] + PART - 1) // PART, gather, 0)
    if stop == 3:
        store.wait()
        return

    n_dest, rp, _ = out_ref.shape
    dests = n_dest // KVH
    qr = dests * rp
    heads = LANES // qr
    packs = w_ref.shape[0]
    n_at = KVH * (steps + 1)
    o_live = live_ref[n_at] * SPAN
    first_shard = live_ref[n_at + 1] == 0
    column = lax.broadcasted_iota(jnp.int32, (8, LANES), 1)[:1]
    col_head = column // qr
    col_row = column % rp
    col_step = col_row // per_device

    def bounds(pk, h):
        first = jnp.full((1, LANES), 1 << 30, jnp.int32)
        last = jnp.zeros((1, LANES), jnp.int32)
        for t in range(steps):
            at = (pk * heads + h) * (steps + 1) + t
            here = (col_head == h) & (col_step == t)
            first = jnp.where(here, live_ref[at] * SPAN, first)
            last = jnp.where(here, live_ref[at + 1] * SPAN, last)
        return first, last

    def product(pk, y):
        return jnp.dot(jnp.concatenate([y, y], 1), w_ref[pk], preferred_element_type=F32)

    token = lax.broadcasted_iota(jnp.int32, (LANES, LANES), 0)

    def slot_scores(pk, at, limits):
        s = jnp.full((LANES, LANES), DEAD, F32)
        rows = pl.ds(at, LANES)
        for h in range(heads):
            g = pk * heads + h
            x = jnp.dot(kg_ref[g, rows, :].astype(BF), qt_ref[:, g * HD:(g + 1) * HD], preferred_element_type=F32)
            y = jnp.concatenate([(x * cg_ref[g, rows, :]).astype(BF), (x * sg_ref[g, rows, :]).astype(BF)], 1)
            first, last = limits[h]
            here = token + at
            s = jnp.where((here >= first) & (here < last), product(pk, y), s)
        return s

    def known_scores(pk):
        s = jnp.full((LANES, LANES), DEAD, F32)
        new = token - OMOST * SPAN
        is_live = (token < o_live) | (first_shard & (new >= 0) & (new <= col_step))
        is_live = is_live & (new < steps) & (col_row < steps * per_device)
        for h in range(heads):
            s = jnp.where(is_live & (col_head == h), product(pk, kx_ref[pk * heads + h]), s)
        return s

    limits = [[bounds(pk, h) for h in range(heads)] for pk in range(packs)]
    extra = kg_ref.shape[1] - main
    blocks = []
    for pk in range(packs):
        most = functools.reduce(jnp.maximum, totals[pk * heads:(pk + 1) * heads])
        blocks.append((jnp.maximum(most * SPAN - main, 0) + LANES - 1) // LANES)

    tops = []
    for pk in range(packs):
        s = known_scores(pk)
        sc_ref[pk, :LANES, :] = s
        top = s
        for at in range(0, main, LANES):
            s = slot_scores(pk, at, limits[pk])
            sc_ref[pk, LANES + at:2 * LANES + at, :] = s
            top = jnp.maximum(top, s)
        tops.append(jnp.max(top, axis=0, keepdims=True))
    if extra > 0:
        for pk in range(packs):
            def more(k, top, pk=pk):
                at = pl.multiple_of(main + k * LANES, LANES)
                s = slot_scores(pk, at, limits[pk])
                sc_ref[pk, pl.ds(pl.multiple_of(LANES + at, LANES), LANES), :] = s
                return jnp.maximum(top, jnp.max(s, axis=0, keepdims=True))

            tops[pk] = lax.fori_loop(0, blocks[pk], more, tops[pk])
    if stop == 4:
        store.wait()
        return

    used = steps * per_device

    def weights(s, top):
        return jnp.where(s > 0.5 * DEAD, jnp.exp(s - top), 0.0)

    def weighted(pt, h, values):
        hi, lo = split2(pt[h * qr:(h + 1) * qr, :])
        r = jnp.dot(jnp.concatenate([hi, lo], 0), values, preferred_element_type=F32)
        return r[:qr] + r[qr:]

    sums = []
    for pk in range(packs):
        pts = []
        total = jnp.zeros((LANES, LANES), F32)
        for at in range(0, LANES + main, LANES):
            p = weights(sc_ref[pk, at:at + LANES, :], tops[pk])
            total = total + p
            pts.append(p.T)
        sums.append(jnp.sum(total, axis=0, keepdims=True))
        pt = jnp.concatenate(pts, 1)
        for h in range(heads):
            g = pk * heads + h
            acc = weighted(pt, h, vg_ref[g, :LANES + main, :])
            for a in range(dests):
                out_ref[g * dests + a] = acc[a * rp:(a + 1) * rp]
    if extra > 0:
        for pk in range(packs):
            def add(k, total, pk=pk):
                at = pl.multiple_of(LANES + main + k * LANES, LANES)
                p = weights(sc_ref[pk, pl.ds(at, LANES), :], tops[pk])
                pt = p.T
                for h in range(heads):
                    g = pk * heads + h

                    @pl.when(totals[g] * SPAN > main + k * LANES)
                    def _():
                        acc = weighted(pt, h, vg_ref[g, pl.ds(at, LANES), :])
                        for a in range(dests):
                            out_ref[g * dests + a] += acc[a * rp:(a + 1) * rp]

                return total + jnp.sum(p, axis=0, keepdims=True)

            sums[pk] = lax.fori_loop(0, blocks[pk], add, sums[pk])
    for d in range(n_dest):
        pk = d // (heads * dests)
        out_ref[d, used:used + 1, :] = tops[pk]
        out_ref[d, used + 1:used + 2, :] = sums[pk]
    store.wait()


def basis(z_ref, a_ref, qt_ref):
    rank = z_ref.shape[0]
    wide = round_up(rank, LANES)
    z = z_ref[...]
    c = lax.dot_general(z, z, NT, preferred_element_type=F32)
    rows = lax.broadcasted_iota(jnp.int32, (rank, wide), 0)
    cols = lax.broadcasted_iota(jnp.int32, (rank, wide), 1)
    a_ref[:, :wide] = jnp.where(rows == cols, 1.0, 0.0)
    a_ref[:, wide:wide + rank] = c
    a_ref[:, wide + rank:] = jnp.zeros((rank, wide - rank), F32)
    nb = 32
    half_tiles = wide // LANES
    for j0 in range(0, rank, nb):
        tiles = [t for t in range(half_tiles) if t * LANES < j0 + nb]
        tiles += [half_tiles + t for t in range(half_tiles) if (t + 1) * LANES > j0]
        part = {t: a_ref[j0:j0 + nb, t * LANES:(t + 1) * LANES] for t in tiles}
        row = lax.broadcasted_iota(jnp.int32, (nb, LANES), 0)
        column = []
        for j in range(nb):
            t, o = divmod(j0 + j, LANES)
            column.append(jnp.broadcast_to(part[half_tiles + t][:, o:o + 1], (nb, LANES)))
        for j in range(nb):
            inverse = lax.rsqrt(jnp.broadcast_to(column[j][j:j + 1, :], (nb, LANES)))
            low = jnp.where(row > j, column[j] * inverse, 0.0)
            for k in range(j + 1, nb):
                column[k] = column[k] - low * jnp.broadcast_to(low[k:k + 1, :], (nb, LANES))
            for t in tiles:
                upper = jnp.broadcast_to(part[t][j:j + 1, :], (nb, LANES)) * inverse
                part[t] = jnp.where(row == j, upper, part[t] - low * upper)
        for t in tiles:
            a_ref[j0:j0 + nb, t * LANES:(t + 1) * LANES] = part[t]
        if j0 + nb < rank:
            upper = jnp.concatenate(
                [part[t] if t in part else jnp.zeros((nb, LANES), F32) for t in range(2 * half_tiles)], 1
            )
            h, m, l = split3(upper)
            left = jnp.concatenate([h, h, m, m, h, l], 0)[:, wide:].astype(BF)
            right = jnp.concatenate([h, m, h, m, l, h], 0).astype(BF)
            for s in range(2):
                d = lax.dot_general(left, right[:, s * wide:(s + 1) * wide], TN, preferred_element_type=F32)
                a_ref[j0 + nb:, s * wide:(s + 1) * wide] -= d[j0 + nb:rank]
    h, m, _ = split3(a_ref[:, :rank])
    q = jnp.dot(jnp.concatenate([h, m], 0).astype(BF), z, preferred_element_type=F32)
    qt_ref[...] = (q[:rank] + q[rank:]).astype(BF)


def attend_call(
    me, slots, live, z, z_other, kx, w, vg, ca, sa, cb, sb, cache_keys,
    *, steps, per_device, main, rp, n_dest, stop=9
):
    seq_len, width = cache_keys.shape
    rank = 2 * z.shape[0]
    tok_all = vg.shape[1] - LANES
    return pl.pallas_call(
        functools.partial(attend_kernel, per_device=per_device, steps=steps, main=main, stop=stop),
        in_specs=[smem()] * 3 + [vmem()] * 9 + [hbm()],
        out_specs=[hbm(), vmem()],
        out_shape=[
            jax.ShapeDtypeStruct((rank, seq_len), F32),
            jax.ShapeDtypeStruct((n_dest, rp, HD), F32),
        ],
        scratch_shapes=[
            pltpu.VMEM((seq_len, width), BF),
            pltpu.VMEM((rank, width), BF),
            pltpu.VMEM((rank, 2 * round_up(rank, LANES)), F32),
            pltpu.VMEM((rank, width), BF),
            pltpu.VMEM((seq_len, rank), F32),
            pltpu.VMEM((rank, seq_len), F32),
            pltpu.VMEM((KVH, tok_all, rank), F32),
            pltpu.VMEM((KVH, tok_all, HD), F32),
            pltpu.VMEM((KVH, tok_all, HD), F32),
            pltpu.VMEM((w.shape[0], LANES + tok_all, LANES), F32),
            pltpu.SemaphoreType.DMA,
            pltpu.SemaphoreType.DMA,
        ],
        compiler_params=pltpu.CompilerParams(vmem_limit_bytes=42 << 20),
        name="attend",
    )(me, slots, live, z, z_other, kx, w, vg, ca, sa, cb, sb, in_hbm(cache_keys))


def merge_kernel(me_ref, parts_ref, out_ref, *, steps, per_device):
    n, rp, _ = parts_ref.shape
    used = steps * per_device
    shift = me_ref[0] % (LANES // rp) * rp
    eye = lax.broadcasted_iota(jnp.int32, (rp, LANES), 0) + shift == lax.broadcasted_iota(jnp.int32, (rp, LANES), 1)

    def column(s, r):
        return jnp.sum(jnp.where(eye, parts_ref[s, r:r + 1, :], 0.0), axis=1, keepdims=True)

    ms = [column(s, used) for s in range(n)]
    top = functools.reduce(jnp.maximum, ms)
    total = jnp.zeros((rp, 1), F32)
    acc = jnp.zeros((rp, HD), F32)
    for s in range(n):
        w = jnp.exp(ms[s] - top)
        total = total + w * column(s, used + 1)
        acc = acc + w * parts_ref[s]
    o = acc / total
    for t in range(steps):
        for i in range(per_device):
            r = t * per_device + i
            out_ref[t:t + 1, i * HD:(i + 1) * HD] = o[r:r + 1, :].astype(BF)


def swap(x, moves):
    return lax.ppermute(x, "seq", moves)


def on_device(
    cache_keys,
    cache_values,
    sketch_matrix,
    queries,
    fresh_keys,
    fresh_values,
    chosen,
    shard_counts,
    outliers,
):
    seq_len, width = cache_keys.shape
    devices = lax.axis_size("seq")
    myself = lax.axis_index("seq")
    length = seq_len * devices
    steps = queries.shape[0]
    rank = sketch_matrix.shape[1]
    per_device = QH // devices
    n_lists = steps * KVH
    most = 3 * chosen.shape[2] // devices
    slots_all = round_up(steps * most, LANES // SPAN)
    tok_all = slots_all * SPAN
    main = min(MAIN, tok_all)
    used = steps * per_device
    rp = round_up(used + 2, 8)
    n_dest = devices
    me = jnp.full((1,), myself, jnp.int32)

    keep, send = sketch_share(me, sketch_matrix.T, cache_keys, length)

    half_width = HD // 2
    exponents = jnp.arange(half_width, dtype=F32) * (2.0 / HD)
    inverse_freq = jnp.exp(-jnp.log(F32(500000.0)) * exponents)
    inverse_freq = jnp.concatenate([inverse_freq, inverse_freq])
    blk = 64
    coarse = (myself * seq_len + blk * jnp.arange(seq_len // blk, dtype=jnp.int32)).astype(F32)[:, None] * inverse_freq
    fine = jnp.arange(blk, dtype=jnp.int32).astype(F32)[:, None] * inverse_freq
    late = (length + jnp.arange(steps, dtype=jnp.int32)).astype(F32)[:, None] * inverse_freq
    turns = (jnp.cos(coarse), jnp.sin(coarse), jnp.cos(fine), jnp.sin(fine))

    tie_shape = jax.ShapeDtypeStruct((1, LANES), F32)

    def find_slots(after):
        return pl.pallas_call(
            functools.partial(slots_kernel, most=most, spans=seq_len // SPAN, steps=steps),
            in_specs=[smem()] * 4 + [anywhere()],
            out_specs=[smem()] * 2 + [vmem()],
            out_shape=[
                jax.ShapeDtypeStruct((KVH, slots_all + 2 * PART), jnp.int32),
                jax.ShapeDtypeStruct((KVH * (steps + 1) + 2 + OMOST,), jnp.int32),
                tie_shape,
            ],
            name="find_slots",
        )(me, chosen.reshape(n_lists, -1), shard_counts.reshape(n_lists, -1), outliers, after)

    def known(live, after):
        return pl.pallas_call(
            functools.partial(known_kernel, per_device=per_device, rp=rp),
            in_specs=[smem()] + [vmem()] * 8 + [hbm(), anywhere()],
            out_specs=[vmem()] * 3,
            out_shape=[
                jax.ShapeDtypeStruct((KVH, LANES, 2 * HD), BF),
                jax.ShapeDtypeStruct((n_dest * rp // LANES, 4 * HD, LANES), BF),
                tie_shape,
            ],
            scratch_shapes=[
                pltpu.VMEM((OMOST, 16, width), BF),
                pltpu.VMEM((LANES, HD), F32),
                pltpu.VMEM((n_dest * rp, HD), F32),
                pltpu.SemaphoreType.DMA((OMOST,)),
            ],
            compiler_params=pltpu.CompilerParams(vmem_limit_bytes=8 << 20),
            name="known_keys",
        )(live, queries, fresh_keys, *turns, jnp.cos(late), jnp.sin(late), in_hbm(cache_keys), after)

    def slot_values(slots, live, after):
        return pl.pallas_call(
            functools.partial(values_kernel, main=main),
            in_specs=[smem()] * 2 + [vmem(), hbm(), anywhere()],
            out_specs=[vmem()] * 2,
            out_shape=[jax.ShapeDtypeStruct((KVH, LANES + tok_all, HD), BF), tie_shape],
            scratch_shapes=[
                pltpu.VMEM((KVH, seq_len, HD), BF),
                pltpu.VMEM((LANES + tok_all, HD), F32),
                pltpu.SemaphoreType.DMA((KVH,)),
            ],
            compiler_params=pltpu.CompilerParams(vmem_limit_bytes=16 << 20),
            name="slot_values",
        )(slots, live, fresh_values, in_hbm(cache_values), after)

    z = keep + swap(send, [(i, i ^ 1) for i in range(devices)])
    hops = [1 << k for k in range(1, devices.bit_length() - 1)]
    for k in range(len(hops)):
        other = k ^ 1 if k < 2 and len(hops) >= 2 else k
        moves = [(i, i ^ hops[k if i % 2 == 0 else other]) for i in range(devices)]
        going = z.astype(BF)
        came = swap(going, moves).astype(F32)
        if k == 0:
            slots, live, tie = find_slots(going)
            came = came + tie[0, 0]
        if k == min(1, len(hops) - 1):
            kx, w, tie = known(live, going)
            came = came + tie[0, 0]
        if k == len(hops) - 1:
            vg, tie = slot_values(slots, live, going)
            came = came + tie[0, 0]
        z = z + came
    z = z.astype(BF)
    z_other = swap(z, [(i, i ^ 1) for i in range(devices)])

    kft, parts = attend_call(
        me, slots, live, z, z_other, kx, w, vg, *turns, cache_keys,
        steps=steps, per_device=per_device, main=main, rp=rp, n_dest=n_dest,
    )
    parts = lax.all_to_all(parts, "seq", 0, 0, tiled=True)
    attended = pl.pallas_call(
        functools.partial(merge_kernel, steps=steps, per_device=per_device),
        in_specs=[smem(), vmem()],
        out_specs=vmem(),
        out_shape=jax.ShapeDtypeStruct((steps, per_device * HD), BF),
        name="merge",
    )(me, parts)
    return (attended, kft.T)


def solution(mesh):
    in_specs = (
        P(("groups", "seq"), None),
        P(("groups", "seq"), None),
        P(),
        P("groups", None),
        P("groups", None),
        P("groups", None),
        P("groups", None, None),
        P("groups", None, None),
        P("groups"),
    )
    out_specs = (P("groups", "seq"), P(("groups", "seq"), None))
    return jax.shard_map(
        on_device, mesh=mesh, in_specs=in_specs, out_specs=out_specs, check_vma=False
    )
```

profile of v0, /device:TPU:0, one launch (start us, length us, event | category | flops | bytes accessed | tf_op | source)
XLA Modules:
  0.0 77.3 jit_solution(2468988094326555854)
XLA Ops:
  0.6 0.0 copy-start.2
  0.6 0.0 copy-start
  0.7 0.0 copy-start.3
  0.7 6.6 %sketch_share.1 = (f32[80,1024]{1,0:T(8,128)S(1)}, f32[80,1024]{1,0:T(8,128)S(1)}) custom-call(s32[1]{0:T(128)} %bitcast.me_ref.core_ref, f32[160,1024]{1,0:T(8,128)} %bitcast.14, bf16[4096,1024]{1,0:T(8,128)(2,1)} %keys_hbm.5), custom_call_target="tpu_custom_call" | custom-call | tf_op jit(solution)/shard_map/sketch_share/pallas_call | solution.py:118
  7.3 0.5 collective-permute-start
  7.8 0.1 pad_maximum_fusion
  7.9 1.2 %collective-permute-done = f32[80,1024]{1,0:T(8,128)S(1)} collective-permute-done((f32[80,1024]{1,0:T(8,128)S(1)}, f32[80,1024]{1,0:T(8,128)S(1)}, u32[]{:S(2)}, u32[]{:S(2)}) %collective-permute-start) | collective-permute-done | bytes 327712 | tf_op jit(solution)/shard_map/ppermute | solution.py:584
  9.1 0.0 copy-start.5
  9.1 3.0 %collective-permute-start.1 = (bf16[80,1024]{1,0:T(8,128)(2,1)S(1)}, bf16[80,1024]{1,0:T(8,128)(2,1)S(1)}, u32[]{:S(2)}, u32[]{:S(2)}) collective-permute-start(bf16[80,1024]{1,0:T(8,128)(2,1)S(1)} %get-tuple-element.26.after_ref), channel_id=1, source_target_pairs={{0,2},{1,5},{2,0},{3,7},{4,6},{5,1},{6,4},{7,3},{8,10},{9,13},{10,... | collective-permute-start | bytes 491528 | tf_op jit(solution)/shard_map/ppermute | solution.py:584
  12.1 0.3 multiply_sine_fusion
  12.4 0.0 copy-done.5
  12.4 6.2 %find_slots.1 = (s32[8,160]{1,0:T(8,128)}, s32[38]{0:T(128)}, f32[1,128]{1,0:T(1,128)}) custom-call(s32[1]{0:T(128)} %bitcast.me_ref.core_ref, s32[24,256]{1,0:T(8,128)} %bitcast.15, s32[24,16]{1,0:T(8,128)} %bitcast.16, s32[32]{0:T(128)} %outl_ref.1, bf16[80,1024]{1,0:T(8,128)(2,1)} %copy-done.5), custom_call_target="tpu_custom_call" | custom-call | tf_op jit(solution)/shard_map/find_slots/pallas_call | solution.py:630
  18.6 0.0 copy-start.6
  18.6 0.0 copy-start.1
  18.6 0.0 collective-permute-done.1
  18.6 0.7 fusion.after_ref
  19.3 0.7 collective-permute-start.2
  20.0 0.1 multiply_sine_fusion.2
  20.1 0.0 copy-done.2
  20.1 0.0 copy-done
  20.1 0.0 copy-start.4
  20.1 0.6 copy-done.4
  20.8 1.8 %known_keys.1 = (bf16[8,128,256]{2,1,0:T(8,128)(2,1)S(1)}, bf16[2,512,128]{2,1,0:T(8,128)(2,1)S(1)}, f32[1,128]{1,0:T(1,128)S(1)}) custom-call(s32[38]{0:T(128)S(1)} %copy-done.4, bf16[3,8192]{1,0:T(4,128)(2,1)S(1)} %copy-done, bf16[3,1024]{1,0:T(4,128)(2,1)S(1)} %copy-done.2, f32[64,128]{1,0:T(8,128)S(1)} %get-tuple-element.34.ca_ref, ...), custom_call_target="tpu_custom_call" | custom-call | tf_op jit(solution)/shard_map/known_keys/pallas_call | solution.py:643
  22.5 2.1 %collective-permute-done.2 = bf16[80,1024]{1,0:T(8,128)(2,1)S(1)} collective-permute-done((bf16[80,1024]{1,0:T(8,128)(2,1)S(1)}, bf16[80,1024]{1,0:T(8,128)(2,1)S(1)}, u32[]{:S(2)}, u32[]{:S(2)}) %collective-permute-start.2) | collective-permute-done | bytes 163872 | tf_op jit(solution)/shard_map/ppermute | solution.py:584
  24.7 0.0 copy-done.6
  24.7 0.1 fusion.1.after_ref
  24.8 2.3 %collective-permute-start.3 = (bf16[80,1024]{1,0:T(8,128)(2,1)S(1)}, bf16[80,1024]{1,0:T(8,128)(2,1)S(1)}, u32[]{:S(2)}, u32[]{:S(2)}) collective-permute-start(bf16[80,1024]{1,0:T(8,128)(2,1)S(1)} %fusion.1.after_ref), channel_id=1, source_target_pairs={{0,8},{1,9},{2,10},{3,11},{4,12},{5,13},{6,14},{7,15},{8,0},{9,1},... | collective-permute-start | bytes 491528 | tf_op jit(solution)/shard_map/ppermute | solution.py:584
  27.1 0.0 copy-done.3
  27.1 0.0 copy-done.1
  27.1 6.9 %slot_values.1 = (bf16[8,1280,128]{2,1,0:T(8,128)(2,1)S(1)}, f32[1,128]{1,0:T(1,128)S(1)}) custom-call(s32[8,160]{1,0:T(8,128)S(1)} %copy-done.1, s32[38]{0:T(128)S(1)} %copy-done.4, bf16[3,1024]{1,0:T(4,128)(2,1)S(1)} %copy-done.3, bf16[4096,1024]{1,0:T(8,128)(2,1)} %values_hbm.1, bf16[80,1024]{1,0:T(8,128)(2,1)S(1)} %fusion.1.after_ref), custom_call_target="tpu_custom_call" | custom-call | tf_op jit(solution)/shard_map/slot_values/pallas_call | solution.py:663
  34.0 0.0 collective-permute-done.3
  34.0 0.1 add_convert_fusion.zmine_ref
  34.1 0.1 collective-permute-start.4
  34.2 1.4 %collective-permute-done.4.zother_ref = bf16[80,1024]{1,0:T(8,128)(2,1)S(1)} collective-permute-done((bf16[80,1024]{1,0:T(8,128)(2,1)S(1)}, bf16[80,1024]{1,0:T(8,128)(2,1)S(1)}, u32[]{:S(2)}, u32[]{:S(2)}) %collective-permute-start.4) | collective-permute-done | bytes 163872 | tf_op jit(solution)/shard_map/ppermute | solution.py:584
  35.6 21.7 %attend.1 = (f32[160,4096]{1,0:T(8,128)}, f32[16,16,128]{2,1,0:T(8,128)S(1)}) custom-call(s32[1]{0:T(128)} %bitcast.me_ref.core_ref, s32[8,160]{1,0:T(8,128)S(1)} %copy-done.1, s32[38]{0:T(128)S(1)} %copy-done.4, bf16[80,1024]{1,0:T(8,128)(2,1)S(1)} %add_convert_fusion.zmine_ref, bf16[80,1024]{1,0:T(8,128)(2,1)S(1)} %collective-permute-done.4.zother_ref, ...), custom_call_target="tpu_custom_call" | custom-call | tf_op jit(solution)/shard_map/attend/pallas_call | solution.py:532
  57.3 18.3 %all_to_all.5.parts_ref = f32[16,16,128]{2,1,0:T(8,128)} all-to-all(f32[16,16,128]{2,1,0:T(8,128)S(1)} %get-tuple-element.24), channel_id=1, replica_groups=mesh['groups'=2,'seq'=16] {'seq'}, dimensions={0} | all-to-all | bytes 262144 | tf_op jit(solution)/shard_map/all_to_all | solution.py:701
  75.6 1.7 %merge.1 = bf16[3,512]{1,0:T(4,128)(2,1)} custom-call(s32[1]{0:T(128)} %bitcast.me_ref.core_ref, f32[16,16,128]{2,1,0:T(8,128)} %all_to_all.5.parts_ref), custom_call_target="tpu_custom_call" | custom-call | tf_op jit(solution)/shard_map/merge/pallas_call | solution.py:702
  (5 shorter events, 0.1 us)
Async XLA Ops:
  0.6 19.5 %copy-start.2 = (bf16[3,1024]{1,0:T(4,128)(2,1)S(1)}, bf16[3,1024]{1,0:T(4,128)(2,1)}, u32[]{:S(2)}) copy-start(bf16[3,1024]{1,0:T(4,128)(2,1)} %fk_ref.1) | copy-start | bytes 18436
  0.6 19.5 %copy-start = (bf16[3,8192]{1,0:T(4,128)(2,1)S(1)}, bf16[3,8192]{1,0:T(4,128)(2,1)}, u32[]{:S(2)}) copy-start(bf16[3,8192]{1,0:T(4,128)(2,1)} %q_ref.1) | copy-start | bytes 147460
  0.7 26.4 %copy-start.3 = (bf16[3,1024]{1,0:T(4,128)(2,1)S(1)}, bf16[3,1024]{1,0:T(4,128)(2,1)}, u32[]{:S(2)}) copy-start(bf16[3,1024]{1,0:T(4,128)(2,1)} %fv_ref.1) | copy-start | bytes 18436
  7.3 1.8 %collective-permute-start = (f32[80,1024]{1,0:T(8,128)S(1)}, f32[80,1024]{1,0:T(8,128)S(1)}, u32[]{:S(2)}, u32[]{:S(2)}) collective-permute-start(f32[80,1024]{1,0:T(8,128)S(1)} %get-tuple-element.15), channel_id=1, source_target_pairs={{0,1},{1,0},{2,3},{3,2},{4,5},{5,4},{6,7},{7,6},{8,9},{9,8},{10,11... | collective-permute-start | bytes 983048 | tf_op jit(solution)/shard_map/ppermute | solution.py:584
  9.1 3.3 %copy-start.5 = (bf16[80,1024]{1,0:T(8,128)(2,1)}, bf16[80,1024]{1,0:T(8,128)(2,1)S(1)}, u32[]{:S(2)}) copy-start(bf16[80,1024]{1,0:T(8,128)(2,1)S(1)} %get-tuple-element.26.after_ref) | copy-start | bytes 491524
  9.1 9.5 %collective-permute-start.1 = (bf16[80,1024]{1,0:T(8,128)(2,1)S(1)}, bf16[80,1024]{1,0:T(8,128)(2,1)S(1)}, u32[]{:S(2)}, u32[]{:S(2)}) collective-permute-start(bf16[80,1024]{1,0:T(8,128)(2,1)S(1)} %get-tuple-element.26.after_ref), channel_id=1, source_target_pairs={{0,2},{1,5},{2,0},{3,7},{4,6},{5,1},{6,4},{7,3},{8,10},{9,13},{10,... | collective-permute-start | bytes 491528 | tf_op jit(solution)/shard_map/ppermute | solution.py:584
  18.6 6.1 %copy-start.6 = (f32[1,128]{1,0:T(1,128)S(1)}, f32[1,128]{1,0:T(1,128)}, u32[]{:S(2)}) copy-start(f32[1,128]{1,0:T(1,128)} %get-tuple-element.18) | copy-start | bytes 1540
  18.6 8.5 %copy-start.1 = (s32[8,160]{1,0:T(8,128)S(1)}, s32[8,160]{1,0:T(8,128)}, u32[]{:S(2)}) copy-start(s32[8,160]{1,0:T(8,128)} %get-tuple-element.16.slots_ref) | copy-start | bytes 15364
  19.3 5.4 %collective-permute-start.2 = (bf16[80,1024]{1,0:T(8,128)(2,1)S(1)}, bf16[80,1024]{1,0:T(8,128)(2,1)S(1)}, u32[]{:S(2)}, u32[]{:S(2)}) collective-permute-start(bf16[80,1024]{1,0:T(8,128)(2,1)S(1)} %fusion.after_ref), channel_id=1, source_target_pairs={{0,4},{1,3},{2,6},{3,1},{4,0},{5,7},{6,2},{7,5},{8,12},{9,11},{10,... | collective-permute-start | bytes 491528 | tf_op jit(solution)/shard_map/ppermute | solution.py:584
  20.1 0.7 copy-start.4
  24.8 9.2 %collective-permute-start.3 = (bf16[80,1024]{1,0:T(8,128)(2,1)S(1)}, bf16[80,1024]{1,0:T(8,128)(2,1)S(1)}, u32[]{:S(2)}, u32[]{:S(2)}) collective-permute-start(bf16[80,1024]{1,0:T(8,128)(2,1)S(1)} %fusion.1.after_ref), channel_id=1, source_target_pairs={{0,8},{1,9},{2,10},{3,11},{4,12},{5,13},{6,14},{7,15},{8,0},{9,1},... | collective-permute-start | bytes 491528 | tf_op jit(solution)/shard_map/ppermute | solution.py:584
  34.1 1.5 %collective-permute-start.4 = (bf16[80,1024]{1,0:T(8,128)(2,1)S(1)}, bf16[80,1024]{1,0:T(8,128)(2,1)S(1)}, u32[]{:S(2)}, u32[]{:S(2)}) collective-permute-start(bf16[80,1024]{1,0:T(8,128)(2,1)S(1)} %add_convert_fusion.zmine_ref), channel_id=1, source_target_pairs={{0,1},{1,0},{2,3},{3,2},{4,5},{5,4},{6,7},{7,6},{8,9},{9,8},{10,11... | collective-permute-start | bytes 491528 | tf_op jit(solution)/shard_map/ppermute | solution.py:584
where the time goes:
time: 77.7 us; the launch traced here: 77.3 us
  Pallas kernels  44.9 us (58%)
  blocking collectives  18.3 us (24%)
  starting transfers between devices  6.51 us (8%)
  waiting for transfers between devices  4.67 us (6%)
  other arithmetic  1.47 us (2%)
  between operations  0.82 us (1%)
    pallas_call x1, Pallas kernels, attend_call(): pl.pallas_call(functools.partial(attend_kernel, per_device=per_device, st...  21.7 us
    all_to_all x1, blocking collectives, on_device(): parts = lax.all_to_all(parts, 'seq', 0, 0, tiled=True)  18.3 us
    pallas_call x1, Pallas kernels, slot_values(): pl.pallas_call(functools.partial(values_kernel, main=main), in_specs=[sme...  6.89 us
    pallas_call x1, Pallas kernels, sketch_share(): pl.pallas_call(functools.partial(sketch_kernel, scale=1.0 / length, chunk...  6.62 us
    ppermute x5, starting transfers between devices, swap(): return lax.ppermute(x, 'seq', moves)  6.51 us
    pallas_call x1, Pallas kernels, find_slots(): pl.pallas_call(functools.partial(slots_kernel, most=most, spans=seq_len /...  6.19 us
    ppermute x5, waiting for transfers between devices, swap(): return lax.ppermute(x, 'seq', moves)  4.67 us
    pallas_call x1, Pallas kernels, known(): pl.pallas_call(functools.partial(known_kernel, per_device=per_device, rp=...  1.78 us
  transfers between devices with their start and end apart: 5, of which 3 were waited for; matrix products, arithmetic and copies ran while one was open for 1% of the time, Pallas kernels for 19%

commit v1 on v0

--- a/solution.py
+++ b/solution.py
@@ -18,6 +18,7 @@
 LANES = 128
 MAIN = 640
 PART = 8
+STRAIGHT = 6
 AHEAD = 3
 NT = (((1,), (1,)), ((), ()))
 TN = (((0,), (0,)), ((), ()))
@@ -132,7 +133,7 @@
     )(me, in_hbm(sketch_t), in_hbm(cache_keys))
 
 
-def slots_kernel(me_ref, chosen_ref, counts_ref, outl_ref, after_ref, slots_ref, live_ref, tie_ref, *, most, spans, steps):
+def slots_kernel(me_ref, chosen_ref, place_ref, outl_ref, after_ref, slots_ref, live_ref, tie_ref, *, most, spans, steps):
     me = me_ref[0]
     base = me * spans
     tie_ref[...] = jnp.zeros_like(tie_ref)
@@ -151,25 +152,27 @@
         live_ref[n_at + 2 + j] = jnp.clip(outl_ref[jnp.minimum(o_first + j, n_out - 1)] - base, 0, spans - 1)
 
     sel = chosen_ref.shape[1]
-    shards = counts_ref.shape[1]
+    n_lists = chosen_ref.shape[0]
     for g in range(KVH):
         at = jnp.int32(0)
         for t in range(steps):
             i = t * KVH + g
-            start = jnp.int32(0)
-            for r in range(shards):
-                start = start + jnp.where(r < me, counts_ref[i, r], 0)
-            count = jnp.minimum(counts_ref[i, me], most)
+            start = place_ref[i]
+            count = jnp.minimum(place_ref[n_lists + i], most)
             live_ref[g * (steps + 1) + t] = at
 
             def put(k, _, i=i, start=start, at=at, g=g):
+                found = []
                 for j in range(PART):
-                    slot = k * PART + j
-                    picked = chosen_ref[i, jnp.minimum(start + slot, sel - 1)]
-                    slots_ref[g, at + slot] = jnp.clip(picked - base, 0, spans - 1)
+                    picked = chosen_ref[i, jnp.minimum(start + (k * PART + j), sel - 1)]
+                    found.append(jnp.clip(picked - base, 0, spans - 1))
+                for j in range(PART):
+                    slots_ref[g, at + (k * PART + j)] = found[j]
                 return 0
 
-            lax.fori_loop(0, (count + PART - 1) // PART, put, 0)
+            put(0, 0)
+            put(1, 0)
+            lax.fori_loop(2, (count + PART - 1) // PART, put, 0)
             at = at + count
         live_ref[g * (steps + 1) + steps] = at
         for j in range(PART):
@@ -251,6 +254,7 @@
 ):
     steps = fv_ref.shape[0]
     rows_all = vtmp_ref.shape[0]
+    spans = values_ref.shape[1] // SPAN
     copies = [
         pltpu.make_async_copy(values_hbm.at[:, pl.ds(g * HD, HD)], values_ref.at[g], sem.at[g]) for g in range(KVH)
     ]
@@ -274,12 +278,15 @@
         count = live_ref[g * (steps + 1) + steps]
 
         def put(k, _, g=g, rows_of=rows_of):
-            for j in range(PART):
-                o = pl.multiple_of(LANES + (k * PART + j) * SPAN, SPAN)
-                vtmp_ref[pl.ds(o, SPAN), :] = rows_of(slots_ref[g, k * PART + j])
+            rows = [rows_of(jnp.clip(slots_ref[g, k * PART + j], 0, spans - 1)) for j in range(PART)]
+            dst = pl.ds(pl.multiple_of(LANES + k * (PART * SPAN), PART * SPAN), PART * SPAN)
+            vtmp_ref[dst, :] = jnp.concatenate(rows, 0)
             return 0
 
-        lax.fori_loop(0, (count + PART - 1) // PART, put, 0)
+        straight = min(STRAIGHT, (rows_all - LANES) // (PART * SPAN))
+        for k in range(straight):
+            put(k, 0)
+        lax.fori_loop(straight, (count + PART - 1) // PART, put, 0)
         vg_ref[g, :LANES + main, :] = vtmp_ref[:LANES + main, :].astype(BF)
         if LANES + main < rows_all:
             def more(k, _, g=g):
@@ -294,7 +301,7 @@
     core_ref, slots_ref, live_ref, zmine_ref, zother_ref, kx_ref, w_ref, vg_ref, ca_ref, sa_ref, cb_ref, sb_ref,
     keys_hbm,
     kft_hbm, out_ref,
-    keys_ref, z_ref, a_ref, qt_ref, kf_ref, kft_ref, kg_ref, cg_ref, sg_ref, sc_ref,
+    keys_ref, z_ref, a_ref, qt_ref, kf_ref, kft_ref, kg_ref, cg_ref, sg_ref, sc_ref, cc_ref, ss_ref,
     sem, out_sem, *, per_device, steps, main, stop=9
 ):
     rank, width = z_ref.shape
@@ -306,6 +313,7 @@
     core = core_ref[0] % 2
     z_ref[pl.ds(pl.multiple_of(core * half, 16), half), :] = zmine_ref[...]
     z_ref[pl.ds(pl.multiple_of((1 - core) * half, 16), half), :] = zother_ref[...]
+    turn_tables(ca_ref, sa_ref, cb_ref, sb_ref, cc_ref, ss_ref)
     basis(z_ref, a_ref, qt_ref)
     qt = qt_ref[...]
 
@@ -324,25 +332,25 @@
         store.wait()
         return
 
-    blk = cb_ref.shape[0] // SPAN
     totals = [live_ref[g * (steps + 1) + steps] for g in range(KVH)]
+    spans = seq_len // SPAN
+    parts_all = kg_ref.shape[1] // (PART * SPAN)
+    straight = min(STRAIGHT, parts_all)
     for g in range(KVH):
         def gather(k, _, g=g):
+            got = []
             for j in range(PART):
-                slot = k * PART + j
-                span = slots_ref[g, slot]
+                span = jnp.clip(slots_ref[g, k * PART + j], 0, spans - 1)
                 src = pl.ds(pl.multiple_of(span * SPAN, SPAN), SPAN)
-                dst = pl.ds(pl.multiple_of(slot * SPAN, SPAN), SPAN)
-                kg_ref[g, dst, :] = kf_ref[src, :]
-                a = span // blk
-                b = pl.ds(pl.multiple_of(span % blk * SPAN, SPAN), SPAN)
-                ca, sa = ca_ref[pl.ds(a, 1), :], sa_ref[pl.ds(a, 1), :]
-                cb, sb = cb_ref[b, :], sb_ref[b, :]
-                cg_ref[g, dst, :] = ca * cb - sa * sb
-                sg_ref[g, dst, :] = sa * cb + ca * sb
+                got.append((kf_ref[src, :], cc_ref[src, :], ss_ref[src, :]))
+            for ref, rows in zip((kg_ref, cg_ref, sg_ref), zip(*got)):
+                dst = pl.ds(pl.multiple_of(k * (PART * SPAN), PART * SPAN), PART * SPAN)
+                ref[g, dst, :] = jnp.concatenate(rows, 0).astype(ref.dtype)
             return 0
 
-        lax.fori_loop(0, (totals[g] + PART - 1) // PART, gather, 0)
+        for k in range(straight):
+            gather(k, 0)
+        lax.fori_loop(straight, (totals[g] + PART - 1) // PART, gather, 0)
     if stop == 3:
         store.wait()
         return
@@ -371,20 +379,24 @@
         return first, last
 
     def product(pk, y):
-        return jnp.dot(jnp.concatenate([y, y], 1), w_ref[pk], preferred_element_type=F32)
+        r = jnp.dot(y, w_ref[pk, :2 * HD, :], preferred_element_type=F32)
+        return r + jnp.dot(y, w_ref[pk, 2 * HD:, :], preferred_element_type=F32)
 
     token = lax.broadcasted_iota(jnp.int32, (LANES, LANES), 0)
 
-    def slot_scores(pk, at, limits):
-        s = jnp.full((LANES, LANES), DEAD, F32)
-        rows = pl.ds(at, LANES)
+    def slot_scores(pk, at, n, limits):
+        rows = pl.ds(at, n)
+        ys = []
         for h in range(heads):
             g = pk * heads + h
             x = jnp.dot(kg_ref[g, rows, :].astype(BF), qt_ref[:, g * HD:(g + 1) * HD], preferred_element_type=F32)
-            y = jnp.concatenate([(x * cg_ref[g, rows, :]).astype(BF), (x * sg_ref[g, rows, :]).astype(BF)], 1)
+            ys.append(jnp.concatenate([(x * cg_ref[g, rows, :]).astype(BF), (x * sg_ref[g, rows, :]).astype(BF)], 1))
+        r = product(pk, jnp.concatenate(ys, 0))
+        s = jnp.full((n, LANES), DEAD, F32)
+        here = lax.broadcasted_iota(jnp.int32, (n, LANES), 0) + at
+        for h in range(heads):
             first, last = limits[h]
-            here = token + at
-            s = jnp.where((here >= first) & (here < last), product(pk, y), s)
+            s = jnp.where((here >= first) & (here < last), r[h * n:(h + 1) * n], s)
         return s
 
     def known_scores(pk):
@@ -392,8 +404,9 @@
         new = token - OMOST * SPAN
         is_live = (token < o_live) | (first_shard & (new >= 0) & (new <= col_step))
         is_live = is_live & (new < steps) & (col_row < steps * per_device)
+        r = product(pk, kx_ref[pk * heads:(pk + 1) * heads].reshape(heads * LANES, 2 * HD))
         for h in range(heads):
-            s = jnp.where(is_live & (col_head == h), product(pk, kx_ref[pk * heads + h]), s)
+            s = jnp.where(is_live & (col_head == h), r[h * LANES:(h + 1) * LANES], s)
         return s
 
     limits = [[bounds(pk, h) for h in range(heads)] for pk in range(packs)]
@@ -407,17 +420,15 @@
     for pk in range(packs):
         s = known_scores(pk)
         sc_ref[pk, :LANES, :] = s
-        top = s
-        for at in range(0, main, LANES):
-            s = slot_scores(pk, at, limits[pk])
-            sc_ref[pk, LANES + at:2 * LANES + at, :] = s
-            top = jnp.maximum(top, s)
-        tops.append(jnp.max(top, axis=0, keepdims=True))
+        top = jnp.max(s, axis=0, keepdims=True)
+        s = slot_scores(pk, 0, main, limits[pk])
+        sc_ref[pk, LANES:LANES + main, :] = s
+        tops.append(jnp.maximum(top, jnp.max(s, axis=0, keepdims=True)))
     if extra > 0:
         for pk in range(packs):
             def more(k, top, pk=pk):
                 at = pl.multiple_of(main + k * LANES, LANES)
-                s = slot_scores(pk, at, limits[pk])
+                s = slot_scores(pk, at, LANES, limits[pk])
                 sc_ref[pk, pl.ds(pl.multiple_of(LANES + at, LANES), LANES), :] = s
                 return jnp.maximum(top, jnp.max(s, axis=0, keepdims=True))
 
@@ -474,6 +485,17 @@
         out_ref[d, used:used + 1, :] = tops[pk]
         out_ref[d, used + 1:used + 2, :] = sums[pk]
     store.wait()
+
+
+def turn_tables(ca_ref, sa_ref, cb_ref, sb_ref, cc_ref, ss_ref):
+    blk = cb_ref.shape[0]
+    cb = cb_ref[...]
+    sb = sb_ref[...]
+    for a in range(cc_ref.shape[0] // blk):
+        ca = ca_ref[a:a + 1, :]
+        sa = sa_ref[a:a + 1, :]
+        cc_ref[a * blk:(a + 1) * blk, :] = ca * cb - sa * sb
+        ss_ref[a * blk:(a + 1) * blk, :] = sa * cb + ca * sb
 
 
 def basis(z_ref, a_ref, qt_ref):
@@ -548,6 +570,8 @@
             pltpu.VMEM((KVH, tok_all, HD), F32),
             pltpu.VMEM((KVH, tok_all, HD), F32),
             pltpu.VMEM((w.shape[0], LANES + tok_all, LANES), F32),
+            pltpu.VMEM((seq_len, HD), F32),
+            pltpu.VMEM((seq_len, HD), F32),
             pltpu.SemaphoreType.DMA,
             pltpu.SemaphoreType.DMA,
         ],
@@ -624,6 +648,12 @@
     late = (length + jnp.arange(steps, dtype=jnp.int32)).astype(F32)[:, None] * inverse_freq
     turns = (jnp.cos(coarse), jnp.sin(coarse), jnp.cos(fine), jnp.sin(fine))
 
+    shard = jnp.arange(devices, dtype=jnp.int32)
+    place = jnp.stack([
+        jnp.sum(jnp.where(shard < myself, shard_counts, 0), axis=2),
+        jnp.sum(jnp.where(shard == myself, shard_counts, 0), axis=2),
+    ]).reshape(2 * n_lists)
+
     tie_shape = jax.ShapeDtypeStruct((1, LANES), F32)
 
     def find_slots(after):
@@ -632,12 +662,12 @@
             in_specs=[smem()] * 4 + [anywhere()],
             out_specs=[smem()] * 2 + [vmem()],
             out_shape=[
-                jax.ShapeDtypeStruct((KVH, slots_all + 2 * PART), jnp.int32),
+                jax.ShapeDtypeStruct((KVH, slots_all + 4 * PART), jnp.int32),
                 jax.ShapeDtypeStruct((KVH * (steps + 1) + 2 + OMOST,), jnp.int32),
                 tie_shape,
             ],
             name="find_slots",
-        )(me, chosen.reshape(n_lists, -1), shard_counts.reshape(n_lists, -1), outliers, after)
+        )(me, chosen.reshape(n_lists, -1), place, outliers, after)
 
     def known(live, after):
         return pl.pallas_call(

time: 77.7 us -> 65.5 us (0.84)
  Pallas kernels: 44.9 us -> 36.1 us
  blocking collectives: 18.3 us -> 12.8 us
  starting transfers between devices: 6.51 us -> 8.86 us
  waiting for transfers between devices: 4.67 us -> 2.87 us
    pallas_call x1, Pallas kernels: 21.7 us -> 14.5 us  [attend_call(): pl.pallas_call(functools.partial(attend_kernel, per_device=per_device, st...]
    all_to_all x1, blocking collectives: 18.3 us -> 12.8 us  [on_device(): parts = lax.all_to_all(parts, 'seq', 0, 0, tiled=True)]
    ppermute x5, starting transfers between devices: 6.51 us -> 8.86 us  [swap(): return lax.ppermute(x, 'seq', moves)]
    ppermute x5, waiting for transfers between devices: 4.67 us -> 2.87 us  [swap(): return lax.ppermute(x, 'seq', moves)]
    pallas_call x1, Pallas kernels: 6.19 us -> 5.09 us  [find_slots(): pl.pallas_call(functools.partial(slots_kernel, most=most, spans=seq_len /...]
  transfers between devices with their start and end apart: 5 -> 5, of which waited for: 3 -> 3; matrix products, arithmetic and copies ran while one was open for 1% -> 2% of each run, Pallas kernels for 19% -> 21%
where the time goes in v1:
time: 65.5 us; the launch traced here: 64.4 us
  Pallas kernels  36.1 us (55%)
  blocking collectives  12.8 us (20%)
  starting transfers between devices  8.86 us (14%)
  waiting for transfers between devices  2.87 us (4%)
  other arithmetic  1.64 us (3%)
  local copies, waits for them, and re-layouts  1.3 us (2%)
  between operations  0.85 us (1%)
    pallas_call x1, Pallas kernels, attend_call(): pl.pallas_call(functools.partial(attend_kernel, per_device=per_device, st...  14.5 us
    all_to_all x1, blocking collectives, on_device(): parts = lax.all_to_all(parts, 'seq', 0, 0, tiled=True)  12.8 us
    ppermute x5, starting transfers between devices, swap(): return lax.ppermute(x, 'seq', moves)  8.86 us
    pallas_call x1, Pallas kernels, sketch_share(): pl.pallas_call(functools.partial(sketch_kernel, scale=1.0 / length, chunk...  6.62 us
    pallas_call x1, Pallas kernels, slot_values(): pl.pallas_call(functools.partial(values_kernel, main=main), in_specs=[sme...  6.52 us
    pallas_call x1, Pallas kernels, find_slots(): pl.pallas_call(functools.partial(slots_kernel, most=most, spans=seq_len /...  5.09 us
    ppermute x5, waiting for transfers between devices, swap(): return lax.ppermute(x, 'seq', moves)  2.87 us
    pallas_call x1, Pallas kernels, known(): pl.pallas_call(functools.partial(known_kernel, per_device=per_device, rp=...  1.78 us
  transfers between devices with their start and end apart: 5, of which 3 were waited for; matrix products, arithmetic and copies ran while one was open for 2% of the time, Pallas kernels for 21%

profile of v1, /device:TPU:0, one launch (start us, length us, event | category | flops | bytes accessed | tf_op | source)
XLA Modules:
  0.0 64.4 jit_solution(15449378239394987879)
XLA Ops:
  0.6 0.0 copy-start.7
  0.6 0.0 copy-start.2
  0.7 0.0 copy-start
  0.7 0.0 copy-start.3
  0.7 6.6 %sketch_share.1 = (f32[80,1024]{1,0:T(8,128)S(1)}, f32[80,1024]{1,0:T(8,128)S(1)}) custom-call(s32[1]{0:T(128)} %bitcast.me_ref.core_ref, f32[160,1024]{1,0:T(8,128)} %bitcast.15, bf16[4096,1024]{1,0:T(8,128)(2,1)} %keys_hbm.5), custom_call_target="tpu_custom_call" | custom-call | tf_op jit(solution)/shard_map/sketch_share/pallas_call | solution.py:119
  7.3 0.5 collective-permute-start
  7.9 0.0 copy-done.7
  7.9 0.2 select_reduce_fusion.1
  8.1 0.1 pad_maximum_fusion
  8.1 0.3 multiply_sine_fusion
  8.4 0.6 collective-permute-done
  9.1 0.0 copy-start.6
  9.1 3.0 %collective-permute-start.1 = (bf16[80,1024]{1,0:T(8,128)(2,1)S(1)}, bf16[80,1024]{1,0:T(8,128)(2,1)S(1)}, u32[]{:S(2)}, u32[]{:S(2)}) collective-permute-start(bf16[80,1024]{1,0:T(8,128)(2,1)S(1)} %get-tuple-element.28.after_ref), channel_id=1, source_target_pairs={{0,2},{1,5},{2,0},{3,7},{4,6},{5,1},{6,4},{7,3},{8,10},{9,13},{10,... | collective-permute-start | bytes 491528 | tf_op jit(solution)/shard_map/ppermute | solution.py:608
  12.1 0.6 reshape.27.place_ref
  12.7 0.0 copy-done.6
  12.7 5.1 %find_slots.1 = (s32[8,176]{1,0:T(8,128)}, s32[38]{0:T(128)}, f32[1,128]{1,0:T(1,128)}) custom-call(s32[1]{0:T(128)} %bitcast.me_ref.core_ref, s32[24,256]{1,0:T(8,128)} %bitcast.16, s32[48]{0:T(128)} %reshape.27.place_ref, s32[32]{0:T(128)} %outl_ref.1, bf16[80,1024]{1,0:T(8,128)(2,1)} %copy-done.6), custom_call_target="tpu_custom_call" | custom-call | tf_op jit(solution)/shard_map/find_slots/pallas_call | solution.py:660
  17.8 0.0 copy-start.8
  17.8 0.0 copy-start.1
  17.8 0.0 copy-start.5
  17.8 0.0 collective-permute-done.1
  17.8 0.6 fusion.after_ref
  18.5 1.9 %collective-permute-start.2 = (bf16[80,1024]{1,0:T(8,128)(2,1)S(1)}, bf16[80,1024]{1,0:T(8,128)(2,1)S(1)}, u32[]{:S(2)}, u32[]{:S(2)}) collective-permute-start(bf16[80,1024]{1,0:T(8,128)(2,1)S(1)} %fusion.after_ref), channel_id=1, source_target_pairs={{0,4},{1,3},{2,6},{3,1},{4,0},{5,7},{6,2},{7,5},{8,12},{9,11},{10,... | collective-permute-start | bytes 491528 | tf_op jit(solution)/shard_map/ppermute | solution.py:608
  20.4 0.1 multiply_sine_fusion.2
  20.5 0.0 copy-done.2
  20.5 0.0 copy-done
  20.5 0.0 copy-start.4
  20.5 0.7 %copy-done.4 = s32[38]{0:T(128)S(1)} copy-done((s32[38]{0:T(128)S(1)}, s32[38]{0:T(128)}, u32[]{:S(2)}) %copy-start.4) | copy-done | bytes 176
  21.2 1.8 %known_keys.1 = (bf16[8,128,256]{2,1,0:T(8,128)(2,1)S(1)}, bf16[2,512,128]{2,1,0:T(8,128)(2,1)S(1)}, f32[1,128]{1,0:T(1,128)S(1)}) custom-call(s32[38]{0:T(128)S(1)} %copy-done.4, bf16[3,8192]{1,0:T(4,128)(2,1)S(1)} %copy-done, bf16[3,1024]{1,0:T(4,128)(2,1)S(1)} %copy-done.2, f32[64,128]{1,0:T(8,128)S(1)} %get-tuple-element.36.ca_ref, ...), custom_call_target="tpu_custom_call" | custom-call | tf_op jit(solution)/shard_map/known_keys/pallas_call | solution.py:673
  23.0 0.9 %collective-permute-done.2 = bf16[80,1024]{1,0:T(8,128)(2,1)S(1)} collective-permute-done((bf16[80,1024]{1,0:T(8,128)(2,1)S(1)}, bf16[80,1024]{1,0:T(8,128)(2,1)S(1)}, u32[]{:S(2)}, u32[]{:S(2)}) %collective-permute-start.2) | collective-permute-done | bytes 163872 | tf_op jit(solution)/shard_map/ppermute | solution.py:608
  23.9 0.0 copy-done.8
  23.9 0.1 fusion.1.after_ref
  24.0 3.4 %collective-permute-start.3 = (bf16[80,1024]{1,0:T(8,128)(2,1)S(1)}, bf16[80,1024]{1,0:T(8,128)(2,1)S(1)}, u32[]{:S(2)}, u32[]{:S(2)}) collective-permute-start(bf16[80,1024]{1,0:T(8,128)(2,1)S(1)} %fusion.1.after_ref), channel_id=1, source_target_pairs={{0,8},{1,9},{2,10},{3,11},{4,12},{5,13},{6,14},{7,15},{8,0},{9,1},... | collective-permute-start | bytes 491528 | tf_op jit(solution)/shard_map/ppermute | solution.py:608
  27.4 0.0 copy-done.3
  27.4 0.0 copy-done.1
  27.4 0.0 copy-done.5
  27.4 6.5 %slot_values.1 = (bf16[8,1280,128]{2,1,0:T(8,128)(2,1)S(1)}, f32[1,128]{1,0:T(1,128)S(1)}) custom-call(s32[8,176]{1,0:T(8,128)S(1)} %copy-done.1, s32[38]{0:T(128)S(1)} %copy-done.5, bf16[3,1024]{1,0:T(4,128)(2,1)S(1)} %copy-done.3, bf16[4096,1024]{1,0:T(8,128)(2,1)} %values_hbm.1, bf16[80,1024]{1,0:T(8,128)(2,1)S(1)} %fusion.1.after_ref), custom_call_target="tpu_custom_call" | custom-call | tf_op jit(solution)/shard_map/slot_values/pallas_call | solution.py:693
  33.9 0.0 collective-permute-done.3
  33.9 0.1 add_convert_fusion.zmine_ref
  34.1 0.1 collective-permute-start.4
  34.1 1.4 %collective-permute-done.4.zother_ref = bf16[80,1024]{1,0:T(8,128)(2,1)S(1)} collective-permute-done((bf16[80,1024]{1,0:T(8,128)(2,1)S(1)}, bf16[80,1024]{1,0:T(8,128)(2,1)S(1)}, u32[]{:S(2)}, u32[]{:S(2)}) %collective-permute-start.4) | collective-permute-done | bytes 163872 | tf_op jit(solution)/shard_map/ppermute | solution.py:608
  35.5 14.5 %attend.1 = (f32[160,4096]{1,0:T(8,128)}, f32[16,16,128]{2,1,0:T(8,128)S(1)}) custom-call(s32[1]{0:T(128)} %bitcast.me_ref.core_ref, s32[8,176]{1,0:T(8,128)S(1)} %copy-done.1, s32[38]{0:T(128)S(1)} %copy-done.5, bf16[80,1024]{1,0:T(8,128)(2,1)S(1)} %add_convert_fusion.zmine_ref, bf16[80,1024]{1,0:T(8,128)(2,1)S(1)} %collective-permute-done.4.zother_ref, ...), custom_call_target="tpu_custom_call" | custom-call | tf_op jit(solution)/shard_map/attend/pallas_call | solution.py:554
  50.0 12.8 %all_to_all.5.parts_ref = f32[16,16,128]{2,1,0:T(8,128)} all-to-all(f32[16,16,128]{2,1,0:T(8,128)S(1)} %get-tuple-element.24), channel_id=1, replica_groups=mesh['groups'=2,'seq'=16] {'seq'}, dimensions={0} | all-to-all | bytes 262144 | tf_op jit(solution)/shard_map/all_to_all | solution.py:731
  62.8 1.7 %merge.1 = bf16[3,512]{1,0:T(4,128)(2,1)} custom-call(s32[1]{0:T(128)} %bitcast.me_ref.core_ref, f32[16,16,128]{2,1,0:T(8,128)} %all_to_all.5.parts_ref), custom_call_target="tpu_custom_call" | custom-call | tf_op jit(solution)/shard_map/merge/pallas_call | solution.py:732
  (7 shorter events, 0.1 us)
Async XLA Ops:
  0.6 7.2 %copy-start.7 = (s32[3,8,16]{2,1,0:T(8,128)S(1)}, s32[3,8,16]{2,1,0:T(8,128)}, u32[]{:S(2)}) copy-start(s32[3,8,16]{2,1,0:T(8,128)} %param.16) | copy-start | bytes 4612
  0.6 19.9 %copy-start.2 = (bf16[3,1024]{1,0:T(4,128)(2,1)S(1)}, bf16[3,1024]{1,0:T(4,128)(2,1)}, u32[]{:S(2)}) copy-start(bf16[3,1024]{1,0:T(4,128)(2,1)} %fk_ref.1) | copy-start | bytes 18436
  0.7 19.9 %copy-start = (bf16[3,8192]{1,0:T(4,128)(2,1)S(1)}, bf16[3,8192]{1,0:T(4,128)(2,1)}, u32[]{:S(2)}) copy-start(bf16[3,8192]{1,0:T(4,128)(2,1)} %q_ref.1) | copy-start | bytes 147460
  0.7 26.7 %copy-start.3 = (bf16[3,1024]{1,0:T(4,128)(2,1)S(1)}, bf16[3,1024]{1,0:T(4,128)(2,1)}, u32[]{:S(2)}) copy-start(bf16[3,1024]{1,0:T(4,128)(2,1)} %fv_ref.1) | copy-start | bytes 18436
  7.3 1.8 %collective-permute-start = (f32[80,1024]{1,0:T(8,128)S(1)}, f32[80,1024]{1,0:T(8,128)S(1)}, u32[]{:S(2)}, u32[]{:S(2)}) collective-permute-start(f32[80,1024]{1,0:T(8,128)S(1)} %get-tuple-element.15), channel_id=1, source_target_pairs={{0,1},{1,0},{2,3},{3,2},{4,5},{5,4},{6,7},{7,6},{8,9},{9,8},{10,11... | collective-permute-start | bytes 983048 | tf_op jit(solution)/shard_map/ppermute | solution.py:608
  9.1 3.6 %copy-start.6 = (bf16[80,1024]{1,0:T(8,128)(2,1)}, bf16[80,1024]{1,0:T(8,128)(2,1)S(1)}, u32[]{:S(2)}) copy-start(bf16[80,1024]{1,0:T(8,128)(2,1)S(1)} %get-tuple-element.28.after_ref) | copy-start | bytes 491524
  9.1 8.7 %collective-permute-start.1 = (bf16[80,1024]{1,0:T(8,128)(2,1)S(1)}, bf16[80,1024]{1,0:T(8,128)(2,1)S(1)}, u32[]{:S(2)}, u32[]{:S(2)}) collective-permute-start(bf16[80,1024]{1,0:T(8,128)(2,1)S(1)} %get-tuple-element.28.after_ref), channel_id=1, source_target_pairs={{0,2},{1,5},{2,0},{3,7},{4,6},{5,1},{6,4},{7,3},{8,10},{9,13},{10,... | collective-permute-start | bytes 491528 | tf_op jit(solution)/shard_map/ppermute | solution.py:608
  17.8 6.1 %copy-start.8 = (f32[1,128]{1,0:T(1,128)S(1)}, f32[1,128]{1,0:T(1,128)}, u32[]{:S(2)}) copy-start(f32[1,128]{1,0:T(1,128)} %get-tuple-element.18) | copy-start | bytes 1540
  17.8 9.6 %copy-start.1 = (s32[8,176]{1,0:T(8,128)S(1)}, s32[8,176]{1,0:T(8,128)}, u32[]{:S(2)}) copy-start(s32[8,176]{1,0:T(8,128)} %get-tuple-element.16.slots_ref) | copy-start | bytes 16900
  17.8 9.6 %copy-start.5 = (s32[38]{0:T(128)S(1)}, s32[38]{0:T(128)}, u32[]{:S(2)}) copy-start(s32[38]{0:T(128)} %get-tuple-element.17.live_ref) | copy-start | bytes 460
  18.5 5.4 %collective-permute-start.2 = (bf16[80,1024]{1,0:T(8,128)(2,1)S(1)}, bf16[80,1024]{1,0:T(8,128)(2,1)S(1)}, u32[]{:S(2)}, u32[]{:S(2)}) collective-permute-start(bf16[80,1024]{1,0:T(8,128)(2,1)S(1)} %fusion.after_ref), channel_id=1, source_target_pairs={{0,4},{1,3},{2,6},{3,1},{4,0},{5,7},{6,2},{7,5},{8,12},{9,11},{10,... | collective-permute-start | bytes 491528 | tf_op jit(solution)/shard_map/ppermute | solution.py:608
  20.5 0.7 %copy-start.4 = (s32[38]{0:T(128)S(1)}, s32[38]{0:T(128)}, u32[]{:S(2)}) copy-start(s32[38]{0:T(128)} %get-tuple-element.17.live_ref) | copy-start | bytes 460
  24.0 9.9 %collective-permute-start.3 = (bf16[80,1024]{1,0:T(8,128)(2,1)S(1)}, bf16[80,1024]{1,0:T(8,128)(2,1)S(1)}, u32[]{:S(2)}, u32[]{:S(2)}) collective-permute-start(bf16[80,1024]{1,0:T(8,128)(2,1)S(1)} %fusion.1.after_ref), channel_id=1, source_target_pairs={{0,8},{1,9},{2,10},{3,11},{4,12},{5,13},{6,14},{7,15},{8,0},{9,1},... | collective-permute-start | bytes 491528 | tf_op jit(solution)/shard_map/ppermute | solution.py:608
  34.1 1.5 %collective-permute-start.4 = (bf16[80,1024]{1,0:T(8,128)(2,1)S(1)}, bf16[80,1024]{1,0:T(8,128)(2,1)S(1)}, u32[]{:S(2)}, u32[]{:S(2)}) collective-permute-start(bf16[80,1024]{1,0:T(8,128)(2,1)S(1)} %add_convert_fusion.zmine_ref), channel_id=1, source_target_pairs={{0,1},{1,0},{2,3},{3,2},{4,5},{5,4},{6,7},{7,6},{8,9},{9,8},{10,11... | collective-permute-start | bytes 491528 | tf_op jit(solution)/shard_map/ppermute | solution.py:608

commit v2 on v1

--- a/solution.py
+++ b/solution.py
@@ -18,7 +18,8 @@
 LANES = 128
 MAIN = 640
 PART = 8
-STRAIGHT = 6
+STRAIGHT = 2
+EARLY = 3
 AHEAD = 3
 NT = (((1,), (1,)), ((), ()))
 TN = (((0,), (0,)), ((), ()))
@@ -133,61 +134,61 @@
     )(me, in_hbm(sketch_t), in_hbm(cache_keys))
 
 
-def slots_kernel(me_ref, chosen_ref, place_ref, outl_ref, after_ref, slots_ref, live_ref, tie_ref, *, most, spans, steps):
-    me = me_ref[0]
-    base = me * spans
-    tie_ref[...] = jnp.zeros_like(tie_ref)
-
-    n_out = outl_ref.shape[0]
-    o_first = jnp.int32(0)
-    o_here = jnp.int32(0)
-    for i in range(n_out):
-        s = outl_ref[i]
-        o_first = o_first + (s < base).astype(jnp.int32)
-        o_here = o_here + ((s >= base) & (s < base + spans)).astype(jnp.int32)
-    n_at = KVH * (steps + 1)
-    live_ref[n_at] = jnp.minimum(o_here, OMOST)
-    live_ref[n_at + 1] = me
-    for j in range(OMOST):
-        live_ref[n_at + 2 + j] = jnp.clip(outl_ref[jnp.minimum(o_first + j, n_out - 1)] - base, 0, spans - 1)
-
-    sel = chosen_ref.shape[1]
-    n_lists = chosen_ref.shape[0]
-    for g in range(KVH):
-        at = jnp.int32(0)
+class Lists:
+    def __init__(self, me_ref, chosen_ref, begin_ref, count_ref, outl_ref, spans, most=None):
+        self.chosen, self.begin, self.counts, self.outl = chosen_ref, begin_ref, count_ref, outl_ref
+        self.spans, self.most = spans, most
+        self.base = me_ref[0] * spans
+
+    def span(self, t, g, slot):
+        i = t * KVH + g
+        last = self.chosen.shape[1] - 1
+        picked = self.chosen[i, jnp.minimum(self.begin[t, g] + slot, last)]
+        return jnp.clip(picked - self.base, 0, self.spans - 1)
+
+    def count(self, t, g):
+        return jnp.minimum(self.counts[t, g], self.most)
+
+    def starts(self, g, steps):
+        at = [jnp.int32(0)]
         for t in range(steps):
-            i = t * KVH + g
-            start = place_ref[i]
-            count = jnp.minimum(place_ref[n_lists + i], most)
-            live_ref[g * (steps + 1) + t] = at
-
-            def put(k, _, i=i, start=start, at=at, g=g):
-                found = []
-                for j in range(PART):
-                    picked = chosen_ref[i, jnp.minimum(start + (k * PART + j), sel - 1)]
-                    found.append(jnp.clip(picked - base, 0, spans - 1))
-                for j in range(PART):
-                    slots_ref[g, at + (k * PART + j)] = found[j]
+            at.append(at[-1] + self.count(t, g))
+        return at
+
+    def outliers(self):
+        n = self.outl.shape[0]
+        first = jnp.int32(0)
+        here = jnp.int32(0)
+        for i in range(n):
+            s = self.outl[i]
+            first = first + (s < self.base).astype(jnp.int32)
+            here = here + ((s >= self.base) & (s < self.base + self.spans)).astype(jnp.int32)
+        found = [
+            jnp.clip(self.outl[jnp.minimum(first + j, n - 1)] - self.base, 0, self.spans - 1) for j in range(OMOST)
+        ]
+        return jnp.minimum(here, OMOST), found
+
+    def each_part(self, g, steps, copy):
+        at = self.starts(g, steps)
+        for t in range(steps):
+            def part(k, _, t=t):
+                copy([self.span(t, g, k * PART + j) for j in range(PART)], at[t] + k * PART)
                 return 0
 
-            put(0, 0)
-            put(1, 0)
-            lax.fori_loop(2, (count + PART - 1) // PART, put, 0)
-            at = at + count
-        live_ref[g * (steps + 1) + steps] = at
-        for j in range(PART):
-            slots_ref[g, at + j] = 0
+            for k in range(STRAIGHT):
+                part(k, 0)
+            lax.fori_loop(STRAIGHT, (self.count(t, g) + PART - 1) // PART, part, 0)
+        return at
 
 
 def known_kernel(
-    live_ref, q_ref, fk_ref, ca_ref, sa_ref, cb_ref, sb_ref, cq_ref, sq_ref, keys_hbm, after_ref,
+    me_ref, outl_ref, q_ref, fk_ref, ca_ref, sa_ref, cb_ref, sb_ref, cq_ref, sq_ref, keys_hbm, after_ref,
     kx_ref, w_ref, tie_ref,
-    okeys_ref, xtmp_ref, qtmp_ref, osem, *, per_device, rp
+    okeys_ref, xtmp_ref, qtmp_ref, osem, *, per_device, rp, spans
 ):
     steps = q_ref.shape[0]
     tie_ref[...] = jnp.zeros_like(tie_ref)
-    n_at = KVH * (steps + 1)
-    o_span = [live_ref[n_at + 2 + j] for j in range(OMOST)]
+    _, o_span = Lists(me_ref, None, None, None, outl_ref, spans).outliers()
     o_copies = [
         pltpu.make_async_copy(
             keys_hbm.at[pl.ds(pl.multiple_of(o_span[j] // 2 * 16, 16), 16)], okeys_ref.at[j], osem.at[j]
@@ -250,59 +251,56 @@
 
 
 def values_kernel(
-    slots_ref, live_ref, fv_ref, values_hbm, after_ref, vg_ref, tie_ref, values_ref, vtmp_ref, sem, *, main
+    me_ref, chosen_ref, begin_ref, count_ref, outl_ref, fv_ref, values_hbm, after_ref, vg_ref, tie_ref,
+    values_ref, vtmp_ref, sem, *, main, g0, most
 ):
     steps = fv_ref.shape[0]
     rows_all = vtmp_ref.shape[0]
-    spans = values_ref.shape[1] // SPAN
+    n = vg_ref.shape[0]
     copies = [
-        pltpu.make_async_copy(values_hbm.at[:, pl.ds(g * HD, HD)], values_ref.at[g], sem.at[g]) for g in range(KVH)
+        pltpu.make_async_copy(values_hbm.at[:, pl.ds((g0 + i) * HD, HD)], values_ref.at[i], sem.at[i]) for i in range(n)
     ]
     for c in copies[:AHEAD]:
         c.start()
     tie_ref[...] = jnp.zeros_like(tie_ref)
     vtmp_ref[...] = jnp.zeros_like(vtmp_ref)
-    n_at = KVH * (steps + 1)
-
-    for g in range(KVH):
-        def rows_of(span, g=g):
-            wide = values_ref[g, pl.ds(pl.multiple_of(span // 2 * 16, 16), 16), :].astype(F32)
+    lists = Lists(me_ref, chosen_ref, begin_ref, count_ref, outl_ref, values_ref.shape[1] // SPAN, most)
+    _, o_span = lists.outliers()
+
+    for i in range(n):
+        g = g0 + i
+
+        def rows_of(span, i=i):
+            wide = values_ref[i, pl.ds(pl.multiple_of(span // 2 * 16, 16), 16), :].astype(F32)
             return jnp.where(span % 2 == 0, wide[:8], wide[8:])
 
-        copies[g].wait()
-        if g + AHEAD < KVH:
-            copies[g + AHEAD].start()
+        def put(spans, slot, rows_of=rows_of):
+            dst = pl.ds(pl.multiple_of(LANES + slot * SPAN, SPAN), PART * SPAN)
+            vtmp_ref[dst, :] = jnp.concatenate([rows_of(span) for span in spans], 0)
+
+        copies[i].wait()
+        if i + AHEAD < n:
+            copies[i + AHEAD].start()
         for j in range(OMOST):
-            vtmp_ref[j * SPAN:(j + 1) * SPAN, :] = rows_of(live_ref[n_at + 2 + j])
+            vtmp_ref[j * SPAN:(j + 1) * SPAN, :] = rows_of(o_span[j])
         vtmp_ref[OMOST * SPAN:OMOST * SPAN + steps, :] = fv_ref[:, g * HD:(g + 1) * HD].astype(F32)
-        count = live_ref[g * (steps + 1) + steps]
-
-        def put(k, _, g=g, rows_of=rows_of):
-            rows = [rows_of(jnp.clip(slots_ref[g, k * PART + j], 0, spans - 1)) for j in range(PART)]
-            dst = pl.ds(pl.multiple_of(LANES + k * (PART * SPAN), PART * SPAN), PART * SPAN)
-            vtmp_ref[dst, :] = jnp.concatenate(rows, 0)
-            return 0
-
-        straight = min(STRAIGHT, (rows_all - LANES) // (PART * SPAN))
-        for k in range(straight):
-            put(k, 0)
-        lax.fori_loop(straight, (count + PART - 1) // PART, put, 0)
-        vg_ref[g, :LANES + main, :] = vtmp_ref[:LANES + main, :].astype(BF)
+        total = lists.each_part(g, steps, put)[steps]
+        vg_ref[i, :LANES + main, :] = vtmp_ref[:LANES + main, :].astype(BF)
         if LANES + main < rows_all:
-            def more(k, _, g=g):
+            def more(k, _, i=i):
                 at = pl.ds(pl.multiple_of(LANES + main + k * LANES, LANES), LANES)
-                vg_ref[g, at, :] = vtmp_ref[at, :].astype(BF)
+                vg_ref[i, at, :] = vtmp_ref[at, :].astype(BF)
                 return 0
 
-            lax.fori_loop(0, (jnp.maximum(count * SPAN - main, 0) + LANES - 1) // LANES, more, 0)
+            lax.fori_loop(0, (jnp.maximum(total * SPAN - main, 0) + LANES - 1) // LANES, more, 0)
 
 
 def attend_kernel(
-    core_ref, slots_ref, live_ref, zmine_ref, zother_ref, kx_ref, w_ref, vg_ref, ca_ref, sa_ref, cb_ref, sb_ref,
-    keys_hbm,
+    me_ref, chosen_ref, begin_ref, count_ref, outl_ref, zmine_ref, zother_ref, kx_ref, w_ref, vga_ref, vgb_ref,
+    ca_ref, sa_ref, cb_ref, sb_ref, keys_hbm,
     kft_hbm, out_ref,
-    keys_ref, z_ref, a_ref, qt_ref, kf_ref, kft_ref, kg_ref, cg_ref, sg_ref, sc_ref, cc_ref, ss_ref,
-    sem, out_sem, *, per_device, steps, main, stop=9
+    keys_ref, z_ref, a_ref, qt_ref, kf_ref, kft_ref, kg_ref, cg_ref, sg_ref, sc_ref, cc_ref, ss_ref, acc_ref,
+    sem, out_sem, *, per_device, steps, main, most, stop=9
 ):
     rank, width = z_ref.shape
     half = rank // 2
@@ -310,7 +308,7 @@
     load = pltpu.make_async_copy(keys_hbm, keys_ref, sem)
     load.start()
 
-    core = core_ref[0] % 2
+    core = me_ref[0] % 2
     z_ref[pl.ds(pl.multiple_of(core * half, 16), half), :] = zmine_ref[...]
     z_ref[pl.ds(pl.multiple_of((1 - core) * half, 16), half), :] = zother_ref[...]
     turn_tables(ca_ref, sa_ref, cb_ref, sb_ref, cc_ref, ss_ref)
@@ -332,25 +330,25 @@
         store.wait()
         return
 
-    totals = [live_ref[g * (steps + 1) + steps] for g in range(KVH)]
-    spans = seq_len // SPAN
-    parts_all = kg_ref.shape[1] // (PART * SPAN)
-    straight = min(STRAIGHT, parts_all)
+    lists = Lists(me_ref, chosen_ref, begin_ref, count_ref, outl_ref, seq_len // SPAN, most)
+    starts = []
     for g in range(KVH):
-        def gather(k, _, g=g):
+        def gather(spans, slot, g=g):
             got = []
-            for j in range(PART):
-                span = jnp.clip(slots_ref[g, k * PART + j], 0, spans - 1)
+            for span in spans:
                 src = pl.ds(pl.multiple_of(span * SPAN, SPAN), SPAN)
                 got.append((kf_ref[src, :], cc_ref[src, :], ss_ref[src, :]))
+            dst = pl.ds(pl.multiple_of(slot * SPAN, SPAN), PART * SPAN)
             for ref, rows in zip((kg_ref, cg_ref, sg_ref), zip(*got)):
-                dst = pl.ds(pl.multiple_of(k * (PART * SPAN), PART * SPAN), PART * SPAN)
-                ref[g, dst, :] = jnp.concatenate(rows, 0).astype(ref.dtype)
-            return 0
-
-        for k in range(straight):
-            gather(k, 0)
-        lax.fori_loop(straight, (totals[g] + PART - 1) // PART, gather, 0)
+                ref[g, dst, :] = jnp.concatenate(rows, 0)
+
+        starts.append(lists.each_part(g, steps, gather))
+    totals = [at[steps] for at in starts]
+
+    def values(g, rows):
+        n = vga_ref.shape[0]
+        return vga_ref[g, rows, :] if g < n else vgb_ref[g - n, rows, :]
+
     if stop == 3:
         store.wait()
         return
@@ -360,9 +358,8 @@
     qr = dests * rp
     heads = LANES // qr
     packs = w_ref.shape[0]
-    n_at = KVH * (steps + 1)
-    o_live = live_ref[n_at] * SPAN
-    first_shard = live_ref[n_at + 1] == 0
+    o_live = lists.outliers()[0] * SPAN
+    first_shard = me_ref[0] == 0
     column = lax.broadcasted_iota(jnp.int32, (8, LANES), 1)[:1]
     col_head = column // qr
     col_row = column % rp
@@ -372,10 +369,10 @@
         first = jnp.full((1, LANES), 1 << 30, jnp.int32)
         last = jnp.zeros((1, LANES), jnp.int32)
         for t in range(steps):
-            at = (pk * heads + h) * (steps + 1) + t
+            at = starts[pk * heads + h]
             here = (col_head == h) & (col_step == t)
-            first = jnp.where(here, live_ref[at] * SPAN, first)
-            last = jnp.where(here, live_ref[at + 1] * SPAN, last)
+            first = jnp.where(here, at[t] * SPAN, first)
+            last = jnp.where(here, at[t + 1] * SPAN, last)
         return first, last
 
     def product(pk, y):
@@ -413,8 +410,8 @@
     extra = kg_ref.shape[1] - main
     blocks = []
     for pk in range(packs):
-        most = functools.reduce(jnp.maximum, totals[pk * heads:(pk + 1) * heads])
-        blocks.append((jnp.maximum(most * SPAN - main, 0) + LANES - 1) // LANES)
+        longest = functools.reduce(jnp.maximum, totals[pk * heads:(pk + 1) * heads])
+        blocks.append((jnp.maximum(longest * SPAN - main, 0) + LANES - 1) // LANES)
 
     tops = []
     for pk in range(packs):
@@ -459,9 +456,9 @@
         pt = jnp.concatenate(pts, 1)
         for h in range(heads):
             g = pk * heads + h
-            acc = weighted(pt, h, vg_ref[g, :LANES + main, :])
+            acc = weighted(pt, h, values(g, slice(0, LANES + main)))
             for a in range(dests):
-                out_ref[g * dests + a] = acc[a * rp:(a + 1) * rp]
+                acc_ref[g * dests + a] = acc[a * rp:(a + 1) * rp]
     if extra > 0:
         for pk in range(packs):
             def add(k, total, pk=pk):
@@ -473,17 +470,20 @@
 
                     @pl.when(totals[g] * SPAN > main + k * LANES)
                     def _():
-                        acc = weighted(pt, h, vg_ref[g, pl.ds(at, LANES), :])
+                        acc = weighted(pt, h, values(g, pl.ds(at, LANES)))
                         for a in range(dests):
-                            out_ref[g * dests + a] += acc[a * rp:(a + 1) * rp]
+                            acc_ref[g * dests + a] += acc[a * rp:(a + 1) * rp]
 
                 return total + jnp.sum(p, axis=0, keepdims=True)
 
             sums[pk] = lax.fori_loop(0, blocks[pk], add, sums[pk])
     for d in range(n_dest):
         pk = d // (heads * dests)
-        out_ref[d, used:used + 1, :] = tops[pk]
-        out_ref[d, used + 1:used + 2, :] = sums[pk]
+        row = lax.broadcasted_iota(jnp.int32, (rp, LANES), 0)
+        r = acc_ref[d]
+        for k, extra_row in enumerate((*split3(tops[pk]), sums[pk])):
+            r = jnp.where(row == used + k, extra_row, r)
+        out_ref[d] = r.astype(BF)
     store.wait()
 
 
@@ -545,19 +545,19 @@
 
 
 def attend_call(
-    me, slots, live, z, z_other, kx, w, vg, ca, sa, cb, sb, cache_keys,
-    *, steps, per_device, main, rp, n_dest, stop=9
+    me, lists, z, z_other, kx, w, vga, vgb, ca, sa, cb, sb, cache_keys,
+    *, steps, per_device, main, most, rp, n_dest, stop=9
 ):
     seq_len, width = cache_keys.shape
     rank = 2 * z.shape[0]
-    tok_all = vg.shape[1] - LANES
+    tok_all = vga.shape[1] - LANES
     return pl.pallas_call(
-        functools.partial(attend_kernel, per_device=per_device, steps=steps, main=main, stop=stop),
-        in_specs=[smem()] * 3 + [vmem()] * 9 + [hbm()],
+        functools.partial(attend_kernel, per_device=per_device, steps=steps, main=main, most=most, stop=stop),
+        in_specs=[smem()] * 5 + [vmem()] * 10 + [hbm()],
         out_specs=[hbm(), vmem()],
         out_shape=[
             jax.ShapeDtypeStruct((rank, seq_len), F32),
-            jax.ShapeDtypeStruct((n_dest, rp, HD), F32),
+            jax.ShapeDtypeStruct((n_dest, rp, HD), BF),
         ],
         scratch_shapes=[
             pltpu.VMEM((seq_len, width), BF),
@@ -572,32 +572,28 @@
             pltpu.VMEM((w.shape[0], LANES + tok_all, LANES), F32),
             pltpu.VMEM((seq_len, HD), F32),
             pltpu.VMEM((seq_len, HD), F32),
+            pltpu.VMEM((n_dest, rp, HD), F32),
             pltpu.SemaphoreType.DMA,
             pltpu.SemaphoreType.DMA,
         ],
         compiler_params=pltpu.CompilerParams(vmem_limit_bytes=42 << 20),
         name="attend",
-    )(me, slots, live, z, z_other, kx, w, vg, ca, sa, cb, sb, in_hbm(cache_keys))
-
-
-def merge_kernel(me_ref, parts_ref, out_ref, *, steps, per_device):
+    )(me, *lists, z, z_other, kx, w, vga, vgb, ca, sa, cb, sb, in_hbm(cache_keys))
+
+
+def merge_kernel(me_ref, parts_ref, out_ref, top_ref, sum_ref, *, steps, per_device):
     n, rp, _ = parts_ref.shape
     used = steps * per_device
-    shift = me_ref[0] % (LANES // rp) * rp
-    eye = lax.broadcasted_iota(jnp.int32, (rp, LANES), 0) + shift == lax.broadcasted_iota(jnp.int32, (rp, LANES), 1)
-
-    def column(s, r):
-        return jnp.sum(jnp.where(eye, parts_ref[s, r:r + 1, :], 0.0), axis=1, keepdims=True)
-
-    ms = [column(s, used) for s in range(n)]
-    top = functools.reduce(jnp.maximum, ms)
-    total = jnp.zeros((rp, 1), F32)
-    acc = jnp.zeros((rp, HD), F32)
+    parts = parts_ref[...].astype(F32)
+    rows = pl.ds(pl.multiple_of(me_ref[0] % (LANES // rp) * rp, 8), rp)
+    top_ref[...] = (parts[:, used, :] + parts[:, used + 1, :] + parts[:, used + 2, :]).T
+    sum_ref[...] = parts[:, used + 3, :].T
+    tops = top_ref[rows, :]
+    w = jnp.exp(tops - jnp.max(tops, axis=1, keepdims=True))
+    w = w / jnp.sum(w * sum_ref[rows, :], axis=1, keepdims=True)
+    o = jnp.zeros((rp, HD), F32)
     for s in range(n):
-        w = jnp.exp(ms[s] - top)
-        total = total + w * column(s, used + 1)
-        acc = acc + w * parts_ref[s]
-    o = acc / total
+        o = o + w[:, s:s + 1] * parts[s]
     for t in range(steps):
         for i in range(per_device):
             r = t * per_device + i
@@ -628,11 +624,11 @@
     per_device = QH // devices
     n_lists = steps * KVH
     most = 3 * chosen.shape[2] // devices
-    slots_all = round_up(steps * most, LANES // SPAN)
+    slots_all = round_up(max(steps * most, steps * STRAIGHT * PART), LANES // SPAN)
     tok_all = slots_all * SPAN
     main = min(MAIN, tok_all)
     used = steps * per_device
-    rp = round_up(used + 2, 8)
+    rp = round_up(used + 4, 16)
     n_dest = devices
     me = jnp.full((1,), myself, jnp.int32)
 
@@ -649,30 +645,15 @@
     turns = (jnp.cos(coarse), jnp.sin(coarse), jnp.cos(fine), jnp.sin(fine))
 
     shard = jnp.arange(devices, dtype=jnp.int32)
-    place = jnp.stack([
-        jnp.sum(jnp.where(shard < myself, shard_counts, 0), axis=2),
-        jnp.sum(jnp.where(shard == myself, shard_counts, 0), axis=2),
-    ]).reshape(2 * n_lists)
-
+    begin = jnp.sum(jnp.where(shard < myself, shard_counts, 0), axis=2)
+    count = jnp.sum(jnp.where(shard == myself, shard_counts, 0), axis=2)
+    lists = (chosen.reshape(n_lists, -1), begin, count, outliers)
     tie_shape = jax.ShapeDtypeStruct((1, LANES), F32)
 
-    def find_slots(after):
+    def known(after):
         return pl.pallas_call(
-            functools.partial(slots_kernel, most=most, spans=seq_len // SPAN, steps=steps),
-            in_specs=[smem()] * 4 + [anywhere()],
-            out_specs=[smem()] * 2 + [vmem()],
-            out_shape=[
-                jax.ShapeDtypeStruct((KVH, slots_all + 4 * PART), jnp.int32),
-                jax.ShapeDtypeStruct((KVH * (steps + 1) + 2 + OMOST,), jnp.int32),
-                tie_shape,
-            ],
-            name="find_slots",
-        )(me, chosen.reshape(n_lists, -1), place, outliers, after)
-
-    def known(live, after):
-        return pl.pallas_call(
-            functools.partial(known_kernel, per_device=per_device, rp=rp),
-            in_specs=[smem()] + [vmem()] * 8 + [hbm(), anywhere()],
+            functools.partial(known_kernel, per_device=per_device, rp=rp, spans=seq_len // SPAN),
+            in_specs=[smem()] * 2 + [vmem()] * 8 + [hbm(), anywhere()],
             out_specs=[vmem()] * 3,
             out_shape=[
                 jax.ShapeDtypeStruct((KVH, LANES, 2 * HD), BF),
@@ -687,22 +668,22 @@
             ],
             compiler_params=pltpu.CompilerParams(vmem_limit_bytes=8 << 20),
             name="known_keys",
-        )(live, queries, fresh_keys, *turns, jnp.cos(late), jnp.sin(late), in_hbm(cache_keys), after)
-
-    def slot_values(slots, live, after):
+        )(me, outliers, queries, fresh_keys, *turns, jnp.cos(late), jnp.sin(late), in_hbm(cache_keys), after)
+
+    def slot_values(g0, n, after):
         return pl.pallas_call(
-            functools.partial(values_kernel, main=main),
-            in_specs=[smem()] * 2 + [vmem(), hbm(), anywhere()],
+            functools.partial(values_kernel, main=main, g0=g0, most=most),
+            in_specs=[smem()] * 5 + [vmem(), hbm(), anywhere()],
             out_specs=[vmem()] * 2,
-            out_shape=[jax.ShapeDtypeStruct((KVH, LANES + tok_all, HD), BF), tie_shape],
+            out_shape=[jax.ShapeDtypeStruct((n, LANES + tok_all, HD), BF), tie_shape],
             scratch_shapes=[
-                pltpu.VMEM((KVH, seq_len, HD), BF),
+                pltpu.VMEM((n, seq_len, HD), BF),
                 pltpu.VMEM((LANES + tok_all, HD), F32),
-                pltpu.SemaphoreType.DMA((KVH,)),
+                pltpu.SemaphoreType.DMA((n,)),
             ],
             compiler_params=pltpu.CompilerParams(vmem_limit_bytes=16 << 20),
             name="slot_values",
-        )(slots, live, fresh_values, in_hbm(cache_values), after)
+        )(me, *lists, fresh_values, in_hbm(cache_values), after)
 
     z = keep + swap(send, [(i, i ^ 1) for i in range(devices)])
     hops = [1 << k for k in range(1, devices.bit_length() - 1)]
@@ -712,21 +693,21 @@
         going = z.astype(BF)
         came = swap(going, moves).astype(F32)
         if k == 0:
-            slots, live, tie = find_slots(going)
+            kx, w, tie = known(going)
             came = came + tie[0, 0]
         if k == min(1, len(hops) - 1):
-            kx, w, tie = known(live, going)
+            vga, tie = slot_values(0, EARLY, going)
             came = came + tie[0, 0]
         if k == len(hops) - 1:
-            vg, tie = slot_values(slots, live, going)
+            vgb, tie = slot_values(EARLY, KVH - EARLY, going)
             came = came + tie[0, 0]
         z = z + came
     z = z.astype(BF)
     z_other = swap(z, [(i, i ^ 1) for i in range(devices)])
 
     kft, parts = attend_call(
-        me, slots, live, z, z_other, kx, w, vg, *turns, cache_keys,
-        steps=steps, per_device=per_device, main=main, rp=rp, n_dest=n_dest,
+        me, lists, z, z_other, kx, w, vga, vgb, *turns, cache_keys,
+        steps=steps, per_device=per_device, main=main, most=most, rp=rp, n_dest=n_dest,
     )
     parts = lax.all_to_all(parts, "seq", 0, 0, tiled=True)
     attended = pl.pallas_call(
@@ -734,6 +715,7 @@
         in_specs=[smem(), vmem()],
         out_specs=vmem(),
         out_shape=jax.ShapeDtypeStruct((steps, per_device * HD), BF),
+        scratch_shapes=[pltpu.VMEM((LANES, devices), F32)] * 2,
         name="merge",
     )(me, parts)
     return (attended, kft.T)

time: 65.5 us -> 65.9 us (level); the launches traced: 64.4 us -> 66.4 us
  waiting for transfers between devices: 2.87 us -> 5.02 us
  blocking collectives: 12.8 us -> 14.4 us
  local copies, waits for them, and re-layouts: 1.3 us -> 0.03 us
  Pallas kernels: 36.1 us -> 36.8 us
  starting transfers between devices: 8.86 us -> 8.2 us
    ppermute x5, waiting for transfers between devices: 2.87 us -> 5.02 us  [swap(): return lax.ppermute(x, 'seq', moves)]
    all_to_all x1, blocking collectives: 12.8 us -> 14.4 us  [on_device(): parts = lax.all_to_all(parts, 'seq', 0, 0, tiled=True)]
    pallas_call x1, Pallas kernels: 14.5 us -> 15.7 us  [attend_call(): pl.pallas_call(functools.partial(attend_kernel, per_device=per_device, st...]
    pallas_call x2, Pallas kernels: 11.6 us -> 10.8 us  [slot_values(): pl.pallas_call(functools.partial(values_kernel, main=main, g0=g0, most=mo...]
    unnamed x18 -> x12, local copies, waits for them, and re-layouts: 0.7 us -> 0.03 us
    ppermute x5, starting transfers between devices: 8.86 us -> 8.2 us  [swap(): return lax.ppermute(x, 'seq', moves)]
  transfers between devices with their start and end apart: 5 -> 5, of which waited for: 3 -> 4; matrix products, arithmetic and copies ran while one was open for 2% -> 1% of each run, Pallas kernels for 21% -> 19%
where the time goes in v2:
time: 65.9 us; the launch traced here: 66.4 us
  Pallas kernels  36.8 us (56%)
  blocking collectives  14.4 us (22%)
  starting transfers between devices  8.2 us (12%)
  waiting for transfers between devices  5.02 us (8%)
  other arithmetic  1.09 us (2%)
  between operations  0.82 us (1%)
    pallas_call x1, Pallas kernels, attend_call(): pl.pallas_call(functools.partial(attend_kernel, per_device=per_device, st...  15.7 us
    all_to_all x1, blocking collectives, on_device(): parts = lax.all_to_all(parts, 'seq', 0, 0, tiled=True)  14.4 us
    pallas_call x2, Pallas kernels, slot_values(): pl.pallas_call(functools.partial(values_kernel, main=main, g0=g0, most=mo...  10.8 us
    ppermute x5, starting transfers between devices, swap(): return lax.ppermute(x, 'seq', moves)  8.2 us
    pallas_call x1, Pallas kernels, sketch_share(): pl.pallas_call(functools.partial(sketch_kernel, scale=1.0 / length, chunk...  6.63 us
    ppermute x5, waiting for transfers between devices, swap(): return lax.ppermute(x, 'seq', moves)  5.02 us
    pallas_call x1, Pallas kernels, on_device(): pl.pallas_call(functools.partial(merge_kernel, steps=steps, per_device=pe...  1.88 us
    pallas_call x1, Pallas kernels, known(): pl.pallas_call(functools.partial(known_kernel, per_device=per_device, rp=...  1.81 us
  transfers between devices with their start and end apart: 5, of which 4 were waited for; matrix products, arithmetic and copies ran while one was open for 1% of the time, Pallas kernels for 19%

profile of v2, /device:TPU:0, one launch (start us, length us, event | category | flops | bytes accessed | tf_op | source)
XLA Modules:
  0.0 66.4 jit_solution(3648896040901277269)
XLA Ops:
  0.6 0.0 copy-start.4
  0.6 0.0 copy-start.3
  0.7 0.0 copy-start.1
  0.7 0.0 copy-start.5
  0.7 0.0 copy-start
  0.7 0.0 copy-start.2
  0.7 6.6 %sketch_share.1 = (f32[80,1024]{1,0:T(8,128)S(1)}, f32[80,1024]{1,0:T(8,128)S(1)}) custom-call(s32[1]{0:T(128)} %bitcast.me_ref, f32[160,1024]{1,0:T(8,128)} %bitcast.19, bf16[4096,1024]{1,0:T(8,128)(2,1)} %keys_hbm.5), custom_call_target="tpu_custom_call" | custom-call | tf_op jit(solution)/shard_map/sketch_share/pallas_call | solution.py:120
  7.3 0.5 collective-permute-start
  7.9 0.1 pad_maximum_fusion
  8.0 0.3 multiply_sine_fusion
  8.3 0.8 %collective-permute-done = f32[80,1024]{1,0:T(8,128)S(1)} collective-permute-done((f32[80,1024]{1,0:T(8,128)S(1)}, f32[80,1024]{1,0:T(8,128)S(1)}, u32[]{:S(2)}, u32[]{:S(2)}) %collective-permute-start) | collective-permute-done | bytes 327712 | tf_op jit(solution)/shard_map/ppermute | solution.py:604
  9.2 3.0 %collective-permute-start.1 = (bf16[80,1024]{1,0:T(8,128)(2,1)S(1)}, bf16[80,1024]{1,0:T(8,128)(2,1)S(1)}, u32[]{:S(2)}, u32[]{:S(2)}) collective-permute-start(bf16[80,1024]{1,0:T(8,128)(2,1)S(1)} %get-tuple-element.26.after_ref), channel_id=1, source_target_pairs={{0,2},{1,5},{2,0},{3,7},{4,6},{5,1},{6,4},{7,3},{8,10},{9,13},{10,... | collective-permute-start | bytes 491528 | tf_op jit(solution)/shard_map/ppermute | solution.py:604
  12.1 0.1 multiply_sine_fusion.2
  12.2 0.0 copy-done.4
  12.2 0.0 copy-done.3
  12.2 0.0 copy-done.1
  12.3 1.8 %known_keys.1 = (bf16[8,128,256]{2,1,0:T(8,128)(2,1)S(1)}, bf16[2,512,128]{2,1,0:T(8,128)(2,1)S(1)}, f32[1,128]{1,0:T(1,128)S(1)}) custom-call(s32[1]{0:T(128)} %bitcast.me_ref, s32[32]{0:T(128)S(1)} %copy-done.4, bf16[3,8192]{1,0:T(4,128)(2,1)S(1)} %copy-done.1, bf16[3,1024]{1,0:T(4,128)(2,1)S(1)} %copy-done.3, f32[64,128]{1,0:T(8,128)S(1)} %get-tuple-element.34.ca_ref, ...), custom_call_target="tpu_custom_call" | custom-call | tf_op jit(solution)/shard_map/known_keys/pallas_call | solution.py:654
  14.1 1.3 %collective-permute-done.1 = bf16[80,1024]{1,0:T(8,128)(2,1)S(1)} collective-permute-done((bf16[80,1024]{1,0:T(8,128)(2,1)S(1)}, bf16[80,1024]{1,0:T(8,128)(2,1)S(1)}, u32[]{:S(2)}, u32[]{:S(2)}) %collective-permute-start.1) | collective-permute-done | bytes 163872 | tf_op jit(solution)/shard_map/ppermute | solution.py:604
  15.4 0.1 fusion.after_ref
  15.5 2.1 %collective-permute-start.2 = (bf16[80,1024]{1,0:T(8,128)(2,1)S(1)}, bf16[80,1024]{1,0:T(8,128)(2,1)S(1)}, u32[]{:S(2)}, u32[]{:S(2)}) collective-permute-start(bf16[80,1024]{1,0:T(8,128)(2,1)S(1)} %fusion.after_ref), channel_id=1, source_target_pairs={{0,4},{1,3},{2,6},{3,1},{4,0},{5,7},{6,2},{7,5},{8,12},{9,11},{10,... | collective-permute-start | bytes 491528 | tf_op jit(solution)/shard_map/ppermute | solution.py:604
  17.6 0.0 copy-done.5
  17.7 0.2 select_reduce_fusion
  17.8 0.0 copy-done
  17.8 0.0 copy-done.2
  17.9 4.7 %slot_values.2 = (bf16[3,1280,128]{2,1,0:T(8,128)(2,1)S(1)}, f32[1,128]{1,0:T(1,128)S(1)}) custom-call(s32[1]{0:T(128)} %bitcast.me_ref, s32[24,256]{1,0:T(8,128)S(1)} %bitcast.10, s32[3,8]{1,0:T(4,128)S(1)} %get-tuple-element.25.begin_ref, s32[3,8]{1,0:T(4,128)S(1)} %get-tuple-element.24.count_ref, s32[32]{0:T(128)S(1)} %copy-done.4, ...), custom_call_target="tpu_custom_call" | custom-call | tf_op jit(solution)/shard_map/slot_values/pallas_call | solution.py:674
  22.5 0.0 collective-permute-done.2
  22.5 0.1 fusion.1.after_ref
  22.7 2.5 %collective-permute-start.3 = (bf16[80,1024]{1,0:T(8,128)(2,1)S(1)}, bf16[80,1024]{1,0:T(8,128)(2,1)S(1)}, u32[]{:S(2)}, u32[]{:S(2)}) collective-permute-start(bf16[80,1024]{1,0:T(8,128)(2,1)S(1)} %fusion.1.after_ref), channel_id=1, source_target_pairs={{0,8},{1,9},{2,10},{3,11},{4,12},{5,13},{6,14},{7,15},{8,0},{9,1},... | collective-permute-start | bytes 491528 | tf_op jit(solution)/shard_map/ppermute | solution.py:604
  25.2 6.1 %slot_values.3 = (bf16[5,1280,128]{2,1,0:T(8,128)(2,1)S(1)}, f32[1,128]{1,0:T(1,128)S(1)}) custom-call(s32[1]{0:T(128)} %bitcast.me_ref, s32[24,256]{1,0:T(8,128)S(1)} %bitcast.11, s32[3,8]{1,0:T(4,128)S(1)} %get-tuple-element.25.begin_ref, s32[3,8]{1,0:T(4,128)S(1)} %get-tuple-element.24.count_ref, s32[32]{0:T(128)S(1)} %copy-done.4, ...), custom_call_target="tpu_custom_call" | custom-call | tf_op jit(solution)/shard_map/slot_values/pallas_call | solution.py:674
  31.3 1.5 %collective-permute-done.3 = bf16[80,1024]{1,0:T(8,128)(2,1)S(1)} collective-permute-done((bf16[80,1024]{1,0:T(8,128)(2,1)S(1)}, bf16[80,1024]{1,0:T(8,128)(2,1)S(1)}, u32[]{:S(2)}, u32[]{:S(2)}) %collective-permute-start.3) | collective-permute-done | bytes 163872 | tf_op jit(solution)/shard_map/ppermute | solution.py:604
  32.8 0.1 add_convert_fusion.zmine_ref
  32.9 0.1 collective-permute-start.4
  33.0 1.4 %collective-permute-done.4.zother_ref = bf16[80,1024]{1,0:T(8,128)(2,1)S(1)} collective-permute-done((bf16[80,1024]{1,0:T(8,128)(2,1)S(1)}, bf16[80,1024]{1,0:T(8,128)(2,1)S(1)}, u32[]{:S(2)}, u32[]{:S(2)}) %collective-permute-start.4) | collective-permute-done | bytes 163872 | tf_op jit(solution)/shard_map/ppermute | solution.py:604
  34.4 15.7 %attend.1 = (f32[160,4096]{1,0:T(8,128)}, bf16[16,16,128]{2,1,0:T(8,128)(2,1)S(1)}) custom-call(s32[1]{0:T(128)} %bitcast.me_ref, s32[24,256]{1,0:T(8,128)S(1)} %bitcast.12, s32[3,8]{1,0:T(4,128)S(1)} %get-tuple-element.25.begin_ref, s32[3,8]{1,0:T(4,128)S(1)} %get-tuple-element.24.count_ref, s32[32]{0:T(128)S(1)} %copy-done.4, ...), custom_call_target="tpu_custom_call" | custom-call | tf_op jit(solution)/shard_map/attend/pallas_call | solution.py:554
  50.1 14.4 %all_to_all.5.parts_ref = bf16[16,16,128]{2,1,0:T(8,128)(2,1)} all-to-all(bf16[16,16,128]{2,1,0:T(8,128)(2,1)S(1)} %get-tuple-element.22), channel_id=1, replica_groups=mesh['groups'=2,'seq'=16] {'seq'}, dimensions={0} | all-to-all | bytes 131072 | tf_op jit(solution)/shard_map/all_to_all | solution.py:712
  64.5 1.9 %merge.1 = bf16[3,512]{1,0:T(4,128)(2,1)} custom-call(s32[1]{0:T(128)} %bitcast.me_ref, bf16[16,16,128]{2,1,0:T(8,128)(2,1)} %all_to_all.5.parts_ref), custom_call_target="tpu_custom_call" | custom-call | tf_op jit(solution)/shard_map/merge/pallas_call | solution.py:713
  (6 shorter events, 0.1 us)
Async XLA Ops:
  0.6 11.6 %copy-start.4 = (s32[32]{0:T(128)S(1)}, s32[32]{0:T(128)}, u32[]{:S(2)}) copy-start(s32[32]{0:T(128)} %outl_ref.7) | copy-start | bytes 388
  0.6 11.6 %copy-start.3 = (bf16[3,1024]{1,0:T(4,128)(2,1)S(1)}, bf16[3,1024]{1,0:T(4,128)(2,1)}, u32[]{:S(2)}) copy-start(bf16[3,1024]{1,0:T(4,128)(2,1)} %fk_ref.1) | copy-start | bytes 18436
  0.7 11.6 %copy-start.1 = (bf16[3,8192]{1,0:T(4,128)(2,1)S(1)}, bf16[3,8192]{1,0:T(4,128)(2,1)}, u32[]{:S(2)}) copy-start(bf16[3,8192]{1,0:T(4,128)(2,1)} %q_ref.1) | copy-start | bytes 147460
  0.7 17.0 %copy-start.5 = (s32[3,8,16]{2,1,0:T(8,128)S(1)}, s32[3,8,16]{2,1,0:T(8,128)}, u32[]{:S(2)}) copy-start(s32[3,8,16]{2,1,0:T(8,128)} %param.16) | copy-start | bytes 4612
  0.7 17.2 %copy-start = (s32[3,8,256]{2,1,0:T(8,128)S(1)}, s32[3,8,256]{2,1,0:T(8,128)}, u32[]{:S(2)}) copy-start(s32[3,8,256]{2,1,0:T(8,128)} %param.15) | copy-start | bytes 73732
  0.7 17.2 %copy-start.2 = (bf16[3,1024]{1,0:T(4,128)(2,1)S(1)}, bf16[3,1024]{1,0:T(4,128)(2,1)}, u32[]{:S(2)}) copy-start(bf16[3,1024]{1,0:T(4,128)(2,1)} %fv_ref.3) | copy-start | bytes 18436
  7.3 1.8 %collective-permute-start = (f32[80,1024]{1,0:T(8,128)S(1)}, f32[80,1024]{1,0:T(8,128)S(1)}, u32[]{:S(2)}, u32[]{:S(2)}) collective-permute-start(f32[80,1024]{1,0:T(8,128)S(1)} %get-tuple-element.14), channel_id=1, source_target_pairs={{0,1},{1,0},{2,3},{3,2},{4,5},{5,4},{6,7},{7,6},{8,9},{9,8},{10,11... | collective-permute-start | bytes 983048 | tf_op jit(solution)/shard_map/ppermute | solution.py:604
  9.2 6.3 %collective-permute-start.1 = (bf16[80,1024]{1,0:T(8,128)(2,1)S(1)}, bf16[80,1024]{1,0:T(8,128)(2,1)S(1)}, u32[]{:S(2)}, u32[]{:S(2)}) collective-permute-start(bf16[80,1024]{1,0:T(8,128)(2,1)S(1)} %get-tuple-element.26.after_ref), channel_id=1, source_target_pairs={{0,2},{1,5},{2,0},{3,7},{4,6},{5,1},{6,4},{7,3},{8,10},{9,13},{10,... | collective-permute-start | bytes 491528 | tf_op jit(solution)/shard_map/ppermute | solution.py:604
  15.5 7.0 %collective-permute-start.2 = (bf16[80,1024]{1,0:T(8,128)(2,1)S(1)}, bf16[80,1024]{1,0:T(8,128)(2,1)S(1)}, u32[]{:S(2)}, u32[]{:S(2)}) collective-permute-start(bf16[80,1024]{1,0:T(8,128)(2,1)S(1)} %fusion.after_ref), channel_id=1, source_target_pairs={{0,4},{1,3},{2,6},{3,1},{4,0},{5,7},{6,2},{7,5},{8,12},{9,11},{10,... | collective-permute-start | bytes 491528 | tf_op jit(solution)/shard_map/ppermute | solution.py:604
  22.7 10.1 %collective-permute-start.3 = (bf16[80,1024]{1,0:T(8,128)(2,1)S(1)}, bf16[80,1024]{1,0:T(8,128)(2,1)S(1)}, u32[]{:S(2)}, u32[]{:S(2)}) collective-permute-start(bf16[80,1024]{1,0:T(8,128)(2,1)S(1)} %fusion.1.after_ref), channel_id=1, source_target_pairs={{0,8},{1,9},{2,10},{3,11},{4,12},{5,13},{6,14},{7,15},{8,0},{9,1},... | collective-permute-start | bytes 491528 | tf_op jit(solution)/shard_map/ppermute | solution.py:604
  32.9 1.5 %collective-permute-start.4 = (bf16[80,1024]{1,0:T(8,128)(2,1)S(1)}, bf16[80,1024]{1,0:T(8,128)(2,1)S(1)}, u32[]{:S(2)}, u32[]{:S(2)}) collective-permute-start(bf16[80,1024]{1,0:T(8,128)(2,1)S(1)} %add_convert_fusion.zmine_ref), channel_id=1, source_target_pairs={{0,1},{1,0},{2,3},{3,2},{4,5},{5,4},{6,7},{7,6},{8,9},{9,8},{10,11... | collective-permute-start | bytes 491528 | tf_op jit(solution)/shard_map/ppermute | solution.py:604

commit v3 on v2

--- a/solution.py
+++ b/solution.py
@@ -18,8 +18,8 @@
 LANES = 128
 MAIN = 640
 PART = 8
-STRAIGHT = 2
-EARLY = 3
+STRAIGHT = 6
+EARLY = 4
 AHEAD = 3
 NT = (((1,), (1,)), ((), ()))
 TN = (((0,), (0,)), ((), ()))
@@ -168,27 +168,53 @@
         ]
         return jnp.minimum(here, OMOST), found
 
-    def each_part(self, g, steps, copy):
+    def find(self, g, steps, put):
         at = self.starts(g, steps)
         for t in range(steps):
             def part(k, _, t=t):
-                copy([self.span(t, g, k * PART + j) for j in range(PART)], at[t] + k * PART)
+                found = [self.span(t, g, k * PART + j) for j in range(PART)]
+                for j in range(PART):
+                    put(at[t] + (k * PART + j), found[j])
                 return 0
 
-            for k in range(STRAIGHT):
+            for k in range(2):
                 part(k, 0)
-            lax.fori_loop(STRAIGHT, (self.count(t, g) + PART - 1) // PART, part, 0)
-        return at
+            lax.fori_loop(2, (self.count(t, g) + PART - 1) // PART, part, 0)
+        for j in range(PART):
+            put(at[steps] + j, 0)
+
+
+def each_part(slots_ref, g, total, parts_all, spans, copy):
+    def part(k, _):
+        copy([jnp.clip(slots_ref[g, k * PART + j], 0, spans - 1) for j in range(PART)], k * PART)
+        return 0
+
+    straight = min(STRAIGHT, parts_all)
+    for k in range(straight):
+        part(k, 0)
+    lax.fori_loop(straight, (total + PART - 1) // PART, part, 0)
+
+
+def slots_kernel(me_ref, chosen_ref, begin_ref, count_ref, after_ref, slots_ref, tie_ref, *, spans, most):
+    steps = begin_ref.shape[0]
+    tie_ref[...] = jnp.zeros_like(tie_ref)
+    lists = Lists(me_ref, chosen_ref, begin_ref, count_ref, None, spans, most)
+    for g in range(slots_ref.shape[0]):
+        def put(slot, span, g=g):
+            slots_ref[g, slot] = span
+
+        lists.find(g, steps, put)
 
 
 def known_kernel(
-    me_ref, outl_ref, q_ref, fk_ref, ca_ref, sa_ref, cb_ref, sb_ref, cq_ref, sq_ref, keys_hbm, after_ref,
-    kx_ref, w_ref, tie_ref,
-    okeys_ref, xtmp_ref, qtmp_ref, osem, *, per_device, rp, spans
+    me_ref, chosen_ref, begin_ref, count_ref, outl_ref, q_ref, fk_ref, ca_ref, sa_ref, cb_ref, sb_ref, cq_ref, sq_ref, keys_hbm, after_ref,
+    slots_ref, kx_ref, w_ref, tie_ref,
+    okeys_ref, xtmp_ref, qtmp_ref, osem, *, per_device, rp, spans, most
 ):
     steps = q_ref.shape[0]
     tie_ref[...] = jnp.zeros_like(tie_ref)
-    _, o_span = Lists(me_ref, None, None, None, outl_ref, spans).outliers()
+    lists = Lists(me_ref, chosen_ref, begin_ref, count_ref, outl_ref, spans, most)
+    _, o_span = lists.outliers()
     o_copies = [
         pltpu.make_async_copy(
             keys_hbm.at[pl.ds(pl.multiple_of(o_span[j] // 2 * 16, 16), 16)], okeys_ref.at[j], osem.at[j]
@@ -223,6 +249,12 @@
         z = jnp.where(lane_r < HD // 2, 1.0, -1.0) * pltpu.roll(x, HD // 2, 1)
         hi, lo = split2(jnp.concatenate([x.T, z.T], 0))
         w_ref[pk] = jnp.concatenate([hi, lo], 0)
+
+    for i in range(slots_ref.shape[0]):
+        def put(slot, span, i=i):
+            slots_ref[i, slot] = span
+
+        lists.find(KVH - slots_ref.shape[0] + i, steps, put)
 
     blk = cb_ref.shape[0] // SPAN
     turns = []
@@ -251,25 +283,24 @@
 
 
 def values_kernel(
-    me_ref, chosen_ref, begin_ref, count_ref, outl_ref, fv_ref, values_hbm, after_ref, vg_ref, tie_ref,
-    values_ref, vtmp_ref, sem, *, main, g0, most
+    me_ref, count_ref, outl_ref, slotsa_ref, slotsb_ref, fv_ref, values_hbm, after_ref, vg_ref, tie_ref,
+    values_ref, vtmp_ref, sem, *, main, most
 ):
     steps = fv_ref.shape[0]
     rows_all = vtmp_ref.shape[0]
     n = vg_ref.shape[0]
     copies = [
-        pltpu.make_async_copy(values_hbm.at[:, pl.ds((g0 + i) * HD, HD)], values_ref.at[i], sem.at[i]) for i in range(n)
+        pltpu.make_async_copy(values_hbm.at[:, pl.ds(i * HD, HD)], values_ref.at[i], sem.at[i]) for i in range(n)
     ]
-    for c in copies[:AHEAD]:
+    for c in copies[:2]:
         c.start()
     tie_ref[...] = jnp.zeros_like(tie_ref)
     vtmp_ref[...] = jnp.zeros_like(vtmp_ref)
-    lists = Lists(me_ref, chosen_ref, begin_ref, count_ref, outl_ref, values_ref.shape[1] // SPAN, most)
+    spans = values_ref.shape[1] // SPAN
+    lists = Lists(me_ref, None, None, count_ref, outl_ref, spans, most)
     _, o_span = lists.outliers()
 
     for i in range(n):
-        g = g0 + i
-
         def rows_of(span, i=i):
             wide = values_ref[i, pl.ds(pl.multiple_of(span // 2 * 16, 16), 16), :].astype(F32)
             return jnp.where(span % 2 == 0, wide[:8], wide[8:])
@@ -279,12 +310,15 @@
             vtmp_ref[dst, :] = jnp.concatenate([rows_of(span) for span in spans], 0)
 
         copies[i].wait()
-        if i + AHEAD < n:
-            copies[i + AHEAD].start()
+        if i + 2 < n:
+            copies[i + 2].start()
         for j in range(OMOST):
             vtmp_ref[j * SPAN:(j + 1) * SPAN, :] = rows_of(o_span[j])
-        vtmp_ref[OMOST * SPAN:OMOST * SPAN + steps, :] = fv_ref[:, g * HD:(g + 1) * HD].astype(F32)
-        total = lists.each_part(g, steps, put)[steps]
+        vtmp_ref[OMOST * SPAN:OMOST * SPAN + steps, :] = fv_ref[:, i * HD:(i + 1) * HD].astype(F32)
+        total = lists.starts(i, steps)[steps]
+        early = slotsa_ref.shape[0]
+        held, h = (slotsa_ref, i) if i < early else (slotsb_ref, i - early)
+        each_part(held, h, total, (rows_all - LANES) // (PART * SPAN), spans, put)
         vg_ref[i, :LANES + main, :] = vtmp_ref[:LANES + main, :].astype(BF)
         if LANES + main < rows_all:
             def more(k, _, i=i):
@@ -296,7 +330,7 @@
 
 
 def attend_kernel(
-    me_ref, chosen_ref, begin_ref, count_ref, outl_ref, zmine_ref, zother_ref, kx_ref, w_ref, vga_ref, vgb_ref,
+    me_ref, count_ref, outl_ref, slotsa_ref, slotsb_ref, zmine_ref, zother_ref, kx_ref, w_ref, vg_ref,
     ca_ref, sa_ref, cb_ref, sb_ref, keys_hbm,
     kft_hbm, out_ref,
     keys_ref, z_ref, a_ref, qt_ref, kf_ref, kft_ref, kg_ref, cg_ref, sg_ref, sc_ref, cc_ref, ss_ref, acc_ref,
@@ -330,7 +364,8 @@
         store.wait()
         return
 
-    lists = Lists(me_ref, chosen_ref, begin_ref, count_ref, outl_ref, seq_len // SPAN, most)
+    spans = seq_len // SPAN
+    lists = Lists(me_ref, None, None, count_ref, outl_ref, spans, most)
     starts = []
     for g in range(KVH):
         def gather(spans, slot, g=g):
@@ -342,12 +377,11 @@
             for ref, rows in zip((kg_ref, cg_ref, sg_ref), zip(*got)):
                 ref[g, dst, :] = jnp.concatenate(rows, 0)
 
-        starts.append(lists.each_part(g, steps, gather))
+        starts.append(lists.starts(g, steps))
+        early = slotsa_ref.shape[0]
+        held, h = (slotsa_ref, g) if g < early else (slotsb_ref, g - early)
+        each_part(held, h, starts[g][steps], kg_ref.shape[1] // (PART * SPAN), spans, gather)
     totals = [at[steps] for at in starts]
-
-    def values(g, rows):
-        n = vga_ref.shape[0]
-        return vga_ref[g, rows, :] if g < n else vgb_ref[g - n, rows, :]
 
     if stop == 3:
         store.wait()
@@ -456,7 +490,7 @@
         pt = jnp.concatenate(pts, 1)
         for h in range(heads):
             g = pk * heads + h
-            acc = weighted(pt, h, values(g, slice(0, LANES + main)))
+            acc = weighted(pt, h, vg_ref[g, :LANES + main, :])
             for a in range(dests):
                 acc_ref[g * dests + a] = acc[a * rp:(a + 1) * rp]
     if extra > 0:
@@ -470,7 +504,7 @@
 
                     @pl.when(totals[g] * SPAN > main + k * LANES)
                     def _():
-                        acc = weighted(pt, h, values(g, pl.ds(at, LANES)))
+                        acc = weighted(pt, h, vg_ref[g, pl.ds(at, LANES), :])
                         for a in range(dests):
                             acc_ref[g * dests + a] += acc[a * rp:(a + 1) * rp]
 
@@ -545,15 +579,15 @@
 
 
 def attend_call(
-    me, lists, z, z_other, kx, w, vga, vgb, ca, sa, cb, sb, cache_keys,
+    me, lists, z, z_other, kx, w, vg, ca, sa, cb, sb, cache_keys,
     *, steps, per_device, main, most, rp, n_dest, stop=9
 ):
     seq_len, width = cache_keys.shape
     rank = 2 * z.shape[0]
-    tok_all = vga.shape[1] - LANES
+    tok_all = vg.shape[1] - LANES
     return pl.pallas_call(
         functools.partial(attend_kernel, per_device=per_device, steps=steps, main=main, most=most, stop=stop),
-        in_specs=[smem()] * 5 + [vmem()] * 10 + [hbm()],
+        in_specs=[smem()] * 5 + [vmem()] * 9 + [hbm()],
         out_specs=[hbm(), vmem()],
         out_shape=[
             jax.ShapeDtypeStruct((rank, seq_len), F32),
@@ -578,7 +612,7 @@
         ],
         compiler_params=pltpu.CompilerParams(vmem_limit_bytes=42 << 20),
         name="attend",
-    )(me, *lists, z, z_other, kx, w, vga, vgb, ca, sa, cb, sb, in_hbm(cache_keys))
+    )(me, *lists, z, z_other, kx, w, vg, ca, sa, cb, sb, in_hbm(cache_keys))
 
 
 def merge_kernel(me_ref, parts_ref, out_ref, top_ref, sum_ref, *, steps, per_device):
@@ -647,15 +681,26 @@
     shard = jnp.arange(devices, dtype=jnp.int32)
     begin = jnp.sum(jnp.where(shard < myself, shard_counts, 0), axis=2)
     count = jnp.sum(jnp.where(shard == myself, shard_counts, 0), axis=2)
-    lists = (chosen.reshape(n_lists, -1), begin, count, outliers)
+    lists = (chosen.reshape(n_lists, -1), begin, count)
+    places = slots_all + 4 * PART
     tie_shape = jax.ShapeDtypeStruct((1, LANES), F32)
+
+    def early_slots(after):
+        return pl.pallas_call(
+            functools.partial(slots_kernel, spans=seq_len // SPAN, most=most),
+            in_specs=[smem()] * 4 + [anywhere()],
+            out_specs=[smem(), vmem()],
+            out_shape=[jax.ShapeDtypeStruct((EARLY, places), jnp.int32), tie_shape],
+            name="early_slots",
+        )(me, *lists, after)
 
     def known(after):
         return pl.pallas_call(
-            functools.partial(known_kernel, per_device=per_device, rp=rp, spans=seq_len // SPAN),
-            in_specs=[smem()] * 2 + [vmem()] * 8 + [hbm(), anywhere()],
-            out_specs=[vmem()] * 3,
+            functools.partial(known_kernel, per_device=per_device, rp=rp, spans=seq_len // SPAN, most=most),
+            in_specs=[smem()] * 5 + [vmem()] * 8 + [hbm(), anywhere()],
+            out_specs=[smem()] + [vmem()] * 3,
             out_shape=[
+                jax.ShapeDtypeStruct((KVH - EARLY, places), jnp.int32),
                 jax.ShapeDtypeStruct((KVH, LANES, 2 * HD), BF),
                 jax.ShapeDtypeStruct((n_dest * rp // LANES, 4 * HD, LANES), BF),
                 tie_shape,
@@ -668,22 +713,22 @@
             ],
             compiler_params=pltpu.CompilerParams(vmem_limit_bytes=8 << 20),
             name="known_keys",
-        )(me, outliers, queries, fresh_keys, *turns, jnp.cos(late), jnp.sin(late), in_hbm(cache_keys), after)
-
-    def slot_values(g0, n, after):
+        )(me, *lists, outliers, queries, fresh_keys, *turns, jnp.cos(late), jnp.sin(late), in_hbm(cache_keys), after)
+
+    def slot_values(held, after):
         return pl.pallas_call(
-            functools.partial(values_kernel, main=main, g0=g0, most=most),
+            functools.partial(values_kernel, main=main, most=most),
             in_specs=[smem()] * 5 + [vmem(), hbm(), anywhere()],
             out_specs=[vmem()] * 2,
-            out_shape=[jax.ShapeDtypeStruct((n, LANES + tok_all, HD), BF), tie_shape],
+            out_shape=[jax.ShapeDtypeStruct((KVH, LANES + tok_all, HD), BF), tie_shape],
             scratch_shapes=[
-                pltpu.VMEM((n, seq_len, HD), BF),
+                pltpu.VMEM((KVH, seq_len, HD), BF),
                 pltpu.VMEM((LANES + tok_all, HD), F32),
-                pltpu.SemaphoreType.DMA((n,)),
+                pltpu.SemaphoreType.DMA((KVH,)),
             ],
             compiler_params=pltpu.CompilerParams(vmem_limit_bytes=16 << 20),
             name="slot_values",
-        )(me, *lists, fresh_values, in_hbm(cache_values), after)
+        )(me, *held, fresh_values, in_hbm(cache_values), after)
 
     z = keep + swap(send, [(i, i ^ 1) for i in range(devices)])
     hops = [1 << k for k in range(1, devices.bit_length() - 1)]
@@ -693,20 +738,21 @@
         going = z.astype(BF)
         came = swap(going, moves).astype(F32)
         if k == 0:
-            kx, w, tie = known(going)
+            slots_a, tie = early_slots(going)
             came = came + tie[0, 0]
         if k == min(1, len(hops) - 1):
-            vga, tie = slot_values(0, EARLY, going)
+            slots_b, kx, w, tie = known(going)
             came = came + tie[0, 0]
         if k == len(hops) - 1:
-            vgb, tie = slot_values(EARLY, KVH - EARLY, going)
+            held = (count, outliers, slots_a, slots_b)
+            vg, tie = slot_values(held, going)
             came = came + tie[0, 0]
         z = z + came
     z = z.astype(BF)
     z_other = swap(z, [(i, i ^ 1) for i in range(devices)])
 
     kft, parts = attend_call(
-        me, lists, z, z_other, kx, w, vga, vgb, *turns, cache_keys,
+        me, held, z, z_other, kx, w, vg, *turns, cache_keys,
         steps=steps, per_device=per_device, main=main, most=most, rp=rp, n_dest=n_dest,
     )
     parts = lax.all_to_all(parts, "seq", 0, 0, tiled=True)

time: 65.9 us -> 65 us (0.986); the launches traced: 66.4 us -> 64.7 us
  waiting for transfers between devices: 5.02 us -> 2.28 us
  local copies, waits for them, and re-layouts: 0.03 us -> 1.36 us
  other arithmetic: 1.09 us -> 2.29 us
  blocking collectives: 14.4 us -> 13.7 us
    ppermute x5, waiting for transfers between devices: 5.02 us -> 2.28 us  [swap(): return lax.ppermute(x, 'seq', moves)]
    pallas_call x1, Pallas kernels: 15.7 us -> 13.1 us  [attend_call(): pl.pallas_call(functools.partial(attend_kernel, per_device=per_device, st...]
    pallas_call x1, Pallas kernels: 1.81 us -> 3.93 us  [known(): pl.pallas_call(functools.partial(known_kernel, per_device=per_device, rp=...]
    unnamed x12 -> x24, local copies, waits for them, and re-layouts: 0.03 us -> 1.36 us
    all_to_all x1, blocking collectives: 14.4 us -> 13.7 us  [on_device(): parts = lax.all_to_all(parts, 'seq', 0, 0, tiled=True)]
  transfers between devices with their start and end apart: 5 -> 5, of which waited for: 4 -> 3; matrix products, arithmetic and copies ran while one was open for 1% -> 2% of each run, Pallas kernels for 19% -> 23%
where the time goes in v3:
time: 65 us; the launch traced here: 64.7 us
  Pallas kernels  36.2 us (56%)
  blocking collectives  13.7 us (21%)
  starting transfers between devices  8.11 us (12%)
  other arithmetic  2.29 us (4%)
  waiting for transfers between devices  2.28 us (4%)
  local copies, waits for them, and re-layouts  1.36 us (2%)
  between operations  0.85 us (1%)
    all_to_all x1, blocking collectives, on_device(): parts = lax.all_to_all(parts, 'seq', 0, 0, tiled=True)  13.7 us
    pallas_call x1, Pallas kernels, attend_call(): pl.pallas_call(functools.partial(attend_kernel, per_device=per_device, st...  13.1 us
    ppermute x5, starting transfers between devices, swap(): return lax.ppermute(x, 'seq', moves)  8.11 us
    pallas_call x1, Pallas kernels, slot_values(): pl.pallas_call(functools.partial(values_kernel, main=main, most=most), in...  7.25 us
    pallas_call x1, Pallas kernels, sketch_share(): pl.pallas_call(functools.partial(sketch_kernel, scale=1.0 / length, chunk...  6.63 us
    pallas_call x1, Pallas kernels, known(): pl.pallas_call(functools.partial(known_kernel, per_device=per_device, rp=...  3.93 us
    pallas_call x1, Pallas kernels, early_slots(): pl.pallas_call(functools.partial(slots_kernel, spans=seq_len // SPAN, mos...  3.41 us
    ppermute x5, waiting for transfers between devices, swap(): return lax.ppermute(x, 'seq', moves)  2.28 us
  transfers between devices with their start and end apart: 5, of which 3 were waited for; matrix products, arithmetic and copies ran while one was open for 2% of the time, Pallas kernels for 23%

profile of v3, /device:TPU:0, one launch (start us, length us, event | category | flops | bytes accessed | tf_op | source)
XLA Modules:
  0.0 64.7 jit_solution(3287370313845549468)
XLA Ops:
  0.6 0.0 copy-start.10
  0.6 0.0 copy-start
  0.7 0.0 copy-start.8
  0.7 0.0 copy-start.7
  0.7 0.0 copy-start.1
  0.7 0.0 copy-start.6
  0.7 6.6 %sketch_share.1 = (f32[80,1024]{1,0:T(8,128)S(1)}, f32[80,1024]{1,0:T(8,128)S(1)}) custom-call(s32[1]{0:T(128)} %bitcast.me_ref, f32[160,1024]{1,0:T(8,128)} %bitcast.15, bf16[4096,1024]{1,0:T(8,128)(2,1)} %keys_hbm.5), custom_call_target="tpu_custom_call" | custom-call | tf_op jit(solution)/shard_map/sketch_share/pallas_call | solution.py:120
  7.3 0.5 collective-permute-start
  7.9 0.1 pad_maximum_fusion
  8.0 0.3 multiply_sine_fusion
  8.3 0.8 %collective-permute-done = f32[80,1024]{1,0:T(8,128)S(1)} collective-permute-done((f32[80,1024]{1,0:T(8,128)S(1)}, f32[80,1024]{1,0:T(8,128)S(1)}, u32[]{:S(2)}, u32[]{:S(2)}) %collective-permute-start) | collective-permute-done | bytes 327712 | tf_op jit(solution)/shard_map/ppermute | solution.py:638
  9.2 0.0 copy-start.9
  9.2 3.0 %collective-permute-start.1 = (bf16[80,1024]{1,0:T(8,128)(2,1)S(1)}, bf16[80,1024]{1,0:T(8,128)(2,1)S(1)}, u32[]{:S(2)}, u32[]{:S(2)}) collective-permute-start(bf16[80,1024]{1,0:T(8,128)(2,1)S(1)} %get-tuple-element.28.after_ref), channel_id=1, source_target_pairs={{0,2},{1,5},{2,0},{3,7},{4,6},{5,1},{6,4},{7,3},{8,10},{9,13},{10,... | collective-permute-start | bytes 491528 | tf_op jit(solution)/shard_map/ppermute | solution.py:638
  12.1 0.0 copy-done.10
  12.1 0.7 %select_reduce_fusion = (s32[3,8]{1,0:T(4,128)}, s32[3,8]{1,0:T(4,128)}) fusion(s32[3,8,16]{2,1,0:T(8,128)S(1)} %copy-done.10, pred[16]{0:T(512)(128)(4,1)S(1)} %get-tuple-element.38, pred[16]{0:T(512)(128)(4,1)S(1)} %get-tuple-element.39), kind=kLoop, calls=%fused_computation.9 | loop fusion | flops 1488 | bytes 1760 | tf_op jit(solution)/shard_map/reduce_sum | solution.py:682
  12.9 0.0 copy-start.3
  12.9 0.0 copy-done.9
  12.9 3.4 %early_slots.1 = (s32[4,176]{1,0:T(4,128)}, f32[1,128]{1,0:T(1,128)}) custom-call(s32[1]{0:T(128)} %bitcast.me_ref, s32[24,256]{1,0:T(8,128)} %bitcast.10, s32[3,8]{1,0:T(4,128)} %get-tuple-element.26.begin_ref, s32[3,8]{1,0:T(4,128)} %get-tuple-element.27.count_ref, bf16[80,1024]{1,0:T(8,128)(2,1)} %copy-done.9), custom_call_target="tpu_custom_call" | custom-call | tf_op jit(solution)/shard_map/early_slots/pallas_call | solution.py:689
  16.3 0.0 copy-start.11
  16.3 0.0 copy-start.5
  16.3 0.0 collective-permute-done.1
  16.3 0.7 %fusion.after_ref = bf16[80,1024]{1,0:T(8,128)(2,1)S(1)} fusion(f32[80,1024]{1,0:T(8,128)S(1)} %get-tuple-element.29, bf16[80,1024]{1,0:T(8,128)(2,1)S(1)} %collective-permute-done.1, f32[]{:T(128)} %bitcast.16), kind=kLoop, calls=%fused_computation.3 | loop fusion | flops 327680 | bytes 655364 | tf_op jit(solution)/shard_map/convert_element_type | solution.py:738
  17.1 1.8 %collective-permute-start.2 = (bf16[80,1024]{1,0:T(8,128)(2,1)S(1)}, bf16[80,1024]{1,0:T(8,128)(2,1)S(1)}, u32[]{:S(2)}, u32[]{:S(2)}) collective-permute-start(bf16[80,1024]{1,0:T(8,128)(2,1)S(1)} %fusion.after_ref), channel_id=1, source_target_pairs={{0,4},{1,3},{2,6},{3,1},{4,0},{5,7},{6,2},{7,5},{8,12},{9,11},{10,... | collective-permute-start | bytes 491528 | tf_op jit(solution)/shard_map/ppermute | solution.py:638
  18.9 0.1 multiply_sine_fusion.2
  19.0 0.0 copy-done
  19.0 0.0 copy-done.8
  19.0 0.0 copy-done.7
  19.0 0.0 copy-done.1
  19.0 0.0 copy-start.2
  19.0 0.6 copy-done.2
  19.7 0.0 copy-start.4
  19.7 0.7 %copy-done.4 = s32[3,8]{1,0:T(4,128)S(1)} copy-done((s32[3,8]{1,0:T(4,128)S(1)}, s32[3,8]{1,0:T(4,128)}, u32[]{:S(2)}) %copy-start.4) | copy-done | bytes 120
  20.3 3.9 %known_keys.1 = (s32[4,176]{1,0:T(4,128)S(1)}, bf16[8,128,256]{2,1,0:T(8,128)(2,1)S(1)}, bf16[2,512,128]{2,1,0:T(8,128)(2,1)S(1)}, f32[1,128]{1,0:T(1,128)S(1)}) custom-call(s32[1]{0:T(128)} %bitcast.me_ref, s32[24,256]{1,0:T(8,128)S(1)} %bitcast.11, s32[3,8]{1,0:T(4,128)S(1)} %copy-done.4, s32[3,8]{1,0:T(4,128)S(1)} %copy-done.2, s32[32]{0:T(128)S(1)} %copy-done.8, ...), custom_call_target="tpu_custom_call" | custom-call | tf_op jit(solution)/shard_map/known_keys/pallas_call | solution.py:698
  24.3 0.0 collective-permute-done.2
  24.3 0.0 copy-done.11
  24.3 0.1 fusion.1.after_ref
  24.4 2.3 %collective-permute-start.3 = (bf16[80,1024]{1,0:T(8,128)(2,1)S(1)}, bf16[80,1024]{1,0:T(8,128)(2,1)S(1)}, u32[]{:S(2)}, u32[]{:S(2)}) collective-permute-start(bf16[80,1024]{1,0:T(8,128)(2,1)S(1)} %fusion.1.after_ref), channel_id=1, source_target_pairs={{0,8},{1,9},{2,10},{3,11},{4,12},{5,13},{6,14},{7,15},{8,0},{9,1},... | collective-permute-start | bytes 491528 | tf_op jit(solution)/shard_map/ppermute | solution.py:638
  26.7 0.0 copy-done.6
  26.7 0.0 copy-done.3
  26.7 0.0 copy-done.5
  26.7 7.2 %slot_values.1 = (bf16[8,1280,128]{2,1,0:T(8,128)(2,1)S(1)}, f32[1,128]{1,0:T(1,128)S(1)}) custom-call(s32[1]{0:T(128)} %bitcast.me_ref, s32[3,8]{1,0:T(4,128)S(1)} %copy-done.3, s32[32]{0:T(128)S(1)} %copy-done.8, s32[4,176]{1,0:T(4,128)S(1)} %copy-done.5, s32[4,176]{1,0:T(4,128)S(1)} %get-tuple-element.18.slotsb_ref, bf16[3,1024]{1,0:T(4,128)(2,1)S(1)} %copy-done.6, ...), custom_call_target="tpu_custom_call" | custom-call | tf_op jit(solution)/shard_map/slot_values/pallas_call | solution.py:719
  34.0 0.4 collective-permute-done.3
  34.4 0.2 add_convert_fusion.zmine_ref
  34.6 0.5 collective-permute-start.4
  35.1 1.0 %collective-permute-done.4.zother_ref = bf16[80,1024]{1,0:T(8,128)(2,1)S(1)} collective-permute-done((bf16[80,1024]{1,0:T(8,128)(2,1)S(1)}, bf16[80,1024]{1,0:T(8,128)(2,1)S(1)}, u32[]{:S(2)}, u32[]{:S(2)}) %collective-permute-start.4) | collective-permute-done | bytes 163872 | tf_op jit(solution)/shard_map/ppermute | solution.py:638
  36.1 13.1 %attend.1 = (f32[160,4096]{1,0:T(8,128)}, bf16[16,16,128]{2,1,0:T(8,128)(2,1)S(1)}) custom-call(s32[1]{0:T(128)} %bitcast.me_ref, s32[3,8]{1,0:T(4,128)S(1)} %copy-done.3, s32[32]{0:T(128)S(1)} %copy-done.8, s32[4,176]{1,0:T(4,128)S(1)} %copy-done.5, s32[4,176]{1,0:T(4,128)S(1)} %get-tuple-element.18.slotsb_ref, ...), custom_call_target="tpu_custom_call" | custom-call | tf_op jit(solution)/shard_map/attend/pallas_call | solution.py:588
  49.2 13.7 %all_to_all.5.parts_ref = bf16[16,16,128]{2,1,0:T(8,128)(2,1)} all-to-all(bf16[16,16,128]{2,1,0:T(8,128)(2,1)S(1)} %get-tuple-element.24), channel_id=1, replica_groups=mesh['groups'=2,'seq'=16] {'seq'}, dimensions={0} | all-to-all | bytes 131072 | tf_op jit(solution)/shard_map/all_to_all | solution.py:758
  62.9 1.9 %merge.1 = bf16[3,512]{1,0:T(4,128)(2,1)} custom-call(s32[1]{0:T(128)} %bitcast.me_ref, bf16[16,16,128]{2,1,0:T(8,128)(2,1)} %all_to_all.5.parts_ref), custom_call_target="tpu_custom_call" | custom-call | tf_op jit(solution)/shard_map/merge/pallas_call | solution.py:759
  (6 shorter events, 0.1 us)
Async XLA Ops:
  0.6 11.5 %copy-start.10 = (s32[3,8,16]{2,1,0:T(8,128)S(1)}, s32[3,8,16]{2,1,0:T(8,128)}, u32[]{:S(2)}) copy-start(s32[3,8,16]{2,1,0:T(8,128)} %param.16) | copy-start | bytes 4612
  0.6 18.3 %copy-start = (s32[3,8,256]{2,1,0:T(8,128)S(1)}, s32[3,8,256]{2,1,0:T(8,128)}, u32[]{:S(2)}) copy-start(s32[3,8,256]{2,1,0:T(8,128)} %param.15) | copy-start | bytes 73732
  0.7 18.3 %copy-start.8 = (s32[32]{0:T(128)S(1)}, s32[32]{0:T(128)}, u32[]{:S(2)}) copy-start(s32[32]{0:T(128)} %outl_ref.5) | copy-start | bytes 388
  0.7 18.3 %copy-start.7 = (bf16[3,1024]{1,0:T(4,128)(2,1)S(1)}, bf16[3,1024]{1,0:T(4,128)(2,1)}, u32[]{:S(2)}) copy-start(bf16[3,1024]{1,0:T(4,128)(2,1)} %fk_ref.1) | copy-start | bytes 18436
  0.7 18.3 %copy-start.1 = (bf16[3,8192]{1,0:T(4,128)(2,1)S(1)}, bf16[3,8192]{1,0:T(4,128)(2,1)}, u32[]{:S(2)}) copy-start(bf16[3,8192]{1,0:T(4,128)(2,1)} %q_ref.1) | copy-start | bytes 147460
  0.7 26.0 %copy-start.6 = (bf16[3,1024]{1,0:T(4,128)(2,1)S(1)}, bf16[3,1024]{1,0:T(4,128)(2,1)}, u32[]{:S(2)}) copy-start(bf16[3,1024]{1,0:T(4,128)(2,1)} %fv_ref.1) | copy-start | bytes 18436
  7.3 1.8 %collective-permute-start = (f32[80,1024]{1,0:T(8,128)S(1)}, f32[80,1024]{1,0:T(8,128)S(1)}, u32[]{:S(2)}, u32[]{:S(2)}) collective-permute-start(f32[80,1024]{1,0:T(8,128)S(1)} %get-tuple-element.15), channel_id=1, source_target_pairs={{0,1},{1,0},{2,3},{3,2},{4,5},{5,4},{6,7},{7,6},{8,9},{9,8},{10,11... | collective-permute-start | bytes 983048 | tf_op jit(solution)/shard_map/ppermute | solution.py:638
  9.2 3.7 %copy-start.9 = (bf16[80,1024]{1,0:T(8,128)(2,1)}, bf16[80,1024]{1,0:T(8,128)(2,1)S(1)}, u32[]{:S(2)}) copy-start(bf16[80,1024]{1,0:T(8,128)(2,1)S(1)} %get-tuple-element.28.after_ref) | copy-start | bytes 491524
  9.2 7.2 %collective-permute-start.1 = (bf16[80,1024]{1,0:T(8,128)(2,1)S(1)}, bf16[80,1024]{1,0:T(8,128)(2,1)S(1)}, u32[]{:S(2)}, u32[]{:S(2)}) collective-permute-start(bf16[80,1024]{1,0:T(8,128)(2,1)S(1)} %get-tuple-element.28.after_ref), channel_id=1, source_target_pairs={{0,2},{1,5},{2,0},{3,7},{4,6},{5,1},{6,4},{7,3},{8,10},{9,13},{10,... | collective-permute-start | bytes 491528 | tf_op jit(solution)/shard_map/ppermute | solution.py:638
  12.9 13.9 %copy-start.3 = (s32[3,8]{1,0:T(4,128)S(1)}, s32[3,8]{1,0:T(4,128)}, u32[]{:S(2)}) copy-start(s32[3,8]{1,0:T(4,128)} %get-tuple-element.27.count_ref) | copy-start | bytes 292
  16.3 8.0 %copy-start.11 = (f32[1,128]{1,0:T(1,128)S(1)}, f32[1,128]{1,0:T(1,128)}, u32[]{:S(2)}) copy-start(f32[1,128]{1,0:T(1,128)} %get-tuple-element.17) | copy-start | bytes 1540
  16.3 10.4 %copy-start.5 = (s32[4,176]{1,0:T(4,128)S(1)}, s32[4,176]{1,0:T(4,128)}, u32[]{:S(2)}) copy-start(s32[4,176]{1,0:T(4,128)} %get-tuple-element.16.slotsa_ref) | copy-start | bytes 8452
  17.1 7.2 %collective-permute-start.2 = (bf16[80,1024]{1,0:T(8,128)(2,1)S(1)}, bf16[80,1024]{1,0:T(8,128)(2,1)S(1)}, u32[]{:S(2)}, u32[]{:S(2)}) collective-permute-start(bf16[80,1024]{1,0:T(8,128)(2,1)S(1)} %fusion.after_ref), channel_id=1, source_target_pairs={{0,4},{1,3},{2,6},{3,1},{4,0},{5,7},{6,2},{7,5},{8,12},{9,11},{10,... | collective-permute-start | bytes 491528 | tf_op jit(solution)/shard_map/ppermute | solution.py:638
  19.0 0.7 %copy-start.2 = (s32[3,8]{1,0:T(4,128)S(1)}, s32[3,8]{1,0:T(4,128)}, u32[]{:S(2)}) copy-start(s32[3,8]{1,0:T(4,128)} %get-tuple-element.27.count_ref) | copy-start | bytes 292
  19.7 0.7 %copy-start.4 = (s32[3,8]{1,0:T(4,128)S(1)}, s32[3,8]{1,0:T(4,128)}, u32[]{:S(2)}) copy-start(s32[3,8]{1,0:T(4,128)} %get-tuple-element.26.begin_ref) | copy-start | bytes 292
  24.4 10.0 %collective-permute-start.3 = (bf16[80,1024]{1,0:T(8,128)(2,1)S(1)}, bf16[80,1024]{1,0:T(8,128)(2,1)S(1)}, u32[]{:S(2)}, u32[]{:S(2)}) collective-permute-start(bf16[80,1024]{1,0:T(8,128)(2,1)S(1)} %fusion.1.after_ref), channel_id=1, source_target_pairs={{0,8},{1,9},{2,10},{3,11},{4,12},{5,13},{6,14},{7,15},{8,0},{9,1},... | collective-permute-start | bytes 491528 | tf_op jit(solution)/shard_map/ppermute | solution.py:638
  34.6 1.5 %collective-permute-start.4 = (bf16[80,1024]{1,0:T(8,128)(2,1)S(1)}, bf16[80,1024]{1,0:T(8,128)(2,1)S(1)}, u32[]{:S(2)}, u32[]{:S(2)}) collective-permute-start(bf16[80,1024]{1,0:T(8,128)(2,1)S(1)} %add_convert_fusion.zmine_ref), channel_id=1, source_target_pairs={{0,1},{1,0},{2,3},{3,2},{4,5},{5,4},{6,7},{7,6},{8,9},{9,8},{10,11... | collective-permute-start | bytes 491528 | tf_op jit(solution)/shard_map/ppermute | solution.py:638

commit v4 on v2

--- a/solution.py
+++ b/solution.py
@@ -16,9 +16,10 @@
 F32 = jnp.float32
 DEAD = -1e30
 LANES = 128
-MAIN = 640
+MAIN = 896
+ROWS = 512
 PART = 8
-STRAIGHT = 2
+STRAIGHT = 6
 EARLY = 3
 AHEAD = 3
 NT = (((1,), (1,)), ((), ()))
@@ -168,17 +169,28 @@
         ]
         return jnp.minimum(here, OMOST), found
 
-    def each_part(self, g, steps, copy):
+    def find(self, g, steps, copy):
         at = self.starts(g, steps)
         for t in range(steps):
             def part(k, _, t=t):
                 copy([self.span(t, g, k * PART + j) for j in range(PART)], at[t] + k * PART)
                 return 0
 
-            for k in range(STRAIGHT):
+            for k in range(2):
                 part(k, 0)
-            lax.fori_loop(STRAIGHT, (self.count(t, g) + PART - 1) // PART, part, 0)
+            lax.fori_loop(2, (self.count(t, g) + PART - 1) // PART, part, 0)
         return at
+
+
+def each_part(slots_ref, g, total, parts_all, spans, copy):
+    def part(k, _):
+        copy([jnp.clip(slots_ref[g, k * PART + j], 0, spans - 1) for j in range(PART)], k * PART)
+        return 0
+
+    straight = min(STRAIGHT, parts_all)
+    for k in range(straight):
+        part(k, 0)
+    lax.fori_loop(straight, (total + PART - 1) // PART, part, 0)
 
 
 def known_kernel(
@@ -251,7 +263,7 @@
 
 
 def values_kernel(
-    me_ref, chosen_ref, begin_ref, count_ref, outl_ref, fv_ref, values_hbm, after_ref, vg_ref, tie_ref,
+    me_ref, chosen_ref, begin_ref, count_ref, outl_ref, fv_ref, values_hbm, after_ref, slots_ref, vg_ref, tie_ref,
     values_ref, vtmp_ref, sem, *, main, g0, most
 ):
     steps = fv_ref.shape[0]
@@ -260,31 +272,32 @@
     copies = [
         pltpu.make_async_copy(values_hbm.at[:, pl.ds((g0 + i) * HD, HD)], values_ref.at[i], sem.at[i]) for i in range(n)
     ]
-    for c in copies[:AHEAD]:
+    for c in copies[:2]:
         c.start()
     tie_ref[...] = jnp.zeros_like(tie_ref)
     vtmp_ref[...] = jnp.zeros_like(vtmp_ref)
-    lists = Lists(me_ref, chosen_ref, begin_ref, count_ref, outl_ref, values_ref.shape[1] // SPAN, most)
+    spans = values_ref.shape[1] // SPAN
+    lists = Lists(me_ref, chosen_ref, begin_ref, count_ref, outl_ref, spans, most)
     _, o_span = lists.outliers()
 
     for i in range(n):
-        g = g0 + i
-
         def rows_of(span, i=i):
             wide = values_ref[i, pl.ds(pl.multiple_of(span // 2 * 16, 16), 16), :].astype(F32)
             return jnp.where(span % 2 == 0, wide[:8], wide[8:])
 
-        def put(spans, slot, rows_of=rows_of):
+        def put(spans, slot, i=i, rows_of=rows_of):
+            for j, span in enumerate(spans):
+                slots_ref[i, slot + j] = span
             dst = pl.ds(pl.multiple_of(LANES + slot * SPAN, SPAN), PART * SPAN)
             vtmp_ref[dst, :] = jnp.concatenate([rows_of(span) for span in spans], 0)
 
         copies[i].wait()
-        if i + AHEAD < n:
-            copies[i + AHEAD].start()
+        if i + 2 < n:
+            copies[i + 2].start()
         for j in range(OMOST):
             vtmp_ref[j * SPAN:(j + 1) * SPAN, :] = rows_of(o_span[j])
-        vtmp_ref[OMOST * SPAN:OMOST * SPAN + steps, :] = fv_ref[:, g * HD:(g + 1) * HD].astype(F32)
-        total = lists.each_part(g, steps, put)[steps]
+        vtmp_ref[OMOST * SPAN:OMOST * SPAN + steps, :] = fv_ref[:, (g0 + i) * HD:(g0 + i + 1) * HD].astype(F32)
+        total = lists.find(g0 + i, steps, put)[steps]
         vg_ref[i, :LANES + main, :] = vtmp_ref[:LANES + main, :].astype(BF)
         if LANES + main < rows_all:
             def more(k, _, i=i):
@@ -296,7 +309,7 @@
 
 
 def attend_kernel(
-    me_ref, chosen_ref, begin_ref, count_ref, outl_ref, zmine_ref, zother_ref, kx_ref, w_ref, vga_ref, vgb_ref,
+    me_ref, count_ref, outl_ref, slotsa_ref, slotsb_ref, zmine_ref, zother_ref, kx_ref, w_ref, vga_ref, vgb_ref,
     ca_ref, sa_ref, cb_ref, sb_ref, keys_hbm,
     kft_hbm, out_ref,
     keys_ref, z_ref, a_ref, qt_ref, kf_ref, kft_ref, kg_ref, cg_ref, sg_ref, sc_ref, cc_ref, ss_ref, acc_ref,
@@ -330,8 +343,14 @@
         store.wait()
         return
 
-    lists = Lists(me_ref, chosen_ref, begin_ref, count_ref, outl_ref, seq_len // SPAN, most)
+    spans = seq_len // SPAN
+    lists = Lists(me_ref, None, None, count_ref, outl_ref, spans, most)
     starts = []
+
+    def values(g, rows):
+        n = vga_ref.shape[0]
+        return vga_ref[g, rows, :] if g < n else vgb_ref[g - n, rows, :]
+
     for g in range(KVH):
         def gather(spans, slot, g=g):
             got = []
@@ -342,12 +361,11 @@
             for ref, rows in zip((kg_ref, cg_ref, sg_ref), zip(*got)):
                 ref[g, dst, :] = jnp.concatenate(rows, 0)
 
-        starts.append(lists.each_part(g, steps, gather))
+        starts.append(lists.starts(g, steps))
+        early = slotsa_ref.shape[0]
+        held, h = (slotsa_ref, g) if g < early else (slotsb_ref, g - early)
+        each_part(held, h, starts[g][steps], kg_ref.shape[1] // (PART * SPAN), spans, gather)
     totals = [at[steps] for at in starts]
-
-    def values(g, rows):
-        n = vga_ref.shape[0]
-        return vga_ref[g, rows, :] if g < n else vgb_ref[g - n, rows, :]
 
     if stop == 3:
         store.wait()
@@ -418,9 +436,12 @@
         s = known_scores(pk)
         sc_ref[pk, :LANES, :] = s
         top = jnp.max(s, axis=0, keepdims=True)
-        s = slot_scores(pk, 0, main, limits[pk])
-        sc_ref[pk, LANES:LANES + main, :] = s
-        tops.append(jnp.maximum(top, jnp.max(s, axis=0, keepdims=True)))
+        for at in range(0, main, ROWS):
+            n = min(ROWS, main - at)
+            s = slot_scores(pk, at, n, limits[pk])
+            sc_ref[pk, LANES + at:LANES + at + n, :] = s
+            top = jnp.maximum(top, jnp.max(s, axis=0, keepdims=True))
+        tops.append(top)
     if extra > 0:
         for pk in range(packs):
             def more(k, top, pk=pk):
@@ -576,7 +597,7 @@
             pltpu.SemaphoreType.DMA,
             pltpu.SemaphoreType.DMA,
         ],
-        compiler_params=pltpu.CompilerParams(vmem_limit_bytes=42 << 20),
+        compiler_params=pltpu.CompilerParams(vmem_limit_bytes=46 << 20),
         name="attend",
     )(me, *lists, z, z_other, kx, w, vga, vgb, ca, sa, cb, sb, in_hbm(cache_keys))
 
@@ -647,7 +668,8 @@
     shard = jnp.arange(devices, dtype=jnp.int32)
     begin = jnp.sum(jnp.where(shard < myself, shard_counts, 0), axis=2)
     count = jnp.sum(jnp.where(shard == myself, shard_counts, 0), axis=2)
-    lists = (chosen.reshape(n_lists, -1), begin, count, outliers)
+    lists = (chosen.reshape(n_lists, -1), begin, count)
+    places = slots_all + 4 * PART
     tie_shape = jax.ShapeDtypeStruct((1, LANES), F32)
 
     def known(after):
@@ -674,8 +696,12 @@
         return pl.pallas_call(
             functools.partial(values_kernel, main=main, g0=g0, most=most),
             in_specs=[smem()] * 5 + [vmem(), hbm(), anywhere()],
-            out_specs=[vmem()] * 2,
-            out_shape=[jax.ShapeDtypeStruct((n, LANES + tok_all, HD), BF), tie_shape],
+            out_specs=[smem(), vmem(), vmem()],
+            out_shape=[
+                jax.ShapeDtypeStruct((n, places), jnp.int32),
+                jax.ShapeDtypeStruct((n, LANES + tok_all, HD), BF),
+                tie_shape,
+            ],
             scratch_shapes=[
                 pltpu.VMEM((n, seq_len, HD), BF),
                 pltpu.VMEM((LANES + tok_all, HD), F32),
@@ -683,7 +709,7 @@
             ],
             compiler_params=pltpu.CompilerParams(vmem_limit_bytes=16 << 20),
             name="slot_values",
-        )(me, *lists, fresh_values, in_hbm(cache_values), after)
+        )(me, *lists, outliers, fresh_values, in_hbm(cache_values), after)
 
     z = keep + swap(send, [(i, i ^ 1) for i in range(devices)])
     hops = [1 << k for k in range(1, devices.bit_length() - 1)]
@@ -696,17 +722,17 @@
             kx, w, tie = known(going)
             came = came + tie[0, 0]
         if k == min(1, len(hops) - 1):
-            vga, tie = slot_values(0, EARLY, going)
+            slots_a, vga, tie = slot_values(0, EARLY, going)
             came = came + tie[0, 0]
         if k == len(hops) - 1:
-            vgb, tie = slot_values(EARLY, KVH - EARLY, going)
+            slots_b, vgb, tie = slot_values(EARLY, KVH - EARLY, going)
             came = came + tie[0, 0]
         z = z + came
     z = z.astype(BF)
     z_other = swap(z, [(i, i ^ 1) for i in range(devices)])
 
     kft, parts = attend_call(
-        me, lists, z, z_other, kx, w, vga, vgb, *turns, cache_keys,
+        me, (count, outliers, slots_a, slots_b), z, z_other, kx, w, vga, vgb, *turns, cache_keys,
         steps=steps, per_device=per_device, main=main, most=most, rp=rp, n_dest=n_dest,
     )
     parts = lax.all_to_all(parts, "seq", 0, 0, tiled=True)

time: 65.9 us -> 63.5 us (0.964)
  blocking collectives: 14.4 us -> 12.5 us
  waiting for transfers between devices: 5.02 us -> 4.23 us
    all_to_all x1, blocking collectives: 14.4 us -> 12.5 us  [on_device(): parts = lax.all_to_all(parts, 'seq', 0, 0, tiled=True)]
    pallas_call x2, Pallas kernels: 10.8 us -> 12.6 us  [slot_values(): pl.pallas_call(functools.partial(values_kernel, main=main, g0=g0, most=mo...]
    pallas_call x1, Pallas kernels: 15.7 us -> 14.1 us  [attend_call(): pl.pallas_call(functools.partial(attend_kernel, per_device=per_device, st...]
    ppermute x5, waiting for transfers between devices: 5.02 us -> 4.23 us  [swap(): return lax.ppermute(x, 'seq', moves)]
  transfers between devices with their start and end apart: 5 -> 5, of which waited for: 4 -> 4; matrix products, arithmetic and copies ran while one was open for 1% -> 1% of each run, Pallas kernels for 19% -> 23%
where the time goes in v4:
time: 63.5 us; the launch traced here: 63.7 us
  Pallas kernels  37.1 us (58%)
  blocking collectives  12.5 us (20%)
  starting transfers between devices  7.95 us (13%)
  waiting for transfers between devices  4.23 us (7%)
  other arithmetic  1.09 us (2%)
  between operations  0.82 us (1%)
    pallas_call x1, Pallas kernels, attend_call(): pl.pallas_call(functools.partial(attend_kernel, per_device=per_device, st...  14.1 us
    pallas_call x2, Pallas kernels, slot_values(): pl.pallas_call(functools.partial(values_kernel, main=main, g0=g0, most=mo...  12.6 us
    all_to_all x1, blocking collectives, on_device(): parts = lax.all_to_all(parts, 'seq', 0, 0, tiled=True)  12.5 us
    ppermute x5, starting transfers between devices, swap(): return lax.ppermute(x, 'seq', moves)  7.95 us
    pallas_call x1, Pallas kernels, sketch_share(): pl.pallas_call(functools.partial(sketch_kernel, scale=1.0 / length, chunk...  6.63 us
    ppermute x5, waiting for transfers between devices, swap(): return lax.ppermute(x, 'seq', moves)  4.23 us
    pallas_call x1, Pallas kernels, on_device(): pl.pallas_call(functools.partial(merge_kernel, steps=steps, per_device=pe...  1.88 us
    pallas_call x1, Pallas kernels, known(): pl.pallas_call(functools.partial(known_kernel, per_device=per_device, rp=...  1.88 us
  transfers between devices with their start and end apart: 5, of which 4 were waited for; matrix products, arithmetic and copies ran while one was open for 1% of the time, Pallas kernels for 23%

profile of v4, /device:TPU:0, one launch (start us, length us, event | category | flops | bytes accessed | tf_op | source)
XLA Modules:
  0.0 63.7 jit_solution(13752086674440479210)
XLA Ops:
  0.6 0.0 copy-start.4
  0.6 0.0 copy-start.3
  0.7 0.0 copy-start.1
  0.7 0.0 copy-start.5
  0.7 0.0 copy-start
  0.7 0.0 copy-start.2
  0.7 6.6 %sketch_share.1 = (f32[80,1024]{1,0:T(8,128)S(1)}, f32[80,1024]{1,0:T(8,128)S(1)}) custom-call(s32[1]{0:T(128)} %bitcast.me_ref, f32[160,1024]{1,0:T(8,128)} %bitcast.18, bf16[4096,1024]{1,0:T(8,128)(2,1)} %keys_hbm.5), custom_call_target="tpu_custom_call" | custom-call | tf_op jit(solution)/shard_map/sketch_share/pallas_call | solution.py:121
  7.3 0.5 collective-permute-start
  7.9 0.1 pad_maximum_fusion
  8.0 0.3 multiply_sine_fusion
  8.3 0.8 %collective-permute-done = f32[80,1024]{1,0:T(8,128)S(1)} collective-permute-done((f32[80,1024]{1,0:T(8,128)S(1)}, f32[80,1024]{1,0:T(8,128)S(1)}, u32[]{:S(2)}, u32[]{:S(2)}) %collective-permute-start) | collective-permute-done | bytes 327712 | tf_op jit(solution)/shard_map/ppermute | solution.py:625
  9.2 3.0 %collective-permute-start.1 = (bf16[80,1024]{1,0:T(8,128)(2,1)S(1)}, bf16[80,1024]{1,0:T(8,128)(2,1)S(1)}, u32[]{:S(2)}, u32[]{:S(2)}) collective-permute-start(bf16[80,1024]{1,0:T(8,128)(2,1)S(1)} %get-tuple-element.30.after_ref), channel_id=1, source_target_pairs={{0,2},{1,5},{2,0},{3,7},{4,6},{5,1},{6,4},{7,3},{8,10},{9,13},{10,... | collective-permute-start | bytes 491528 | tf_op jit(solution)/shard_map/ppermute | solution.py:625
  12.1 0.1 multiply_sine_fusion.2
  12.2 0.0 copy-done.4
  12.2 0.0 copy-done.3
  12.2 0.0 copy-done.1
  12.3 1.9 %known_keys.1 = (bf16[8,128,256]{2,1,0:T(8,128)(2,1)S(1)}, bf16[2,512,128]{2,1,0:T(8,128)(2,1)S(1)}, f32[1,128]{1,0:T(1,128)S(1)}) custom-call(s32[1]{0:T(128)} %bitcast.me_ref, s32[32]{0:T(128)S(1)} %copy-done.4, bf16[3,8192]{1,0:T(4,128)(2,1)S(1)} %copy-done.1, bf16[3,1024]{1,0:T(4,128)(2,1)S(1)} %copy-done.3, f32[64,128]{1,0:T(8,128)S(1)} %get-tuple-element.38.ca_ref, ...), custom_call_target="tpu_custom_call" | custom-call | tf_op jit(solution)/shard_map/known_keys/pallas_call | solution.py:676
  14.1 1.3 %collective-permute-done.1 = bf16[80,1024]{1,0:T(8,128)(2,1)S(1)} collective-permute-done((bf16[80,1024]{1,0:T(8,128)(2,1)S(1)}, bf16[80,1024]{1,0:T(8,128)(2,1)S(1)}, u32[]{:S(2)}, u32[]{:S(2)}) %collective-permute-start.1) | collective-permute-done | bytes 163872 | tf_op jit(solution)/shard_map/ppermute | solution.py:625
  15.4 0.1 fusion.after_ref
  15.5 2.1 %collective-permute-start.2 = (bf16[80,1024]{1,0:T(8,128)(2,1)S(1)}, bf16[80,1024]{1,0:T(8,128)(2,1)S(1)}, u32[]{:S(2)}, u32[]{:S(2)}) collective-permute-start(bf16[80,1024]{1,0:T(8,128)(2,1)S(1)} %fusion.after_ref), channel_id=1, source_target_pairs={{0,4},{1,3},{2,6},{3,1},{4,0},{5,7},{6,2},{7,5},{8,12},{9,11},{10,... | collective-permute-start | bytes 491528 | tf_op jit(solution)/shard_map/ppermute | solution.py:625
  17.6 0.0 copy-done.5
  17.7 0.2 select_reduce_fusion
  17.8 0.0 copy-done
  17.8 0.0 copy-done.2
  17.9 5.6 %slot_values.2 = (s32[3,176]{1,0:T(4,128)S(1)}, bf16[3,1280,128]{2,1,0:T(8,128)(2,1)S(1)}, f32[1,128]{1,0:T(1,128)S(1)}) custom-call(s32[1]{0:T(128)} %bitcast.me_ref, s32[24,256]{1,0:T(8,128)S(1)} %bitcast.10, s32[3,8]{1,0:T(4,128)S(1)} %get-tuple-element.28.begin_ref, s32[3,8]{1,0:T(4,128)S(1)} %get-tuple-element.29.count_ref, s32[32]{0:T(128)S(1)} %copy-done.4, ...), custom_call_target="tpu_custom_call" | custom-call | tf_op jit(solution)/shard_map/slot_values/pallas_call | solution.py:696
  23.4 0.0 collective-permute-done.2
  23.5 0.1 fusion.1.after_ref
  23.6 2.3 %collective-permute-start.3 = (bf16[80,1024]{1,0:T(8,128)(2,1)S(1)}, bf16[80,1024]{1,0:T(8,128)(2,1)S(1)}, u32[]{:S(2)}, u32[]{:S(2)}) collective-permute-start(bf16[80,1024]{1,0:T(8,128)(2,1)S(1)} %fusion.1.after_ref), channel_id=1, source_target_pairs={{0,8},{1,9},{2,10},{3,11},{4,12},{5,13},{6,14},{7,15},{8,0},{9,1},... | collective-permute-start | bytes 491528 | tf_op jit(solution)/shard_map/ppermute | solution.py:625
  25.8 7.0 %slot_values.3 = (s32[5,176]{1,0:T(8,128)S(1)}, bf16[5,1280,128]{2,1,0:T(8,128)(2,1)S(1)}, f32[1,128]{1,0:T(1,128)S(1)}) custom-call(s32[1]{0:T(128)} %bitcast.me_ref, s32[24,256]{1,0:T(8,128)S(1)} %bitcast.11, s32[3,8]{1,0:T(4,128)S(1)} %get-tuple-element.28.begin_ref, s32[3,8]{1,0:T(4,128)S(1)} %get-tuple-element.29.count_ref, s32[32]{0:T(128)S(1)} %copy-done.4, ...), custom_call_target="tpu_custom_call" | custom-call | tf_op jit(solution)/shard_map/slot_values/pallas_call | solution.py:696
  32.9 0.7 %collective-permute-done.3 = bf16[80,1024]{1,0:T(8,128)(2,1)S(1)} collective-permute-done((bf16[80,1024]{1,0:T(8,128)(2,1)S(1)}, bf16[80,1024]{1,0:T(8,128)(2,1)S(1)}, u32[]{:S(2)}, u32[]{:S(2)}) %collective-permute-start.3) | collective-permute-done | bytes 163872 | tf_op jit(solution)/shard_map/ppermute | solution.py:625
  33.6 0.1 add_convert_fusion.zmine_ref
  33.8 0.1 collective-permute-start.4
  33.8 1.4 %collective-permute-done.4.zother_ref = bf16[80,1024]{1,0:T(8,128)(2,1)S(1)} collective-permute-done((bf16[80,1024]{1,0:T(8,128)(2,1)S(1)}, bf16[80,1024]{1,0:T(8,128)(2,1)S(1)}, u32[]{:S(2)}, u32[]{:S(2)}) %collective-permute-start.4) | collective-permute-done | bytes 163872 | tf_op jit(solution)/shard_map/ppermute | solution.py:625
  35.2 14.1 %attend.1 = (f32[160,4096]{1,0:T(8,128)}, bf16[16,16,128]{2,1,0:T(8,128)(2,1)S(1)}) custom-call(s32[1]{0:T(128)} %bitcast.me_ref, s32[3,8]{1,0:T(4,128)S(1)} %get-tuple-element.29.count_ref, s32[32]{0:T(128)S(1)} %copy-done.4, s32[3,176]{1,0:T(4,128)S(1)} %get-tuple-element.18.slotsa_ref, s32[5,176]{1,0:T(8,128)S(1)} %get-tuple-element.20.slotsb_ref, ...), custom_call_target="tpu_custom_call" | custom-call | tf_op jit(solution)/shard_map/attend/pallas_call | solution.py:575
  49.3 12.5 %all_to_all.5.parts_ref = bf16[16,16,128]{2,1,0:T(8,128)(2,1)} all-to-all(bf16[16,16,128]{2,1,0:T(8,128)(2,1)S(1)} %get-tuple-element.26), channel_id=1, replica_groups=mesh['groups'=2,'seq'=16] {'seq'}, dimensions={0} | all-to-all | bytes 131072 | tf_op jit(solution)/shard_map/all_to_all | solution.py:738
  61.8 1.9 %merge.1 = bf16[3,512]{1,0:T(4,128)(2,1)} custom-call(s32[1]{0:T(128)} %bitcast.me_ref, bf16[16,16,128]{2,1,0:T(8,128)(2,1)} %all_to_all.5.parts_ref), custom_call_target="tpu_custom_call" | custom-call | tf_op jit(solution)/shard_map/merge/pallas_call | solution.py:739
  (6 shorter events, 0.1 us)
Async XLA Ops:
  0.6 11.6 %copy-start.4 = (s32[32]{0:T(128)S(1)}, s32[32]{0:T(128)}, u32[]{:S(2)}) copy-start(s32[32]{0:T(128)} %outl_ref.7) | copy-start | bytes 388
  0.6 11.6 %copy-start.3 = (bf16[3,1024]{1,0:T(4,128)(2,1)S(1)}, bf16[3,1024]{1,0:T(4,128)(2,1)}, u32[]{:S(2)}) copy-start(bf16[3,1024]{1,0:T(4,128)(2,1)} %fk_ref.1) | copy-start | bytes 18436
  0.7 11.6 %copy-start.1 = (bf16[3,8192]{1,0:T(4,128)(2,1)S(1)}, bf16[3,8192]{1,0:T(4,128)(2,1)}, u32[]{:S(2)}) copy-start(bf16[3,8192]{1,0:T(4,128)(2,1)} %q_ref.1) | copy-start | bytes 147460
  0.7 17.0 %copy-start.5 = (s32[3,8,16]{2,1,0:T(8,128)S(1)}, s32[3,8,16]{2,1,0:T(8,128)}, u32[]{:S(2)}) copy-start(s32[3,8,16]{2,1,0:T(8,128)} %param.16) | copy-start | bytes 4612
  0.7 17.2 %copy-start = (s32[3,8,256]{2,1,0:T(8,128)S(1)}, s32[3,8,256]{2,1,0:T(8,128)}, u32[]{:S(2)}) copy-start(s32[3,8,256]{2,1,0:T(8,128)} %param.15) | copy-start | bytes 73732
  0.7 17.2 %copy-start.2 = (bf16[3,1024]{1,0:T(4,128)(2,1)S(1)}, bf16[3,1024]{1,0:T(4,128)(2,1)}, u32[]{:S(2)}) copy-start(bf16[3,1024]{1,0:T(4,128)(2,1)} %fv_ref.3) | copy-start | bytes 18436
  7.3 1.8 %collective-permute-start = (f32[80,1024]{1,0:T(8,128)S(1)}, f32[80,1024]{1,0:T(8,128)S(1)}, u32[]{:S(2)}, u32[]{:S(2)}) collective-permute-start(f32[80,1024]{1,0:T(8,128)S(1)} %get-tuple-element.16), channel_id=1, source_target_pairs={{0,1},{1,0},{2,3},{3,2},{4,5},{5,4},{6,7},{7,6},{8,9},{9,8},{10,11... | collective-permute-start | bytes 983048 | tf_op jit(solution)/shard_map/ppermute | solution.py:625
  9.2 6.3 %collective-permute-start.1 = (bf16[80,1024]{1,0:T(8,128)(2,1)S(1)}, bf16[80,1024]{1,0:T(8,128)(2,1)S(1)}, u32[]{:S(2)}, u32[]{:S(2)}) collective-permute-start(bf16[80,1024]{1,0:T(8,128)(2,1)S(1)} %get-tuple-element.30.after_ref), channel_id=1, source_target_pairs={{0,2},{1,5},{2,0},{3,7},{4,6},{5,1},{6,4},{7,3},{8,10},{9,13},{10,... | collective-permute-start | bytes 491528 | tf_op jit(solution)/shard_map/ppermute | solution.py:625
  15.5 7.9 %collective-permute-start.2 = (bf16[80,1024]{1,0:T(8,128)(2,1)S(1)}, bf16[80,1024]{1,0:T(8,128)(2,1)S(1)}, u32[]{:S(2)}, u32[]{:S(2)}) collective-permute-start(bf16[80,1024]{1,0:T(8,128)(2,1)S(1)} %fusion.after_ref), channel_id=1, source_target_pairs={{0,4},{1,3},{2,6},{3,1},{4,0},{5,7},{6,2},{7,5},{8,12},{9,11},{10,... | collective-permute-start | bytes 491528 | tf_op jit(solution)/shard_map/ppermute | solution.py:625
  23.6 10.0 %collective-permute-start.3 = (bf16[80,1024]{1,0:T(8,128)(2,1)S(1)}, bf16[80,1024]{1,0:T(8,128)(2,1)S(1)}, u32[]{:S(2)}, u32[]{:S(2)}) collective-permute-start(bf16[80,1024]{1,0:T(8,128)(2,1)S(1)} %fusion.1.after_ref), channel_id=1, source_target_pairs={{0,8},{1,9},{2,10},{3,11},{4,12},{5,13},{6,14},{7,15},{8,0},{9,1},... | collective-permute-start | bytes 491528 | tf_op jit(solution)/shard_map/ppermute | solution.py:625
  33.8 1.5 %collective-permute-start.4 = (bf16[80,1024]{1,0:T(8,128)(2,1)S(1)}, bf16[80,1024]{1,0:T(8,128)(2,1)S(1)}, u32[]{:S(2)}, u32[]{:S(2)}) collective-permute-start(bf16[80,1024]{1,0:T(8,128)(2,1)S(1)} %add_convert_fusion.zmine_ref), channel_id=1, source_target_pairs={{0,1},{1,0},{2,3},{3,2},{4,5},{5,4},{6,7},{7,6},{8,9},{9,8},{10,11... | collective-permute-start | bytes 491528 | tf_op jit(solution)/shard_map/ppermute | solution.py:625

commit v5 on v4

--- a/solution.py
+++ b/solution.py
@@ -176,8 +176,7 @@
                 copy([self.span(t, g, k * PART + j) for j in range(PART)], at[t] + k * PART)
                 return 0
 
-            for k in range(2):
-                part(k, 0)
+            copy([self.span(t, g, j) for j in range(2 * PART)], at[t])
             lax.fori_loop(2, (self.count(t, g) + PART - 1) // PART, part, 0)
         return at
 
@@ -286,10 +285,11 @@
             return jnp.where(span % 2 == 0, wide[:8], wide[8:])
 
         def put(spans, slot, i=i, rows_of=rows_of):
+            rows = jnp.concatenate([rows_of(span) for span in spans], 0)
+            dst = pl.ds(pl.multiple_of(LANES + slot * SPAN, SPAN), len(spans) * SPAN)
+            vtmp_ref[dst, :] = rows
             for j, span in enumerate(spans):
                 slots_ref[i, slot + j] = span
-            dst = pl.ds(pl.multiple_of(LANES + slot * SPAN, SPAN), PART * SPAN)
-            vtmp_ref[dst, :] = jnp.concatenate([rows_of(span) for span in spans], 0)
 
         copies[i].wait()
         if i + 2 < n:

time: 63.5 us -> 63 us (level); the launches traced: 63.7 us -> 62.4 us
  blocking collectives: 12.5 us -> 11.5 us
    all_to_all x1, blocking collectives: 12.5 us -> 11.5 us  [on_device(): parts = lax.all_to_all(parts, 'seq', 0, 0, tiled=True)]
where the time goes in v5:
time: 63 us; the launch traced here: 62.4 us
  Pallas kernels  36.7 us (58%)
  blocking collectives  11.5 us (18%)
  starting transfers between devices  8.09 us (13%)
  waiting for transfers between devices  4.16 us (7%)
  other arithmetic  1.09 us (2%)
  between operations  0.82 us (1%)
    pallas_call x1, Pallas kernels, attend_call(): pl.pallas_call(functools.partial(attend_kernel, per_device=per_device, st...  13.9 us
    pallas_call x2, Pallas kernels, slot_values(): pl.pallas_call(functools.partial(values_kernel, main=main, g0=g0, most=mo...  12.4 us
    all_to_all x1, blocking collectives, on_device(): parts = lax.all_to_all(parts, 'seq', 0, 0, tiled=True)  11.5 us
    ppermute x5, starting transfers between devices, swap(): return lax.ppermute(x, 'seq', moves)  8.09 us
    pallas_call x1, Pallas kernels, sketch_share(): pl.pallas_call(functools.partial(sketch_kernel, scale=1.0 / length, chunk...  6.63 us
    ppermute x5, waiting for transfers between devices, swap(): return lax.ppermute(x, 'seq', moves)  4.16 us
    pallas_call x1, Pallas kernels, on_device(): pl.pallas_call(functools.partial(merge_kernel, steps=steps, per_device=pe...  1.88 us
    pallas_call x1, Pallas kernels, known(): pl.pallas_call(functools.partial(known_kernel, per_device=per_device, rp=...  1.86 us
  transfers between devices with their start and end apart: 5, of which 4 were waited for; matrix products, arithmetic and copies ran while one was open for 1% of the time, Pallas kernels for 23%

profile of v5, /device:TPU:0, one launch (start us, length us, event | category | flops | bytes accessed | tf_op | source)
XLA Modules:
  0.0 62.4 jit_solution(12358467760498547453)
XLA Ops:
  0.6 0.0 copy-start.4
  0.6 0.0 copy-start.3
  0.7 0.0 copy-start.1
  0.7 0.0 copy-start.5
  0.7 0.0 copy-start
  0.7 0.0 copy-start.2
  0.7 6.6 %sketch_share.1 = (f32[80,1024]{1,0:T(8,128)S(1)}, f32[80,1024]{1,0:T(8,128)S(1)}) custom-call(s32[1]{0:T(128)} %bitcast.me_ref, f32[160,1024]{1,0:T(8,128)} %bitcast.18, bf16[4096,1024]{1,0:T(8,128)(2,1)} %keys_hbm.5), custom_call_target="tpu_custom_call" | custom-call | tf_op jit(solution)/shard_map/sketch_share/pallas_call | solution.py:121
  7.3 0.5 collective-permute-start
  7.9 0.1 pad_maximum_fusion
  8.0 0.3 multiply_sine_fusion
  8.3 0.8 %collective-permute-done = f32[80,1024]{1,0:T(8,128)S(1)} collective-permute-done((f32[80,1024]{1,0:T(8,128)S(1)}, f32[80,1024]{1,0:T(8,128)S(1)}, u32[]{:S(2)}, u32[]{:S(2)}) %collective-permute-start) | collective-permute-done | bytes 327712 | tf_op jit(solution)/shard_map/ppermute | solution.py:625
  9.2 3.0 %collective-permute-start.1 = (bf16[80,1024]{1,0:T(8,128)(2,1)S(1)}, bf16[80,1024]{1,0:T(8,128)(2,1)S(1)}, u32[]{:S(2)}, u32[]{:S(2)}) collective-permute-start(bf16[80,1024]{1,0:T(8,128)(2,1)S(1)} %get-tuple-element.30.after_ref), channel_id=1, source_target_pairs={{0,2},{1,5},{2,0},{3,7},{4,6},{5,1},{6,4},{7,3},{8,10},{9,13},{10,... | collective-permute-start | bytes 491528 | tf_op jit(solution)/shard_map/ppermute | solution.py:625
  12.1 0.1 multiply_sine_fusion.2
  12.2 0.0 copy-done.4
  12.2 0.0 copy-done.3
  12.2 0.0 copy-done.1
  12.3 1.9 %known_keys.1 = (bf16[8,128,256]{2,1,0:T(8,128)(2,1)S(1)}, bf16[2,512,128]{2,1,0:T(8,128)(2,1)S(1)}, f32[1,128]{1,0:T(1,128)S(1)}) custom-call(s32[1]{0:T(128)} %bitcast.me_ref, s32[32]{0:T(128)S(1)} %copy-done.4, bf16[3,8192]{1,0:T(4,128)(2,1)S(1)} %copy-done.1, bf16[3,1024]{1,0:T(4,128)(2,1)S(1)} %copy-done.3, f32[64,128]{1,0:T(8,128)S(1)} %get-tuple-element.38.ca_ref, ...), custom_call_target="tpu_custom_call" | custom-call | tf_op jit(solution)/shard_map/known_keys/pallas_call | solution.py:676
  14.1 1.3 %collective-permute-done.1 = bf16[80,1024]{1,0:T(8,128)(2,1)S(1)} collective-permute-done((bf16[80,1024]{1,0:T(8,128)(2,1)S(1)}, bf16[80,1024]{1,0:T(8,128)(2,1)S(1)}, u32[]{:S(2)}, u32[]{:S(2)}) %collective-permute-start.1) | collective-permute-done | bytes 163872 | tf_op jit(solution)/shard_map/ppermute | solution.py:625
  15.4 0.1 fusion.after_ref
  15.5 2.1 %collective-permute-start.2 = (bf16[80,1024]{1,0:T(8,128)(2,1)S(1)}, bf16[80,1024]{1,0:T(8,128)(2,1)S(1)}, u32[]{:S(2)}, u32[]{:S(2)}) collective-permute-start(bf16[80,1024]{1,0:T(8,128)(2,1)S(1)} %fusion.after_ref), channel_id=1, source_target_pairs={{0,4},{1,3},{2,6},{3,1},{4,0},{5,7},{6,2},{7,5},{8,12},{9,11},{10,... | collective-permute-start | bytes 491528 | tf_op jit(solution)/shard_map/ppermute | solution.py:625
  17.6 0.0 copy-done.5
  17.7 0.2 select_reduce_fusion
  17.8 0.0 copy-done
  17.8 0.0 copy-done.2
  17.9 5.6 %slot_values.2 = (s32[3,176]{1,0:T(4,128)S(1)}, bf16[3,1280,128]{2,1,0:T(8,128)(2,1)S(1)}, f32[1,128]{1,0:T(1,128)S(1)}) custom-call(s32[1]{0:T(128)} %bitcast.me_ref, s32[24,256]{1,0:T(8,128)S(1)} %bitcast.10, s32[3,8]{1,0:T(4,128)S(1)} %get-tuple-element.28.begin_ref, s32[3,8]{1,0:T(4,128)S(1)} %get-tuple-element.29.count_ref, s32[32]{0:T(128)S(1)} %copy-done.4, ...), custom_call_target="tpu_custom_call" | custom-call | tf_op jit(solution)/shard_map/slot_values/pallas_call | solution.py:696
  23.5 0.0 collective-permute-done.2
  23.5 0.1 fusion.1.after_ref
  23.6 2.4 %collective-permute-start.3 = (bf16[80,1024]{1,0:T(8,128)(2,1)S(1)}, bf16[80,1024]{1,0:T(8,128)(2,1)S(1)}, u32[]{:S(2)}, u32[]{:S(2)}) collective-permute-start(bf16[80,1024]{1,0:T(8,128)(2,1)S(1)} %fusion.1.after_ref), channel_id=1, source_target_pairs={{0,8},{1,9},{2,10},{3,11},{4,12},{5,13},{6,14},{7,15},{8,0},{9,1},... | collective-permute-start | bytes 491528 | tf_op jit(solution)/shard_map/ppermute | solution.py:625
  26.0 6.8 %slot_values.3 = (s32[5,176]{1,0:T(8,128)S(1)}, bf16[5,1280,128]{2,1,0:T(8,128)(2,1)S(1)}, f32[1,128]{1,0:T(1,128)S(1)}) custom-call(s32[1]{0:T(128)} %bitcast.me_ref, s32[24,256]{1,0:T(8,128)S(1)} %bitcast.11, s32[3,8]{1,0:T(4,128)S(1)} %get-tuple-element.28.begin_ref, s32[3,8]{1,0:T(4,128)S(1)} %get-tuple-element.29.count_ref, s32[32]{0:T(128)S(1)} %copy-done.4, ...), custom_call_target="tpu_custom_call" | custom-call | tf_op jit(solution)/shard_map/slot_values/pallas_call | solution.py:696
  32.8 0.7 %collective-permute-done.3 = bf16[80,1024]{1,0:T(8,128)(2,1)S(1)} collective-permute-done((bf16[80,1024]{1,0:T(8,128)(2,1)S(1)}, bf16[80,1024]{1,0:T(8,128)(2,1)S(1)}, u32[]{:S(2)}, u32[]{:S(2)}) %collective-permute-start.3) | collective-permute-done | bytes 163872 | tf_op jit(solution)/shard_map/ppermute | solution.py:625
  33.5 0.1 add_convert_fusion.zmine_ref
  33.6 0.1 collective-permute-start.4
  33.7 1.4 %collective-permute-done.4.zother_ref = bf16[80,1024]{1,0:T(8,128)(2,1)S(1)} collective-permute-done((bf16[80,1024]{1,0:T(8,128)(2,1)S(1)}, bf16[80,1024]{1,0:T(8,128)(2,1)S(1)}, u32[]{:S(2)}, u32[]{:S(2)}) %collective-permute-start.4) | collective-permute-done | bytes 163872 | tf_op jit(solution)/shard_map/ppermute | solution.py:625
  35.1 13.9 %attend.1 = (f32[160,4096]{1,0:T(8,128)}, bf16[16,16,128]{2,1,0:T(8,128)(2,1)S(1)}) custom-call(s32[1]{0:T(128)} %bitcast.me_ref, s32[3,8]{1,0:T(4,128)S(1)} %get-tuple-element.29.count_ref, s32[32]{0:T(128)S(1)} %copy-done.4, s32[3,176]{1,0:T(4,128)S(1)} %get-tuple-element.18.slotsa_ref, s32[5,176]{1,0:T(8,128)S(1)} %get-tuple-element.20.slotsb_ref, ...), custom_call_target="tpu_custom_call" | custom-call | tf_op jit(solution)/shard_map/attend/pallas_call | solution.py:575
  49.0 11.5 %all_to_all.5.parts_ref = bf16[16,16,128]{2,1,0:T(8,128)(2,1)} all-to-all(bf16[16,16,128]{2,1,0:T(8,128)(2,1)S(1)} %get-tuple-element.26), channel_id=1, replica_groups=mesh['groups'=2,'seq'=16] {'seq'}, dimensions={0} | all-to-all | bytes 131072 | tf_op jit(solution)/shard_map/all_to_all | solution.py:738
  60.5 1.9 %merge.1 = bf16[3,512]{1,0:T(4,128)(2,1)} custom-call(s32[1]{0:T(128)} %bitcast.me_ref, bf16[16,16,128]{2,1,0:T(8,128)(2,1)} %all_to_all.5.parts_ref), custom_call_target="tpu_custom_call" | custom-call | tf_op jit(solution)/shard_map/merge/pallas_call | solution.py:739
  (6 shorter events, 0.1 us)
Async XLA Ops:
  0.6 11.6 %copy-start.4 = (s32[32]{0:T(128)S(1)}, s32[32]{0:T(128)}, u32[]{:S(2)}) copy-start(s32[32]{0:T(128)} %outl_ref.7) | copy-start | bytes 388
  0.6 11.6 %copy-start.3 = (bf16[3,1024]{1,0:T(4,128)(2,1)S(1)}, bf16[3,1024]{1,0:T(4,128)(2,1)}, u32[]{:S(2)}) copy-start(bf16[3,1024]{1,0:T(4,128)(2,1)} %fk_ref.1) | copy-start | bytes 18436
  0.7 11.6 %copy-start.1 = (bf16[3,8192]{1,0:T(4,128)(2,1)S(1)}, bf16[3,8192]{1,0:T(4,128)(2,1)}, u32[]{:S(2)}) copy-start(bf16[3,8192]{1,0:T(4,128)(2,1)} %q_ref.1) | copy-start | bytes 147460
  0.7 17.0 %copy-start.5 = (s32[3,8,16]{2,1,0:T(8,128)S(1)}, s32[3,8,16]{2,1,0:T(8,128)}, u32[]{:S(2)}) copy-start(s32[3,8,16]{2,1,0:T(8,128)} %param.16) | copy-start | bytes 4612
  0.7 17.2 %copy-start = (s32[3,8,256]{2,1,0:T(8,128)S(1)}, s32[3,8,256]{2,1,0:T(8,128)}, u32[]{:S(2)}) copy-start(s32[3,8,256]{2,1,0:T(8,128)} %param.15) | copy-start | bytes 73732
  0.7 17.2 %copy-start.2 = (bf16[3,1024]{1,0:T(4,128)(2,1)S(1)}, bf16[3,1024]{1,0:T(4,128)(2,1)}, u32[]{:S(2)}) copy-start(bf16[3,1024]{1,0:T(4,128)(2,1)} %fv_ref.3) | copy-start | bytes 18436
  7.3 1.8 %collective-permute-start = (f32[80,1024]{1,0:T(8,128)S(1)}, f32[80,1024]{1,0:T(8,128)S(1)}, u32[]{:S(2)}, u32[]{:S(2)}) collective-permute-start(f32[80,1024]{1,0:T(8,128)S(1)} %get-tuple-element.16), channel_id=1, source_target_pairs={{0,1},{1,0},{2,3},{3,2},{4,5},{5,4},{6,7},{7,6},{8,9},{9,8},{10,11... | collective-permute-start | bytes 983048 | tf_op jit(solution)/shard_map/ppermute | solution.py:625
  9.2 6.3 %collective-permute-start.1 = (bf16[80,1024]{1,0:T(8,128)(2,1)S(1)}, bf16[80,1024]{1,0:T(8,128)(2,1)S(1)}, u32[]{:S(2)}, u32[]{:S(2)}) collective-permute-start(bf16[80,1024]{1,0:T(8,128)(2,1)S(1)} %get-tuple-element.30.after_ref), channel_id=1, source_target_pairs={{0,2},{1,5},{2,0},{3,7},{4,6},{5,1},{6,4},{7,3},{8,10},{9,13},{10,... | collective-permute-start | bytes 491528 | tf_op jit(solution)/shard_map/ppermute | solution.py:625
  15.5 8.0 %collective-permute-start.2 = (bf16[80,1024]{1,0:T(8,128)(2,1)S(1)}, bf16[80,1024]{1,0:T(8,128)(2,1)S(1)}, u32[]{:S(2)}, u32[]{:S(2)}) collective-permute-start(bf16[80,1024]{1,0:T(8,128)(2,1)S(1)} %fusion.after_ref), channel_id=1, source_target_pairs={{0,4},{1,3},{2,6},{3,1},{4,0},{5,7},{6,2},{7,5},{8,12},{9,11},{10,... | collective-permute-start | bytes 491528 | tf_op jit(solution)/shard_map/ppermute | solution.py:625
  23.6 9.8 %collective-permute-start.3 = (bf16[80,1024]{1,0:T(8,128)(2,1)S(1)}, bf16[80,1024]{1,0:T(8,128)(2,1)S(1)}, u32[]{:S(2)}, u32[]{:S(2)}) collective-permute-start(bf16[80,1024]{1,0:T(8,128)(2,1)S(1)} %fusion.1.after_ref), channel_id=1, source_target_pairs={{0,8},{1,9},{2,10},{3,11},{4,12},{5,13},{6,14},{7,15},{8,0},{9,1},... | collective-permute-start | bytes 491528 | tf_op jit(solution)/shard_map/ppermute | solution.py:625
  33.6 1.5 %collective-permute-start.4 = (bf16[80,1024]{1,0:T(8,128)(2,1)S(1)}, bf16[80,1024]{1,0:T(8,128)(2,1)S(1)}, u32[]{:S(2)}, u32[]{:S(2)}) collective-permute-start(bf16[80,1024]{1,0:T(8,128)(2,1)S(1)} %add_convert_fusion.zmine_ref), channel_id=1, source_target_pairs={{0,1},{1,0},{2,3},{3,2},{4,5},{5,4},{6,7},{7,6},{8,9},{9,8},{10,11... | collective-permute-start | bytes 491528 | tf_op jit(solution)/shard_map/ppermute | solution.py:625

commit v6 on v4

--- a/solution.py
+++ b/solution.py
@@ -272,7 +272,7 @@
     copies = [
         pltpu.make_async_copy(values_hbm.at[:, pl.ds((g0 + i) * HD, HD)], values_ref.at[i], sem.at[i]) for i in range(n)
     ]
-    for c in copies[:2]:
+    for c in copies[:AHEAD + 1]:
         c.start()
     tie_ref[...] = jnp.zeros_like(tie_ref)
     vtmp_ref[...] = jnp.zeros_like(vtmp_ref)
@@ -292,8 +292,8 @@
             vtmp_ref[dst, :] = jnp.concatenate([rows_of(span) for span in spans], 0)
 
         copies[i].wait()
-        if i + 2 < n:
-            copies[i + 2].start()
+        if i + AHEAD + 1 < n:
+            copies[i + AHEAD + 1].start()
         for j in range(OMOST):
             vtmp_ref[j * SPAN:(j + 1) * SPAN, :] = rows_of(o_span[j])
         vtmp_ref[OMOST * SPAN:OMOST * SPAN + steps, :] = fv_ref[:, (g0 + i) * HD:(g0 + i + 1) * HD].astype(F32)

time: 63.5 us -> 63.3 us (level)
  Pallas kernels: 37.1 us -> 37.8 us
  waiting for transfers between devices: 4.23 us -> 3.56 us
    ppermute x5, waiting for transfers between devices: 4.23 us -> 3.56 us  [swap(): return lax.ppermute(x, 'seq', moves)]
  transfers between devices with their start and end apart: 5 -> 5, of which waited for: 4 -> 3; matrix products, arithmetic and copies ran while one was open for 1% -> 1% of each run, Pallas kernels for 23% -> 24%
where the time goes in v6:
time: 63.3 us
  Pallas kernels  37.8 us (60%)
  blocking collectives  12.1 us (19%)
  starting transfers between devices  7.95 us (13%)
  waiting for transfers between devices  3.56 us (6%)
  other arithmetic  1.09 us (2%)
  between operations  0.83 us (1%)
    pallas_call x1, Pallas kernels, attend_call(): pl.pallas_call(functools.partial(attend_kernel, per_device=per_device, st...  14.4 us
    pallas_call x2, Pallas kernels, slot_values(): pl.pallas_call(functools.partial(values_kernel, main=main, g0=g0, most=mo...  13.1 us
    all_to_all x1, blocking collectives, on_device(): parts = lax.all_to_all(parts, 'seq', 0, 0, tiled=True)  12.1 us
    ppermute x5, starting transfers between devices, swap(): return lax.ppermute(x, 'seq', moves)  7.95 us
    pallas_call x1, Pallas kernels, sketch_share(): pl.pallas_call(functools.partial(sketch_kernel, scale=1.0 / length, chunk...  6.63 us
    ppermute x5, waiting for transfers between devices, swap(): return lax.ppermute(x, 'seq', moves)  3.56 us
    pallas_call x1, Pallas kernels, on_device(): pl.pallas_call(functools.partial(merge_kernel, steps=steps, per_device=pe...  1.88 us
    pallas_call x1, Pallas kernels, known(): pl.pallas_call(functools.partial(known_kernel, per_device=per_device, rp=...  1.81 us
  transfers between devices with their start and end apart: 5, of which 3 were waited for; matrix products, arithmetic and copies ran while one was open for 1% of the time, Pallas kernels for 24%

profile of v6, /device:TPU:0, one launch (start us, length us, event | category | flops | bytes accessed | tf_op | source)
XLA Modules:
  0.0 63.3 jit_solution(6068465098204405523)
XLA Ops:
  0.6 0.0 copy-start.4
  0.6 0.0 copy-start.3
  0.7 0.0 copy-start.1
  0.7 0.0 copy-start.5
  0.7 0.0 copy-start
  0.7 0.0 copy-start.2
  0.7 6.6 %sketch_share.1 = (f32[80,1024]{1,0:T(8,128)S(1)}, f32[80,1024]{1,0:T(8,128)S(1)}) custom-call(s32[1]{0:T(128)} %bitcast.me_ref, f32[160,1024]{1,0:T(8,128)} %bitcast.18, bf16[4096,1024]{1,0:T(8,128)(2,1)} %keys_hbm.5), custom_call_target="tpu_custom_call" | custom-call | tf_op jit(solution)/shard_map/sketch_share/pallas_call | solution.py:121
  7.3 0.5 collective-permute-start
  7.9 0.1 pad_maximum_fusion
  8.0 0.3 multiply_sine_fusion
  8.3 0.8 %collective-permute-done = f32[80,1024]{1,0:T(8,128)S(1)} collective-permute-done((f32[80,1024]{1,0:T(8,128)S(1)}, f32[80,1024]{1,0:T(8,128)S(1)}, u32[]{:S(2)}, u32[]{:S(2)}) %collective-permute-start) | collective-permute-done | bytes 327712 | tf_op jit(solution)/shard_map/ppermute | solution.py:625
  9.2 3.0 %collective-permute-start.1 = (bf16[80,1024]{1,0:T(8,128)(2,1)S(1)}, bf16[80,1024]{1,0:T(8,128)(2,1)S(1)}, u32[]{:S(2)}, u32[]{:S(2)}) collective-permute-start(bf16[80,1024]{1,0:T(8,128)(2,1)S(1)} %get-tuple-element.30.after_ref), channel_id=1, source_target_pairs={{0,2},{1,5},{2,0},{3,7},{4,6},{5,1},{6,4},{7,3},{8,10},{9,13},{10,... | collective-permute-start | bytes 491528 | tf_op jit(solution)/shard_map/ppermute | solution.py:625
  12.1 0.1 multiply_sine_fusion.2
  12.2 0.0 copy-done.4
  12.2 0.0 copy-done.3
  12.2 0.0 copy-done.1
  12.3 1.8 %known_keys.1 = (bf16[8,128,256]{2,1,0:T(8,128)(2,1)S(1)}, bf16[2,512,128]{2,1,0:T(8,128)(2,1)S(1)}, f32[1,128]{1,0:T(1,128)S(1)}) custom-call(s32[1]{0:T(128)} %bitcast.me_ref, s32[32]{0:T(128)S(1)} %copy-done.4, bf16[3,8192]{1,0:T(4,128)(2,1)S(1)} %copy-done.1, bf16[3,1024]{1,0:T(4,128)(2,1)S(1)} %copy-done.3, f32[64,128]{1,0:T(8,128)S(1)} %get-tuple-element.38.ca_ref, ...), custom_call_target="tpu_custom_call" | custom-call | tf_op jit(solution)/shard_map/known_keys/pallas_call | solution.py:676
  14.1 1.3 %collective-permute-done.1 = bf16[80,1024]{1,0:T(8,128)(2,1)S(1)} collective-permute-done((bf16[80,1024]{1,0:T(8,128)(2,1)S(1)}, bf16[80,1024]{1,0:T(8,128)(2,1)S(1)}, u32[]{:S(2)}, u32[]{:S(2)}) %collective-permute-start.1) | collective-permute-done | bytes 163872 | tf_op jit(solution)/shard_map/ppermute | solution.py:625
  15.4 0.1 fusion.after_ref
  15.5 2.1 %collective-permute-start.2 = (bf16[80,1024]{1,0:T(8,128)(2,1)S(1)}, bf16[80,1024]{1,0:T(8,128)(2,1)S(1)}, u32[]{:S(2)}, u32[]{:S(2)}) collective-permute-start(bf16[80,1024]{1,0:T(8,128)(2,1)S(1)} %fusion.after_ref), channel_id=1, source_target_pairs={{0,4},{1,3},{2,6},{3,1},{4,0},{5,7},{6,2},{7,5},{8,12},{9,11},{10,... | collective-permute-start | bytes 491528 | tf_op jit(solution)/shard_map/ppermute | solution.py:625
  17.6 0.0 copy-done.5
  17.7 0.2 select_reduce_fusion
  17.8 0.0 copy-done
  17.8 0.0 copy-done.2
  17.9 5.5 %slot_values.2 = (s32[3,176]{1,0:T(4,128)S(1)}, bf16[3,1280,128]{2,1,0:T(8,128)(2,1)S(1)}, f32[1,128]{1,0:T(1,128)S(1)}) custom-call(s32[1]{0:T(128)} %bitcast.me_ref, s32[24,256]{1,0:T(8,128)S(1)} %bitcast.10, s32[3,8]{1,0:T(4,128)S(1)} %get-tuple-element.28.begin_ref, s32[3,8]{1,0:T(4,128)S(1)} %get-tuple-element.29.count_ref, s32[32]{0:T(128)S(1)} %copy-done.4, ...), custom_call_target="tpu_custom_call" | custom-call | tf_op jit(solution)/shard_map/slot_values/pallas_call | solution.py:696
  23.3 0.0 collective-permute-done.2
  23.4 0.1 fusion.1.after_ref
  23.5 2.3 %collective-permute-start.3 = (bf16[80,1024]{1,0:T(8,128)(2,1)S(1)}, bf16[80,1024]{1,0:T(8,128)(2,1)S(1)}, u32[]{:S(2)}, u32[]{:S(2)}) collective-permute-start(bf16[80,1024]{1,0:T(8,128)(2,1)S(1)} %fusion.1.after_ref), channel_id=1, source_target_pairs={{0,8},{1,9},{2,10},{3,11},{4,12},{5,13},{6,14},{7,15},{8,0},{9,1},... | collective-permute-start | bytes 491528 | tf_op jit(solution)/shard_map/ppermute | solution.py:625
  25.7 7.6 %slot_values.3 = (s32[5,176]{1,0:T(8,128)S(1)}, bf16[5,1280,128]{2,1,0:T(8,128)(2,1)S(1)}, f32[1,128]{1,0:T(1,128)S(1)}) custom-call(s32[1]{0:T(128)} %bitcast.me_ref, s32[24,256]{1,0:T(8,128)S(1)} %bitcast.11, s32[3,8]{1,0:T(4,128)S(1)} %get-tuple-element.28.begin_ref, s32[3,8]{1,0:T(4,128)S(1)} %get-tuple-element.29.count_ref, s32[32]{0:T(128)S(1)} %copy-done.4, ...), custom_call_target="tpu_custom_call" | custom-call | tf_op jit(solution)/shard_map/slot_values/pallas_call | solution.py:696
  33.4 0.0 collective-permute-done.3
  33.4 0.1 add_convert_fusion.zmine_ref
  33.5 0.1 collective-permute-start.4
  33.6 1.4 %collective-permute-done.4.zother_ref = bf16[80,1024]{1,0:T(8,128)(2,1)S(1)} collective-permute-done((bf16[80,1024]{1,0:T(8,128)(2,1)S(1)}, bf16[80,1024]{1,0:T(8,128)(2,1)S(1)}, u32[]{:S(2)}, u32[]{:S(2)}) %collective-permute-start.4) | collective-permute-done | bytes 163872 | tf_op jit(solution)/shard_map/ppermute | solution.py:625
  35.0 14.4 %attend.1 = (f32[160,4096]{1,0:T(8,128)}, bf16[16,16,128]{2,1,0:T(8,128)(2,1)S(1)}) custom-call(s32[1]{0:T(128)} %bitcast.me_ref, s32[3,8]{1,0:T(4,128)S(1)} %get-tuple-element.29.count_ref, s32[32]{0:T(128)S(1)} %copy-done.4, s32[3,176]{1,0:T(4,128)S(1)} %get-tuple-element.18.slotsa_ref, s32[5,176]{1,0:T(8,128)S(1)} %get-tuple-element.20.slotsb_ref, ...), custom_call_target="tpu_custom_call" | custom-call | tf_op jit(solution)/shard_map/attend/pallas_call | solution.py:575
  49.3 12.1 %all_to_all.5.parts_ref = bf16[16,16,128]{2,1,0:T(8,128)(2,1)} all-to-all(bf16[16,16,128]{2,1,0:T(8,128)(2,1)S(1)} %get-tuple-element.26), channel_id=1, replica_groups=mesh['groups'=2,'seq'=16] {'seq'}, dimensions={0} | all-to-all | bytes 131072 | tf_op jit(solution)/shard_map/all_to_all | solution.py:738
  61.4 1.9 %merge.1 = bf16[3,512]{1,0:T(4,128)(2,1)} custom-call(s32[1]{0:T(128)} %bitcast.me_ref, bf16[16,16,128]{2,1,0:T(8,128)(2,1)} %all_to_all.5.parts_ref), custom_call_target="tpu_custom_call" | custom-call | tf_op jit(solution)/shard_map/merge/pallas_call | solution.py:739
  (6 shorter events, 0.1 us)
Async XLA Ops:
  0.6 11.6 %copy-start.4 = (s32[32]{0:T(128)S(1)}, s32[32]{0:T(128)}, u32[]{:S(2)}) copy-start(s32[32]{0:T(128)} %outl_ref.7) | copy-start | bytes 388
  0.6 11.6 %copy-start.3 = (bf16[3,1024]{1,0:T(4,128)(2,1)S(1)}, bf16[3,1024]{1,0:T(4,128)(2,1)}, u32[]{:S(2)}) copy-start(bf16[3,1024]{1,0:T(4,128)(2,1)} %fk_ref.1) | copy-start | bytes 18436
  0.7 11.6 %copy-start.1 = (bf16[3,8192]{1,0:T(4,128)(2,1)S(1)}, bf16[3,8192]{1,0:T(4,128)(2,1)}, u32[]{:S(2)}) copy-start(bf16[3,8192]{1,0:T(4,128)(2,1)} %q_ref.1) | copy-start | bytes 147460
  0.7 17.0 %copy-start.5 = (s32[3,8,16]{2,1,0:T(8,128)S(1)}, s32[3,8,16]{2,1,0:T(8,128)}, u32[]{:S(2)}) copy-start(s32[3,8,16]{2,1,0:T(8,128)} %param.16) | copy-start | bytes 4612
  0.7 17.2 %copy-start = (s32[3,8,256]{2,1,0:T(8,128)S(1)}, s32[3,8,256]{2,1,0:T(8,128)}, u32[]{:S(2)}) copy-start(s32[3,8,256]{2,1,0:T(8,128)} %param.15) | copy-start | bytes 73732
  0.7 17.2 %copy-start.2 = (bf16[3,1024]{1,0:T(4,128)(2,1)S(1)}, bf16[3,1024]{1,0:T(4,128)(2,1)}, u32[]{:S(2)}) copy-start(bf16[3,1024]{1,0:T(4,128)(2,1)} %fv_ref.3) | copy-start | bytes 18436
  7.3 1.8 %collective-permute-start = (f32[80,1024]{1,0:T(8,128)S(1)}, f32[80,1024]{1,0:T(8,128)S(1)}, u32[]{:S(2)}, u32[]{:S(2)}) collective-permute-start(f32[80,1024]{1,0:T(8,128)S(1)} %get-tuple-element.16), channel_id=1, source_target_pairs={{0,1},{1,0},{2,3},{3,2},{4,5},{5,4},{6,7},{7,6},{8,9},{9,8},{10,11... | collective-permute-start | bytes 983048 | tf_op jit(solution)/shard_map/ppermute | solution.py:625
  9.2 6.3 %collective-permute-start.1 = (bf16[80,1024]{1,0:T(8,128)(2,1)S(1)}, bf16[80,1024]{1,0:T(8,128)(2,1)S(1)}, u32[]{:S(2)}, u32[]{:S(2)}) collective-permute-start(bf16[80,1024]{1,0:T(8,128)(2,1)S(1)} %get-tuple-element.30.after_ref), channel_id=1, source_target_pairs={{0,2},{1,5},{2,0},{3,7},{4,6},{5,1},{6,4},{7,3},{8,10},{9,13},{10,... | collective-permute-start | bytes 491528 | tf_op jit(solution)/shard_map/ppermute | solution.py:625
  15.5 7.8 %collective-permute-start.2 = (bf16[80,1024]{1,0:T(8,128)(2,1)S(1)}, bf16[80,1024]{1,0:T(8,128)(2,1)S(1)}, u32[]{:S(2)}, u32[]{:S(2)}) collective-permute-start(bf16[80,1024]{1,0:T(8,128)(2,1)S(1)} %fusion.after_ref), channel_id=1, source_target_pairs={{0,4},{1,3},{2,6},{3,1},{4,0},{5,7},{6,2},{7,5},{8,12},{9,11},{10,... | collective-permute-start | bytes 491528 | tf_op jit(solution)/shard_map/ppermute | solution.py:625
  23.5 9.9 %collective-permute-start.3 = (bf16[80,1024]{1,0:T(8,128)(2,1)S(1)}, bf16[80,1024]{1,0:T(8,128)(2,1)S(1)}, u32[]{:S(2)}, u32[]{:S(2)}) collective-permute-start(bf16[80,1024]{1,0:T(8,128)(2,1)S(1)} %fusion.1.after_ref), channel_id=1, source_target_pairs={{0,8},{1,9},{2,10},{3,11},{4,12},{5,13},{6,14},{7,15},{8,0},{9,1},... | collective-permute-start | bytes 491528 | tf_op jit(solution)/shard_map/ppermute | solution.py:625
  33.5 1.5 %collective-permute-start.4 = (bf16[80,1024]{1,0:T(8,128)(2,1)S(1)}, bf16[80,1024]{1,0:T(8,128)(2,1)S(1)}, u32[]{:S(2)}, u32[]{:S(2)}) collective-permute-start(bf16[80,1024]{1,0:T(8,128)(2,1)S(1)} %add_convert_fusion.zmine_ref), channel_id=1, source_target_pairs={{0,1},{1,0},{2,3},{3,2},{4,5},{5,4},{6,7},{7,6},{8,9},{9,8},{10,11... | collective-permute-start | bytes 491528 | tf_op jit(solution)/shard_map/ppermute | solution.py:625
